TPU v7x, 256 devices: a whole 4x4x8 slice. The times are simulated.
256 devices in a mesh: dp: 4 (over y), group: 16 (over z_hi, x), tensor: 4 (over z_lo, core).
Axes of the slice: x: 4, y: 4, z: 8 (z_hi: 4, z_lo: 2; z = z_hi * 2 + z_lo), core: 2. Of those that a mesh axis runs over, the one named last changes fastest.
Arguments:
- queries: bfloat16 [4, 16, 256, 4096], P('dp', 'group', None, 'tensor'), may hold values from -6 to 6
- comp_keys: bfloat16 [4, 16, 256, 512], P('dp', 'group', None, 'tensor'), may hold values from -4 to 4
- comp_values: bfloat16 [4, 16, 256, 512], P('dp', 'group', None, 'tensor'), may hold values from -4 to 4
- prompt_keys: bfloat16 [4, 2048, 512], P('dp', 'group', 'tensor'), may hold values from -6 to 6
- prompt_values: bfloat16 [4, 2048, 512], P('dp', 'group', 'tensor'), may hold values from -4 to 4
- out_weight: bfloat16 [4096, 4096], P('tensor'), may hold values from -1.5 to 1.5
- cotangent: bfloat16 [4, 16, 256, 4096], P('dp', 'group', None, 'tensor'), may hold values from -5 to 5
- lengths: int32 [4, 16], P('dp', 'group'), may hold values from 1 to 256, 1216 in all within a row
Outputs:
- output: bfloat16 [4, 16, 256, 4096], P('dp', 'group', None, 'tensor')
- query_grad: bfloat16 [4, 16, 256, 4096], P('dp', 'group', None, 'tensor')
- comp_key_grad: bfloat16 [4, 16, 256, 512], P('dp', 'group', None, 'tensor')
- comp_value_grad: bfloat16 [4, 16, 256, 512], P('dp', 'group', None, 'tensor')
- prompt_key_grad: bfloat16 [4, 2048, 512], P('dp', 'group', 'tensor')
- prompt_value_grad: bfloat16 [4, 2048, 512], P('dp', 'group', 'tensor')
Inputs may be any that keep to these rules, and one draw needn't show every extreme that they name: Each prompt's 16 lengths sum to 1216, and the longest of them is exactly 256.
All inputs are finite; a program needn't handle non-finite values. No bound on the sum of `lengths` on one device may be relied on, other than what follows from the above.
Results may differ from a plain program's by a relative error of at most 0.025.
Values may be sent and summed in bfloat16 or wider, within the bound.
No kernel may reach another device: no remote copies, remote signals or barrier semaphores. Data moves between devices by JAX's collectives and lax.ppermute only.
A program may use at most 64 MiB of HBM per device.

v0:
```python
import jax
import jax.numpy as jnp
from jax import lax
from jax.sharding import PartitionSpec as P

HD = 128


NEG_FILL = -1e30


def block_pass(query_rows, dout_rows, row_ids, length, all_keys, all_values, prompt_len):
    score_scale = query_rows.shape[-1] ** (-0.5)
    scores = (
        jnp.einsum("ikgd,jkd->kgij", query_rows, all_keys, preferred_element_type=jnp.float32)
        * score_scale
    )
    key_index = jnp.arange(all_keys.shape[0], dtype=jnp.int32)
    live_rows = row_ids < length
    allowed = (key_index[None, :] < prompt_len) | (
        key_index[None, :] - prompt_len <= row_ids[:, None]
    )
    allowed = allowed & live_rows[:, None]
    masked = jnp.where(allowed, scores, NEG_FILL)
    top_score = jnp.max(masked, axis=-1, keepdims=True)
    expo = jnp.where(allowed, jnp.exp(masked - top_score), 0.0)
    normer = jnp.sum(expo, axis=-1, keepdims=True)
    normer = jnp.where(live_rows[:, None], normer, 1.0)
    attn_weights = expo / normer
    weights_low = attn_weights.astype(jnp.bfloat16)
    mixed_out = jnp.einsum(
        "kgij,jkd->ikgd", weights_low, all_values, preferred_element_type=jnp.float32
    ).astype(jnp.bfloat16)
    dprob = jnp.einsum("ikgd,jkd->kgij", dout_rows, all_values, preferred_element_type=jnp.float32)
    row_delta = jnp.sum(attn_weights * dprob, axis=-1, keepdims=True)
    dscore = (attn_weights * (dprob - row_delta) * score_scale).astype(jnp.bfloat16)
    dquery = jnp.einsum(
        "kgij,jkd->ikgd", dscore, all_keys, preferred_element_type=jnp.float32
    ).astype(jnp.bfloat16)
    dkeys = jnp.einsum("kgij,ikgd->jkd", dscore, query_rows, preferred_element_type=jnp.float32)
    dvalues = jnp.einsum(
        "kgij,ikgd->jkd", weights_low, dout_rows, preferred_element_type=jnp.float32
    )
    return (mixed_out, dquery, dkeys, dvalues)


def per_device(
    queries, comp_keys, comp_values, prompt_keys, prompt_values, out_weight, cotangent, lengths
):
    slot_count = queries.shape[2]
    query_cols = queries.shape[3]
    key_cols = comp_keys.shape[3]
    head_size = HD
    kv_local = key_cols // head_size
    per_group = query_cols // key_cols
    gathered_keys, gathered_values = (
        lax.all_gather(prompt_keys, "group", axis=1, tiled=True),
        lax.all_gather(prompt_values, "group", axis=1, tiled=True),
    )
    prompt_len = gathered_keys.shape[1]
    dout_wide = lax.dot_general(
        lax.all_gather(cotangent, "tensor", axis=3, tiled=True)[0, 0],
        out_weight,
        (((1,), (1,)), ((), ())),
        preferred_element_type=jnp.float32,
    )
    dout_low = dout_wide.astype(jnp.bfloat16)
    all_keys = jnp.concatenate([gathered_keys[0], comp_keys[0, 0]], 0).reshape(
        -1, kv_local, head_size
    )
    all_values = jnp.concatenate([gathered_values[0], comp_values[0, 0]], 0).reshape(
        -1, kv_local, head_size
    )
    table_rows = all_keys.shape[0]
    length = lengths[0, 0]
    dout_heads = dout_low.reshape(slot_count, kv_local, per_group, head_size)
    query_heads = queries[0, 0].reshape(slot_count, kv_local, per_group, head_size)
    row_block = min(slot_count, 128)
    block_count = slot_count // row_block

    def block_step(block_index, state_now):
        mixed_all, dquery_all, dkeys_sum, dvalues_sum = state_now
        row_start = block_index * row_block
        query_rows = lax.dynamic_slice_in_dim(query_heads, row_start, row_block, 0)
        dout_rows = lax.dynamic_slice_in_dim(dout_heads, row_start, row_block, 0)
        block_rows = row_start + jnp.arange(row_block, dtype=jnp.int32)
        mixed_rows, dquery_rows, dkeys, dvalues = block_pass(
            query_rows, dout_rows, block_rows, length, all_keys, all_values, prompt_len
        )
        mixed_all = lax.dynamic_update_slice_in_dim(mixed_all, mixed_rows, row_start, 0)
        dquery_all = lax.dynamic_update_slice_in_dim(dquery_all, dquery_rows, row_start, 0)
        return (mixed_all, dquery_all, dkeys_sum + dkeys, dvalues_sum + dvalues)

    initial = (
        jnp.zeros((slot_count, kv_local, per_group, head_size), jnp.bfloat16),
        jnp.zeros((slot_count, kv_local, per_group, head_size), jnp.bfloat16),
        jnp.zeros((table_rows, kv_local, head_size), jnp.float32),
        jnp.zeros((table_rows, kv_local, head_size), jnp.float32),
    )
    mixed_all, dquery_all, dkeys_sum, dvalues_sum = lax.fori_loop(
        0, block_count, block_step, initial
    )
    mixed_flat = mixed_all.reshape(slot_count, query_cols)
    dquery_flat = dquery_all.reshape(slot_count, query_cols)
    prompt_kgrad = dkeys_sum[:prompt_len].reshape(1, prompt_len, key_cols)
    prompt_vgrad = dvalues_sum[:prompt_len].reshape(1, prompt_len, key_cols)
    owned_kgrad, owned_vgrad = (
        lax.psum_scatter(
            prompt_kgrad.astype(jnp.bfloat16), "group", scatter_dimension=1, tiled=True
        ).astype(jnp.float32),
        lax.psum_scatter(
            prompt_vgrad.astype(jnp.bfloat16), "group", scatter_dimension=1, tiled=True
        ).astype(jnp.float32),
    )
    comp_kgrad_wide = dkeys_sum[prompt_len:].reshape(slot_count, key_cols)
    comp_vgrad_wide = dvalues_sum[prompt_len:].reshape(slot_count, key_cols)
    partial_term = jnp.dot(mixed_flat, out_weight, preferred_element_type=jnp.float32).astype(
        jnp.bfloat16
    )
    partial_term = lax.optimization_barrier(partial_term).astype(jnp.float32)
    output = lax.psum_scatter(
        partial_term.reshape(1, 1, slot_count, -1).astype(jnp.bfloat16),
        "tensor",
        scatter_dimension=3,
        tiled=True,
    )
    query_grad = dquery_flat.reshape(1, 1, slot_count, query_cols)
    comp_kgrad = comp_kgrad_wide.astype(jnp.bfloat16).reshape(1, 1, slot_count, key_cols)
    comp_vgrad = comp_vgrad_wide.astype(jnp.bfloat16).reshape(1, 1, slot_count, key_cols)
    return (
        output,
        query_grad,
        comp_kgrad,
        comp_vgrad,
        owned_kgrad.astype(jnp.bfloat16),
        owned_vgrad.astype(jnp.bfloat16),
    )


def solution(mesh):
    in_specs = (
        P("dp", "group", None, "tensor"),
        P("dp", "group", None, "tensor"),
        P("dp", "group", None, "tensor"),
        P("dp", "group", "tensor"),
        P("dp", "group", "tensor"),
        P("tensor", None),
        P("dp", "group", None, "tensor"),
        P("dp", "group"),
    )
    out_specs = (
        P("dp", "group", None, "tensor"),
        P("dp", "group", None, "tensor"),
        P("dp", "group", None, "tensor"),
        P("dp", "group", None, "tensor"),
        P("dp", "group", "tensor"),
        P("dp", "group", "tensor"),
    )
    return jax.shard_map(
        per_device, mesh=mesh, in_specs=in_specs, out_specs=out_specs, check_vma=False
    )
```

profile of v0, /device:TPU:8, one launch (start us, length us, event | category | flops | bytes accessed | tf_op | source)
XLA Modules:
  0.0 382.4 jit_solution(5769653955599372652)
XLA Ops:
  7.2 0.0 all-gather.2.cloned.1.call-start
  7.2 0.7 all-gather.2.cloned.1.call-update
  7.9 0.0 reduce-scatter.8.cloned.1.call-start
  8.0 1.2 copy.22
  9.2 51.9 %all_gather.9 = bf16[1,2048,128]{2,1,0:T(8,128)(2,1)S(1)} all-gather(bf16[1,128,128]{2,1,0:T(8,128)(2,1)} %param.13), channel_id=1, replica_groups=mesh['dp'=4,'group'=16,'tensor'=4] {'group'}, dimensions={1}, use_global_device_ids=true | all-gather | bytes 557056 | tf_op jit(solution)/shard_map/all_gather | solution.py:57
  61.1 42.0 %all_gather.10 = bf16[1,2048,128]{2,1,0:T(8,128)(2,1)S(1)} all-gather(bf16[1,128,128]{2,1,0:T(8,128)(2,1)} %param.14), channel_id=1, replica_groups=mesh['dp'=4,'group'=16,'tensor'=4] {'group'}, dimensions={1}, use_global_device_ids=true | all-gather | bytes 557056 | tf_op jit(solution)/shard_map/all_gather | solution.py:58
  103.1 0.9 maximum_bitcast_fusion
  104.0 1.7 maximum_bitcast_fusion.1
  105.7 6.4 %fusion.46 = bf16[32,8,8,128]{3,1,2,0:T(8,128)(2,1)S(1)} fusion(bf16[1024,4096]{1,0:T(8,128)(2,1)} %param.15, bf16[1,1,256,4096]{3,2,1,0:T(8,128)(2,1)} %all-gather.2.cloned.1.call-done), kind=kOutput, calls=%fused_computation.51 | convolution fusion | flops 2147745792 | bytes 11010048 | tf_op jit(solution)/shard_map/dot_general | solution.py:61
  112.1 0.1 copy.37
  112.2 0.8 broadcast.111.clone
  113.0 0.9 broadcast.111.clone.1
  113.9 57.7 %while.22 = (s32[]{:T(128)}, bf16[256,1,8,128]{0,3,2,1:T(8,128)(2,1)}, bf16[256,1,8,128]{3,2,0,1:T(8,128)(2,1)}, f32[2304,1,128]{0,2,1:T(8,128)S(1)}, f32[2304,1...) while((s32[]{:T(128)}, ...), condition=%wide.region_4.5_spmd.clone, body=%wide.region_0.4_spmd.clone.sunk | while | flops 3711142912 | bytes 177525056 | solution.py:100
  113.9 0.7 broadcast_compare_fusion.2
  114.6 0.1 copy-done.1
  114.7 0.3 or_and_fusion.2
  115.0 2.0 fusion.76
  117.1 2.8 fusion.77
  119.9 0.8 copy-done
  120.7 3.0 fusion.78
  123.7 0.2 copy.51
  123.9 0.0 slice-start
  123.9 0.7 constant_dynamic-update-slice_fusion.2
  124.6 7.4 %fusion.83 = f32[2304,1,128]{0,2,1:T(8,128)} fusion(f32[2304,1,128]{0,2,1:T(8,128)} %get-tuple-element.421, pred[]{:T(512)S(6)} %compare.3, bf16[128,1,8,128]{3,2,0,1:T(8,128)(2,1)S(1)} %constant_dynamic-slice_fusion.2, f32[8,128]{1,0:T(8,128)S(1)} %broadcast_select_fusion.2, f32[8,128]{1,0:T(8,128)S(1)} %get-tuple-element.400, ...), kind=kOutput, calls=%fused_computation.17.clone.1 | convolution fusion | flops 618725376 | bytes 12361729 | tf_op jit(solution)/shard_map/while/body/eval_jaxpr/kgij,ikgd->jkd/dot_general | solution.py:41
  132.1 0.0 copy-done.4
  132.1 3.5 fusion.79
  135.6 3.7 fusion.80
  139.3 0.0 copy-start.2
  139.3 1.4 fusion.81
  140.7 1.0 fusion.82
  141.7 0.9 copy_dynamic-update-slice_fusion.2
  142.6 0.7 broadcast_compare_fusion.2
  143.3 0.1 copy-done.1
  143.4 0.3 or_and_fusion.2
  143.7 2.0 fusion.76
  145.7 2.8 fusion.77
  148.6 0.8 copy-done
  149.4 3.0 fusion.78
  152.4 0.2 copy.51
  152.6 0.0 slice-start
  152.6 0.7 constant_dynamic-update-slice_fusion.2
  153.3 7.8 %fusion.83 = f32[2304,1,128]{0,2,1:T(8,128)} fusion(f32[2304,1,128]{0,2,1:T(8,128)} %get-tuple-element.421, pred[]{:T(512)S(6)} %compare.3, bf16[128,1,8,128]{3,2,0,1:T(8,128)(2,1)S(1)} %constant_dynamic-slice_fusion.2, f32[8,128]{1,0:T(8,128)S(1)} %broadcast_select_fusion.2, f32[8,128]{1,0:T(8,128)S(1)} %get-tuple-element.400, ...), kind=kOutput, calls=%fused_computation.17.clone.1 | convolution fusion | flops 618725376 | bytes 12361729 | tf_op jit(solution)/shard_map/while/body/eval_jaxpr/kgij,ikgd->jkd/dot_general | solution.py:41
  161.1 0.0 slice-done.1
  161.1 3.5 fusion.79
  164.6 3.7 fusion.80
  168.3 0.0 copy-start.2
  168.3 1.4 fusion.81
  169.7 1.0 fusion.82
  170.7 0.9 copy_dynamic-update-slice_fusion.2
  171.6 1.6 copy.28
  173.2 0.8 slice_bitcast_fusion
  174.0 0.0 reduce-scatter.8.cloned.1.call-update
  174.1 0.0 reduce-scatter.6.cloned.1.call-start
  174.1 0.3 copy.27
  174.4 0.8 slice_bitcast_fusion.1
  175.3 0.0 reduce-scatter.6.cloned.1.call-update
  175.3 0.0 reduce-scatter.4.cloned.1.call-start
  175.3 7.3 %convolution_convert_fusion.1 = bf16[256,4096]{1,0:T(8,128)(2,1)} fusion(bf16[256,1024]{0,1:T(8,128)(2,1)} %bitcast.211, bf16[1024,4096]{1,0:T(8,128)(2,1)} %param.15), kind=kOutput, calls=%fused_computation.47 | convolution fusion | flops 2148532224 | bytes 11010048 | tf_op jit(solution)/shard_map/dot_general | solution.py:117
  182.6 0.0 reduce-scatter.4.cloned.1.call-update
  182.6 2.1 reshape_reshape.3
  184.7 0.7 slice_bitcast_fusion.2
  185.4 71.2 %reduce-scatter.8.cloned.1.call-done = bf16[1,128,128]{2,1,0:T(8,128)(2,1)} async-done(((bf16[1,2048,128]{2,1,0:T(8,128)(2,1)}), bf16[1,128,128]{2,1,0:T(8,128)(2,1)}) %reduce-scatter.8.cloned.1.call-update) | async-done | bytes 32784 | tf_op jit(solution)/shard_map/reduce_scatter | solution.py:111
  256.6 87.8 %reduce-scatter.6.cloned.1.call-done = bf16[1,128,128]{2,1,0:T(8,128)(2,1)} async-done(((bf16[1,2048,128]{2,1,0:T(8,128)(2,1)}), bf16[1,128,128]{2,1,0:T(8,128)(2,1)}) %reduce-scatter.6.cloned.1.call-update) | async-done | bytes 32784 | tf_op jit(solution)/shard_map/reduce_scatter | solution.py:108
  344.4 31.4 %reduce-scatter.4.cloned.1.call-done = bf16[1,1,256,1024]{3,2,1,0:T(8,128)(2,1)} async-done(((bf16[1,1,256,4096]{3,2,1,0:T(8,128)(2,1)}), bf16[1,1,256,1024]{3,2,1,0:T(8,128)(2,1)}) %reduce-scatter.4.cloned.1.call-update) | async-done | bytes 524304 | tf_op jit(solution)/shard_map/reduce_scatter | solution.py:121
  (37 shorter events, 0.1 us)
Async XLA Ops:
  7.2 98.5 %all-gather.2.cloned.1.call-start = ((), (), s32[]{:S(2)}) async-start(), calls=%async_computation.3 | async-start | bytes 2621440 | tf_op jit(solution)/shard_map/all_gather | solution.py:62
  7.9 248.7 %reduce-scatter.8.cloned.1.call-start = ((), (), s32[]{:S(2)}) async-start(), calls=%async_computation.6 | async-start | bytes 557056 | tf_op jit(solution)/shard_map/reduce_scatter | solution.py:111
  113.9 0.8 copy-start.1
  115.0 5.7 %copy-start.3 = (bf16[2304,1,128]{2,0,1:T(8,128)(2,1)S(1)}, bf16[2304,1,128]{2,0,1:T(8,128)(2,1)}, u32[]{:S(2)}) copy-start(bf16[2304,1,128]{2,0,1:T(8,128)(2,1)} %get-tuple-element.439) | copy-start | bytes 1769476 | tf_op jit(solution)/shard_map/while
  117.0 3.6 copy-start
  123.9 8.2 %slice-start = ((s8[9437184]{0:T(1024)(128)(4,1)}), s8[4194304]{0:T(1024)(128)(4,1)S(1)}, s32[]{:S(2)}) async-start(s8[9437184]{0:T(1024)(128)(4,1)} %bitcast.206), calls=%async_computation.7 | async-start | bytes 8388608 | tf_op jit(solution)/shard_map/while
  124.6 7.4 %slice-start.1 = ((s8[9437184]{0:T(1024)(128)(4,1)}), s8[4194304]{0:T(1024)(128)(4,1)S(1)}, s32[]{:S(2)}) async-start(s8[9437184]{0:T(1024)(128)(4,1)} %bitcast.206), calls=%async_computation.8 | async-start | bytes 8388608 | tf_op jit(solution)/shard_map/while
  124.6 7.4 %slice-start.2 = ((s8[9437184]{0:T(1024)(128)(4,1)}), s8[1048576]{0:T(1024)(128)(4,1)S(1)}, s32[]{:S(2)}) async-start(s8[9437184]{0:T(1024)(128)(4,1)} %bitcast.206), calls=%async_computation.9 | async-start | bytes 2097152 | tf_op jit(solution)/shard_map/while
  124.6 7.4 %copy-start.4 = (bf16[2304,1,128]{2,0,1:T(8,128)(2,1)S(1)}, bf16[2304,1,128]{2,0,1:T(8,128)(2,1)}, u32[]{:S(2)}) copy-start(bf16[2304,1,128]{2,0,1:T(8,128)(2,1)} %get-tuple-element.439) | copy-start | bytes 1769476 | tf_op jit(solution)/shard_map/while
  139.3 3.3 copy-start.2
  142.6 0.8 copy-start.1
  143.7 5.7 %copy-start.3 = (bf16[2304,1,128]{2,0,1:T(8,128)(2,1)S(1)}, bf16[2304,1,128]{2,0,1:T(8,128)(2,1)}, u32[]{:S(2)}) copy-start(bf16[2304,1,128]{2,0,1:T(8,128)(2,1)} %get-tuple-element.439) | copy-start | bytes 1769476 | tf_op jit(solution)/shard_map/while
  145.7 3.6 copy-start
  152.6 8.5 %slice-start = ((s8[9437184]{0:T(1024)(128)(4,1)}), s8[4194304]{0:T(1024)(128)(4,1)S(1)}, s32[]{:S(2)}) async-start(s8[9437184]{0:T(1024)(128)(4,1)} %bitcast.206), calls=%async_computation.7 | async-start | bytes 8388608 | tf_op jit(solution)/shard_map/while
  153.3 7.8 %slice-start.1 = ((s8[9437184]{0:T(1024)(128)(4,1)}), s8[4194304]{0:T(1024)(128)(4,1)S(1)}, s32[]{:S(2)}) async-start(s8[9437184]{0:T(1024)(128)(4,1)} %bitcast.206), calls=%async_computation.8 | async-start | bytes 8388608 | tf_op jit(solution)/shard_map/while
  153.3 7.8 %slice-start.2 = ((s8[9437184]{0:T(1024)(128)(4,1)}), s8[1048576]{0:T(1024)(128)(4,1)S(1)}, s32[]{:S(2)}) async-start(s8[9437184]{0:T(1024)(128)(4,1)} %bitcast.206), calls=%async_computation.9 | async-start | bytes 2097152 | tf_op jit(solution)/shard_map/while
  153.3 7.8 %copy-start.4 = (bf16[2304,1,128]{2,0,1:T(8,128)(2,1)S(1)}, bf16[2304,1,128]{2,0,1:T(8,128)(2,1)}, u32[]{:S(2)}) copy-start(bf16[2304,1,128]{2,0,1:T(8,128)(2,1)} %get-tuple-element.439) | copy-start | bytes 1769476 | tf_op jit(solution)/shard_map/while
  168.3 3.3 copy-start.2
  174.1 170.4 %reduce-scatter.6.cloned.1.call-start = ((), (), s32[]{:S(2)}) async-start(), calls=%async_computation.5 | async-start | bytes 557056 | tf_op jit(solution)/shard_map/reduce_scatter | solution.py:108
  175.3 200.6 %reduce-scatter.4.cloned.1.call-start = ((), (), s32[]{:S(2)}) async-start(), calls=%async_computation.4 | async-start | bytes 2621440 | tf_op jit(solution)/shard_map/reduce_scatter | solution.py:121
Sparse Core Ops, SparseCore 0:
  9.8 40.0 all-gather.1
  174.2 82.3 reduce-scatter.7
  261.0 83.3 reduce-scatter.5
  347.4 28.4 reduce-scatter.3
where the time goes:
time: 384 us; the launch traced here: 382 us
  waiting for transfers between devices  191 us (50%)
  blocking collectives  93.9 us (24%)
  matrix products  50.8 us (13%)
  other arithmetic  17.5 us (5%)
  local copies, waits for them, and re-layouts  14.8 us (4%)
  between operations  13.8 us (4%)
    reduce_scatter x1, waiting for transfers between devices, per_device(): lax.psum_scatter(prompt_kgrad.astype(jnp.bfloat16), 'group', scatter_dime...  87.8 us
    reduce_scatter x1, waiting for transfers between devices, per_device(): lax.psum_scatter(prompt_vgrad.astype(jnp.bfloat16), 'group', scatter_dime...  71.2 us
    all_gather x1, blocking collectives, per_device(): lax.all_gather(prompt_keys, 'group', axis=1, tiled=True)  51.9 us
    all_gather x1, blocking collectives, per_device(): lax.all_gather(prompt_values, 'group', axis=1, tiled=True)  42 us
    reduce_scatter x1, waiting for transfers between devices, per_device(): lax.psum_scatter(partial_term.reshape(1, 1, slot_count, -1).astype(jnp.bf...  31.4 us
    dot_general x2, matrix products, block_pass(): jnp.einsum('kgij,ikgd->jkd', weights_low, dout_rows, preferred_element_ty...  15.2 us
  transfers between devices with their start and end apart: 4, of which 3 were waited for; matrix products, arithmetic and copies ran while one was open for 4% of the time, Pallas kernels for 0%

commit v1 on v0

v1 whole, which is shorter than its diff:
```python
import functools

import jax
import jax.numpy as jnp
from jax import lax
from jax.experimental import pallas as pl
from jax.experimental.pallas import tpu as pltpu
from jax.sharding import PartitionSpec as P

HD = 128
HEADS = 8
SLOTS = 256
NEG_FILL = -1e30
LOG2E = 1.4426950408889634
SCALE = HD**-0.5
F32 = jnp.float32
BF16 = jnp.bfloat16
VMEM_LIMIT = 48 * 1024 * 1024


def dot_nn(a, b):
    return lax.dot_general(a, b, (((1,), (0,)), ((), ())), preferred_element_type=F32)


def dot_nt(a, b):
    return lax.dot_general(a, b, (((1,), (1,)), ((), ())), preferred_element_type=F32)


def attend(q, tables, turned, causal, weights):
    scores = []
    for table, masked in zip(tables, causal):
        s = dot_nt(table[:, :HD], q) * (SCALE * LOG2E)
        if masked:
            key = lax.broadcasted_iota(jnp.int32, s.shape, 0)
            token = lax.broadcasted_iota(jnp.int32, s.shape, 1)
            s = jnp.where(key <= token, s, NEG_FILL)
        scores.append(s)
    top = functools.reduce(jnp.maximum, [jnp.max(s, axis=0, keepdims=True) for s in scores])
    total, acc = 0.0, 0.0
    for s, vt, w in zip(scores, turned, weights):
        p = jnp.exp2(s - top)
        total = total + jnp.sum(p, axis=0, keepdims=True)
        low = p.astype(BF16)
        w[0] = low
        acc = acc + dot_nn(vt[...], low)
    return top, total, acc


def turn(step, tables, turned, low):
    @pl.when(step == 0)
    def _():
        for table, t in zip(tables, turned):
            t[...] = table[:, low : low + HD].T


def fwd_kernel(count, causal, *refs):
    q = refs[0]
    tables = refs[1 : 1 + count]
    weights = refs[1 + count : 1 + 2 * count]
    top_ref, total_ref, acc_ref = refs[1 + 2 * count : 4 + 2 * count]
    turned = refs[4 + 2 * count :]
    turn(pl.program_id(0), tables, turned, HD)
    top, total, acc = attend(q[...], tables, turned, causal, weights)
    top_ref[0], total_ref[0], acc_ref[...] = top, total, acc


def merge_kernel(count, earlier, *refs):
    length, q, dout = refs[:3]
    tables = refs[3 : 3 + count]
    at = 3 + count
    old = [refs[at + 3 * i : at + 3 * i + 3] for i in range(earlier)]
    at += 3 * earlier
    weights = refs[at : at + count]
    at += count
    alphas = refs[at : at + earlier + 1]
    delta_ref, mixed_ref = refs[at + earlier + 1 : at + earlier + 3]
    turned = refs[at + earlier + 3 :]
    turn(pl.program_id(0), tables, turned, HD)
    parts = [(t[0], l[0], a[...]) for t, l, a in old]
    parts.append(attend(q[...], tables, turned, (False,) * count, weights))
    top = functools.reduce(jnp.maximum, [t for t, _, _ in parts])
    factors = [jnp.exp2(t - top) for t, _, _ in parts]
    total = sum(f * l for f, (_, l, _) in zip(factors, parts))
    live = lax.broadcasted_iota(jnp.int32, top.shape, 1) < length[0, 0]
    inverse = jnp.where(live, 1.0 / total, 0.0)
    mixed = 0.0
    for f, (_, _, acc), alpha in zip(factors, parts, alphas):
        alpha[0] = f * inverse
        mixed = mixed + (f * inverse) * acc
    delta_ref[0] = jnp.sum(mixed * dout[...].astype(F32), axis=0, keepdims=True)
    mixed_ref[...] = mixed.astype(BF16)


def bwd_kernel(count, first, last, *refs):
    q, dout, alpha, delta = refs[:4]
    tables = refs[4 : 4 + count]
    weights = refs[4 + count : 4 + 2 * count]
    at = 4 + 2 * count
    if not first:
        dq_in = refs[at]
        at += 1
    grads = refs[at : at + count]
    dq_ref = refs[at + count]
    turned = refs[at + count + 1 : at + 2 * count + 1]
    sums = refs[at + 2 * count + 1 :]
    step = pl.program_id(0)
    turn(step, tables, turned, 0)

    @pl.when(step == 0)
    def _():
        for s in sums:
            s[...] = jnp.zeros_like(s)

    da = (dout[...].astype(F32) * alpha[0]).astype(BF16)
    shift = delta[0] * alpha[0]
    dq = 0.0 if first else dq_in[...]
    for table, w, kt, s in zip(tables, weights, turned, sums):
        p = w[0]
        dp = dot_nn(table[:, HD:], da)
        ds = (p.astype(F32) * (dp - shift)).astype(BF16)
        s[:, HD:] += dot_nt(p, da)
        s[:, :HD] += dot_nn(ds, q[...])
        dq = dq + dot_nn(kt[...], ds)
    if last:
        dq_ref[...] = (dq * SCALE).T.astype(dq_ref.dtype)
    else:
        dq_ref[...] = dq

    @pl.when(step == HEADS - 1)
    def _():
        for s, g in zip(sums, grads):
            g[:, :HD] = (s[:, :HD] * SCALE).astype(g.dtype)
            g[:, HD:] = s[:, HD:].astype(g.dtype)


Q_SPEC = pl.BlockSpec((SLOTS, HD), lambda h: (0, h))
T_SPEC = pl.BlockSpec((HD, SLOTS), lambda h: (h, 0))
STAT_SPEC = pl.BlockSpec((1, 1, SLOTS), lambda h: (h, 0, 0))
STAT = jax.ShapeDtypeStruct((HEADS, 1, SLOTS), F32)
WIDE = jax.ShapeDtypeStruct((HEADS * HD, SLOTS), F32)
PARAMS = dict(compiler_params=pltpu.CompilerParams(vmem_limit_bytes=VMEM_LIMIT), grid=(HEADS,))


def whole(table):
    return pl.BlockSpec(table.shape, lambda h: (0, 0))


def weight_specs(tables):
    specs = [pl.BlockSpec((1, t.shape[0], SLOTS), lambda h: (h, 0, 0)) for t in tables]
    shapes = [jax.ShapeDtypeStruct((HEADS, t.shape[0], SLOTS), BF16) for t in tables]
    return specs, shapes


def cost(tables, dots):
    rows = sum(t.shape[0] for t in tables)
    area = rows * SLOTS * HEADS
    return pl.CostEstimate(
        flops=4 * dots * area * HD, bytes_accessed=2 * area + 4 * 1024 * 1024, transcendentals=area
    )


def forward(q, tables, causal):
    specs, shapes = weight_specs(tables)
    n = len(tables)
    out = pl.pallas_call(
        functools.partial(fwd_kernel, n, causal),
        in_specs=[Q_SPEC] + [whole(t) for t in tables],
        out_specs=specs + [STAT_SPEC, STAT_SPEC, T_SPEC],
        out_shape=shapes + [STAT, STAT, WIDE],
        scratch_shapes=[pltpu.VMEM((HD, t.shape[0]), BF16) for t in tables],
        cost_estimate=cost(tables, 2),
        name="forward",
        **PARAMS,
    )(q, *tables)
    return out[:n], out[n:]


def forward_merge(length, q, dout, tables, old):
    specs, shapes = weight_specs(tables)
    n = len(tables)
    e = len(old)
    out = pl.pallas_call(
        functools.partial(merge_kernel, n, e),
        in_specs=[pl.BlockSpec(memory_space=pltpu.SMEM), Q_SPEC, T_SPEC]
        + [whole(t) for t in tables]
        + [STAT_SPEC, STAT_SPEC, T_SPEC] * e,
        out_specs=specs + [STAT_SPEC] * (e + 2) + [T_SPEC],
        out_shape=shapes + [STAT] * (e + 2) + [jax.ShapeDtypeStruct((HEADS * HD, SLOTS), BF16)],
        scratch_shapes=[pltpu.VMEM((HD, t.shape[0]), BF16) for t in tables],
        cost_estimate=cost(tables, 2),
        name="forward_merge",
        **PARAMS,
    )(length, q, dout, *tables, *[x for part in old for x in part])
    return out[:n], out[n : n + e + 1], out[n + e + 1], out[n + e + 2]


def backward(q, dout, alpha, delta, tables, weights, kinds, dq, last):
    specs, _ = weight_specs(tables)
    n = len(tables)
    out = pl.pallas_call(
        functools.partial(bwd_kernel, n, dq is None, last),
        in_specs=[Q_SPEC, T_SPEC, STAT_SPEC, STAT_SPEC]
        + [whole(t) for t in tables]
        + specs
        + ([] if dq is None else [T_SPEC]),
        out_specs=[whole(t) for t in tables] + [Q_SPEC if last else T_SPEC],
        out_shape=[jax.ShapeDtypeStruct(t.shape, k) for t, k in zip(tables, kinds)]
        + [jax.ShapeDtypeStruct((SLOTS, HEADS * HD), BF16) if last else WIDE],
        scratch_shapes=[pltpu.VMEM((HD, t.shape[0]), BF16) for t in tables]
        + [pltpu.VMEM(t.shape, F32) for t in tables],
        cost_estimate=cost(tables, 4),
        name="backward",
        **PARAMS,
    )(q, dout, alpha, delta, *tables, *weights, *([] if dq is None else [dq]))
    return out[:n], out[n]


def group_shift(dz, dx):
    return [(z * 4 + x, (z + dz) % 4 * 4 + (x + dx) % 4) for z in range(4) for x in range(4)]


def tensor_flip(bits):
    return [(t, t ^ bits) for t in range(4)]


def per_device(
    queries, comp_keys, comp_values, prompt_keys, prompt_values, out_weight, cotangent, lengths
):
    q = queries[0, 0]
    cot = cotangent[0, 0]

    def over_z(a, s):
        return lax.ppermute(a, "group", group_shift(s, 0))

    def over_x(a, s):
        return lax.ppermute(a, "group", group_shift(0, s))

    def to_core(a):
        return lax.ppermute(a, "tensor", tensor_flip(1))

    def to_chip(a):
        return lax.ppermute(a, "tensor", tensor_flip(2))

    own = jnp.concatenate([prompt_keys[0], prompt_values[0]], axis=1)
    comp = jnp.concatenate([comp_keys[0, 0], comp_values[0, 0]], axis=1)
    chunk0 = jnp.concatenate([own] + [over_z(own, s) for s in (1, 3, 2)], axis=0)
    chunk1, chunk3, chunk2 = [over_x(chunk0, s) for s in (1, 3, 2)]

    me = lax.axis_index("tensor")

    def columns(bits):
        return lax.dynamic_slice_in_dim(out_weight, (me ^ bits) * 1024, 1024, 1)

    cot_chip = to_chip(cot)
    cot_core = to_core(cot)
    cot_diag = to_core(cot_chip)
    dout = sum(
        dot_nt(columns(bits), part)
        for bits, part in ((0, cot), (1, cot_core), (2, cot_chip), (3, cot_diag))
    ).astype(BF16)

    w0, part0 = forward(q, [chunk0, comp], (False, True))
    w13, part13 = forward(q, [chunk1, chunk3], (False, False))
    w2, (alpha0, alpha13, alpha2), delta, mixed = forward_merge(
        lengths, q, dout, [chunk2], [part0, part13]
    )

    (g2,), dq = backward(q, dout, alpha2, delta, [chunk2], w2, (BF16,), None, False)
    (g1, g3), dq = backward(q, dout, alpha13, delta, [chunk1, chunk3], w13, (BF16, BF16), dq, False)

    def partial_out(bits):
        block = lax.dot_general(
            mixed, columns(bits), (((0,), (0,)), ((), ())), preferred_element_type=F32
        )
        return block.astype(BF16)

    other = to_core(jnp.concatenate([partial_out(1), partial_out(3)], axis=0))
    pair_mine = partial_out(0).astype(F32) + other[:SLOTS].astype(F32)
    pair_far = partial_out(2).astype(F32) + other[SLOTS:].astype(F32)
    far = to_chip(pair_far.astype(BF16))
    output = (pair_mine + far.astype(F32)).astype(BF16)

    (g0, gcomp), dq = backward(q, dout, alpha0, delta, [chunk0, comp], w0, (F32, BF16), dq, True)

    back2, back1, back3 = over_x(g2, -2), over_x(g1, -1), over_x(g3, -3)
    rows = g0 + back2.astype(F32) + back1.astype(F32) + back3.astype(F32)
    n = own.shape[0]
    sent = rows.astype(BF16)
    total = rows[:n]
    for i, s in enumerate((1, 3, 2)):
        total = total + over_z(sent[(i + 1) * n : (i + 2) * n], -s).astype(F32)
    total = total.astype(BF16)
    return (
        output[None, None],
        dq[None, None],
        gcomp[None, None, :, :HD],
        gcomp[None, None, :, HD:],
        total[None, :, :HD],
        total[None, :, HD:],
    )


def solution(mesh):
    wide = P("dp", "group", None, "tensor")
    rows = P("dp", "group", "tensor")
    return jax.shard_map(
        per_device,
        mesh=mesh,
        in_specs=(wide, wide, wide, rows, rows, P("tensor", None), wide, P("dp", "group")),
        out_specs=(wide, wide, wide, wide, rows, rows),
        check_vma=False,
    )
```

time: 384 us -> 115 us (0.30)
  waiting for transfers between devices: 191 us -> 23.3 us
  blocking collectives: 93.9 us -> 0 us
  Pallas kernels: 0 us -> 39.5 us
  matrix products: 50.8 us -> 15.6 us
  starting transfers between devices: 0.16 us -> 30.8 us
  other arithmetic: 17.5 us -> 1.04 us
  between operations: 13.8 us -> 1.51 us
  local copies, waits for them, and re-layouts: 14.8 us -> 2.68 us
    reduce_scatter x3 -> x0, waiting for transfers between devices: 190 us -> none  [the longest x1 87.8 us: per_device(): lax.psum_scatter(prompt_kgrad.astype(jnp.bfloat16), 'group', scatter_dime...]
    all_gather x2 -> x0, blocking collectives: 93.9 us -> none  [the longest x1 51.9 us: per_device(): lax.all_gather(prompt_keys, 'group', axis=1, tiled=True)]
    pallas_call x0 -> x6, Pallas kernels: none -> 39.5 us  [the longest x3 20.8 us: backward(): pl.pallas_call(functools.partial(bwd_kernel, n, dq is None, last), in_spe...]
    dot_general x14 -> x8, matrix products: 50.8 us -> 15.6 us  [the longest x4 8.64 us: dot_nt(): lax.dot_general(a, b, (((1,), (1,)), ((), ())), preferred_element_type=F32)]
    ppermute x0 -> x17, starting transfers between devices: none -> 30.8 us  [the longest x6 15.8 us: over_z(): return lax.ppermute(a, 'group', group_shift(s, 0))]
    ppermute x0 -> x17, waiting for transfers between devices: none -> 23.3 us  [the longest x2 9.26 us: to_chip(): return lax.ppermute(a, 'tensor', tensor_flip(2))]
    another operation x2 -> x0, other arithmetic: 7.31 us -> none
    reduce_sum x2 -> x0, other arithmetic: 5.6 us -> none  [block_pass(): normer = jnp.sum(expo, axis=-1, keepdims=True)]
  transfers between devices with their start and end apart: 4 -> 17, of which waited for: 3 -> 6; matrix products, arithmetic and copies ran while one was open for 4% -> 12% of each run, Pallas kernels for 0% -> 30%
where the time goes in v1:
time: 115 us; the launch traced here: 114 us
  Pallas kernels  39.5 us (34%)
  starting transfers between devices  30.8 us (27%)
  waiting for transfers between devices  23.3 us (20%)
  matrix products  15.6 us (14%)
  local copies, waits for them, and re-layouts  2.68 us (2%)
  between operations  1.51 us (1%)
    pallas_call x3, Pallas kernels, backward(): pl.pallas_call(functools.partial(bwd_kernel, n, dq is None, last), in_spe...  20.8 us
    ppermute x6, starting transfers between devices, over_z(): return lax.ppermute(a, 'group', group_shift(s, 0))  15.8 us
    pallas_call x2, Pallas kernels, forward(): pl.pallas_call(functools.partial(fwd_kernel, n, causal), in_specs=[Q_SPEC...  13.6 us
    ppermute x6, starting transfers between devices, over_x(): return lax.ppermute(a, 'group', group_shift(0, s))  10.5 us
    ppermute x2, waiting for transfers between devices, to_chip(): return lax.ppermute(a, 'tensor', tensor_flip(2))  9.26 us
    ppermute x6, waiting for transfers between devices, over_z(): return lax.ppermute(a, 'group', group_shift(s, 0))  8.84 us
    dot_general x4, matrix products, dot_nt(): lax.dot_general(a, b, (((1,), (1,)), ((), ())), preferred_element_type=F32)  8.64 us
    dot_general x4, matrix products, partial_out(): lax.dot_general(mixed, columns(bits), (((0,), (0,)), ((), ())), preferred...  6.94 us
  transfers between devices with their start and end apart: 17, of which 6 were waited for; matrix products, arithmetic and copies ran while one was open for 12% of the time, Pallas kernels for 30%

profile of v1, /device:TPU:8, one launch (start us, length us, event | category | flops | bytes accessed | tf_op | source)
XLA Modules:
  0.0 114.4 jit_solution(5046427505833165660)
XLA Ops:
  0.6 0.0 copy-start.6
  0.6 0.0 copy-start.5
  0.7 2.0 %collective-permute-start.1 = (bf16[256,1024]{1,0:T(8,128)(2,1)}, bf16[256,1024]{1,0:T(8,128)(2,1)}, u32[]{:S(2)}, u32[]{:S(2)}) collective-permute-start(bf16[256,1024]{1,0:T(8,128)(2,1)} %bitcast.32), channel_id=1, source_target_pairs={{0,2},{1,3},{2,0},{3,1},{4,6},{5,7},{6,4},{7,5},{8,10},{9,11},{10,... | collective-permute-start | bytes 1572872 | tf_op jit(solution)/shard_map/ppermute | solution.py:242
  2.7 0.0 collective-permute-start
  2.7 0.8 pad_maximum_fusion.3
  3.4 3.3 %collective-permute-start.3 = (bf16[128,256]{1,0:T(8,128)(2,1)S(1)}, bf16[128,256]{1,0:T(8,128)(2,1)S(1)}, u32[]{:S(2)}, u32[]{:S(2)}) collective-permute-start(bf16[128,256]{1,0:T(8,128)(2,1)S(1)} %pad_maximum_fusion.3), channel_id=1, source_target_pairs={{0,16},{4,20},{8,24},{12,28},{16,32},{20,36},{24,40},{28,44},{32,4... | collective-permute-start | bytes 196616 | tf_op jit(solution)/shard_map/ppermute | solution.py:233
  6.8 2.2 %collective-permute-start.4 = (bf16[128,256]{1,0:T(8,128)(2,1)S(1)}, bf16[128,256]{1,0:T(8,128)(2,1)S(1)}, u32[]{:S(2)}, u32[]{:S(2)}) collective-permute-start(bf16[128,256]{1,0:T(8,128)(2,1)S(1)} %pad_maximum_fusion.3), channel_id=1, source_target_pairs={{0,48},{4,52},{8,56},{12,60},{16,0},{20,4},{24,8},{28,12},{32,16},... | collective-permute-start | bytes 196616 | tf_op jit(solution)/shard_map/ppermute | solution.py:233
  9.0 4.9 %collective-permute-start.5 = (bf16[128,256]{1,0:T(8,128)(2,1)S(1)}, bf16[128,256]{1,0:T(8,128)(2,1)S(1)}, u32[]{:S(2)}, u32[]{:S(2)}) collective-permute-start(bf16[128,256]{1,0:T(8,128)(2,1)S(1)} %pad_maximum_fusion.3), channel_id=1, source_target_pairs={{0,32},{4,36},{8,40},{12,44},{16,48},{20,52},{24,56},{28,60},{32,0... | collective-permute-start | bytes 196616 | tf_op jit(solution)/shard_map/ppermute | solution.py:233
  13.9 3.5 %fusion.14 = f32[1024,256]{1,0:T(8,128)} fusion(bf16[1024,4096]{1,0:T(8,128)(2,1)} %param.13, s32[]{:T(128)S(6)} %select_n.16, bf16[1,1,256,1024]{3,2,1,0:T(8,128)(2,1)} %param.14), kind=kOutput, calls=%fused_computation.14 | convolution fusion | flops 536870912 | bytes 3670020 | tf_op jit(solution)/shard_map/dot_general | solution.py:26
  18.1 6.1 %collective-permute-done.3 = bf16[128,256]{1,0:T(8,128)(2,1)S(1)} collective-permute-done((bf16[128,256]{1,0:T(8,128)(2,1)S(1)}, bf16[128,256]{1,0:T(8,128)(2,1)S(1)}, u32[]{:S(2)}, u32[]{:S(2)}) %collective-permute-start.3) | collective-permute-done | bytes 65568 | tf_op jit(solution)/shard_map/ppermute | solution.py:233
  24.1 0.0 collective-permute-done.4
  24.1 1.6 %collective-permute-done.5 = bf16[128,256]{1,0:T(8,128)(2,1)S(1)} collective-permute-done((bf16[128,256]{1,0:T(8,128)(2,1)S(1)}, bf16[128,256]{1,0:T(8,128)(2,1)S(1)}, u32[]{:S(2)}, u32[]{:S(2)}) %collective-permute-start.5) | collective-permute-done | bytes 65568 | tf_op jit(solution)/shard_map/ppermute | solution.py:233
  25.7 0.0 copy-done.6
  25.7 0.0 copy-done.5
  25.8 1.6 %collective-permute-start.7 = (bf16[512,256]{1,0:T(8,128)(2,1)S(1)}, bf16[512,256]{1,0:T(8,128)(2,1)S(1)}, u32[]{:S(2)}, u32[]{:S(2)}) collective-permute-start(bf16[512,256]{1,0:T(8,128)(2,1)S(1)} %pad_maximum_fusion.1.refs_1_.refs_4_), channel_id=1, source_target_pairs={{0,4},{4,8},{8,12},{12,0},{16,20},{20,24},{24,28},{28,16},{32,36},... | collective-permute-start | bytes 786440 | tf_op jit(solution)/shard_map/ppermute | solution.py:236
  27.3 1.7 %collective-permute-start.8 = (bf16[512,256]{1,0:T(8,128)(2,1)S(1)}, bf16[512,256]{1,0:T(8,128)(2,1)S(1)}, u32[]{:S(2)}, u32[]{:S(2)}) collective-permute-start(bf16[512,256]{1,0:T(8,128)(2,1)S(1)} %pad_maximum_fusion.1.refs_1_.refs_4_), channel_id=1, source_target_pairs={{0,12},{4,0},{8,4},{12,8},{16,28},{20,16},{24,20},{28,24},{32,44},... | collective-permute-start | bytes 786440 | tf_op jit(solution)/shard_map/ppermute | solution.py:236
  29.1 0.0 copy-done.7
  29.1 0.0 copy-done.8
  29.1 1.9 %collective-permute-start.6 = (bf16[512,256]{1,0:T(8,128)(2,1)S(1)}, bf16[512,256]{1,0:T(8,128)(2,1)S(1)}, u32[]{:S(2)}, u32[]{:S(2)}) collective-permute-start(bf16[512,256]{1,0:T(8,128)(2,1)S(1)} %pad_maximum_fusion.1.refs_1_.refs_4_), channel_id=1, source_target_pairs={{0,8},{4,12},{8,0},{12,4},{16,24},{20,28},{24,16},{28,20},{32,40},... | collective-permute-start | bytes 786440 | tf_op jit(solution)/shard_map/ppermute | solution.py:236
  31.0 0.0 copy-done
  31.0 6.0 %forward.2 = (bf16[8,512,256]{2,1,0:T(8,128)(2,1)S(1)}, bf16[8,256,256]{2,1,0:T(8,128)(2,1)S(1)}, f32[8,1,256]{2,1,0:T(1,128)S(1)}, f32[8,1,256]{2,1,0:T(1,128)S(1)}, f32[1024,256]{1,0:T(8,128)S(1)}) custom-call(bf16[256,1024]{1,0:T(8,128)(2,1)S(1)} %bitcast.26, bf16[512,256]{1,0:T(8,128)(2,1)S(1)} %pad_maximum_fusion.1.refs_1_.refs_4_, ...), custom_call_target="tpu_custom_call" | custom-call | flops 1610612736 | bytes 7340032 | tf_op jit(solution)/shard_map/forward/pallas_call | solution.py:165
  37.0 0.0 copy-start.1
  37.0 1.3 %copy-done.1 = bf16[8,512,256]{2,1,0:T(8,128)(2,1)} copy-done((bf16[8,512,256]{2,1,0:T(8,128)(2,1)}, bf16[8,512,256]{2,1,0:T(8,128)(2,1)S(1)}, u32[]{:S(2)}) %copy-start.1) | copy-done | bytes 2097176
  38.3 0.0 collective-permute-done.7.refs_1_.refs_4_
  38.3 0.0 collective-permute-done.8.refs_2_.refs_5_
  38.3 7.7 %forward.3 = (bf16[8,512,256]{2,1,0:T(8,128)(2,1)S(1)}, bf16[8,512,256]{2,1,0:T(8,128)(2,1)}, f32[8,1,256]{2,1,0:T(1,128)S(1)}, f32[8,1,256]{2,1,0:T(1,128)S(1)}, f32[1024,256]{1,0:T(8,128)S(1)}) custom-call(bf16[256,1024]{1,0:T(8,128)(2,1)S(1)} %bitcast.27, bf16[512,256]{1,0:T(8,128)(2,1)S(1)} %collective-permute-done.7.refs_1_.refs_4_, ...), custom_call_target="tpu_custom_call" | custom-call | flops 2147483648 | bytes 8388608 | tf_op jit(solution)/shard_map/forward/pallas_call | solution.py:165
  46.0 0.0 collective-permute-done.1
  46.0 0.1 collective-permute-start.2
  46.1 0.0 copy-done.3
  46.1 2.6 %fusion.6 = f32[1024,256]{1,0:T(8,128)S(1)} fusion(bf16[256,1024]{1,0:T(8,128)(2,1)} %collective-permute-done.1, bf16[1024,4096]{1,0:T(8,128)(2,1)S(1)} %copy-done.3, s32[]{:T(128)S(6)} %select_n.18), kind=kOutput, calls=%fused_computation.6 | convolution fusion | flops 536870912 | bytes 3670020 | tf_op jit(solution)/shard_map/dot_general | solution.py:26
  48.7 0.0 collective-permute-done
  48.7 0.0 copy-done.4
  48.7 1.8 %fusion.19 = f32[1024,256]{1,0:T(8,128)S(1)} fusion(f32[1024,256]{1,0:T(8,128)S(1)} %fusion.6, f32[1024,256]{1,0:T(8,128)S(1)} %copy-done.4, bf16[256,1024]{1,0:T(8,128)(2,1)} %collective-permute-done, bf16[1024,4096]{1,0:T(8,128)(2,1)S(1)} %copy-done.3, s32[]{:T(128)S(6)} %select_n.17), kind=kOutput, calls=%fused_computation.17 | convolution fusion | flops 537395200 | bytes 5767172 | tf_op jit(solution)/shard_map/dot_general | solution.py:26
  50.6 0.0 collective-permute-done.2
  50.6 0.8 fusion.25.refs_2_.refs_1_
  51.4 0.0 collective-permute-done.6.refs_3_.refs_4_
  51.4 5.0 %forward_merge.1 = (bf16[8,512,256]{2,1,0:T(8,128)(2,1)S(1)}, f32[8,1,256]{2,1,0:T(1,128)S(1)}, f32[8,1,256]{2,1,0:T(1,128)S(1)}, f32[8,1,256]{2,1,0:T(1,128)S(1...) custom-call(s32[1,1]{1,0:T(1,128)S(6)} %copy.14.refs_0_, bf16[256,1024]{1,0:T(8,128)(2,1)S(1)} %bitcast.28, ...), custom_call_target="tpu_custom_call" | custom-call | flops 1073741824 | bytes 6291456 | tf_op jit(solution)/shard_map/forward_merge/pallas_call | solution.py:182
  56.4 0.7 fusion.31
  57.1 0.7 fusion.37
  57.9 0.1 pad_maximum_fusion
  58.0 0.3 collective-permute-start.9
  58.2 3.8 %backward.3 = (bf16[512,256]{1,0:T(8,128)(2,1)S(1)}, f32[1024,256]{1,0:T(8,128)S(1)}) custom-call(bf16[256,1024]{1,0:T(8,128)(2,1)S(1)} %bitcast.29, bf16[1024,256]{1,0:T(8,128)(2,1)S(1)} %fusion.25.refs_2_.refs_1_, f32[8,1,256]{2,1,0:T(1,128)S(1)} %get-tuple-element.44.refs_2_, f32[8,1,256]{2,1,0:T(1,128)S(1)} %get-tuple-element.38.refs_3_, ...), custom_call_target="tpu_custom_call" | custom-call | flops 2147483648 | bytes 6291456 | tf_op jit(solution)/shard_map/backward/pallas_call | solution.py:200
  62.1 8.5 %backward.4 = (bf16[512,256]{1,0:T(8,128)(2,1)S(1)}, bf16[512,256]{1,0:T(8,128)(2,1)S(1)}, f32[1024,256]{1,0:T(8,128)S(1)}) custom-call(bf16[256,1024]{1,0:T(8,128)(2,1)S(1)} %bitcast.30, bf16[1024,256]{1,0:T(8,128)(2,1)S(1)} %fusion.25.refs_2_.refs_1_, f32[8,1,256]{2,1,0:T(1,128)S(1)} %get-tuple-element.41.refs_2_, ...), custom_call_target="tpu_custom_call" | custom-call | flops 4294967296 | bytes 8388608 | tf_op jit(solution)/shard_map/backward/pallas_call | solution.py:200
  70.6 3.8 %collective-permute-start.12 = (bf16[512,256]{1,0:T(8,128)(2,1)S(1)}, bf16[512,256]{1,0:T(8,128)(2,1)S(1)}, u32[]{:S(2)}, u32[]{:S(2)}) collective-permute-start(bf16[512,256]{1,0:T(8,128)(2,1)S(1)} %get-tuple-element.52), channel_id=1, source_target_pairs={{0,12},{4,0},{8,4},{12,8},{16,28},{20,16},{24,20},{28,24},{32,44},... | collective-permute-start | bytes 786440 | tf_op jit(solution)/shard_map/ppermute | solution.py:236
  74.4 0.0 collective-permute-start.13
  74.4 1.6 %collective-permute-start.11 = (bf16[512,256]{1,0:T(8,128)(2,1)S(1)}, bf16[512,256]{1,0:T(8,128)(2,1)S(1)}, u32[]{:S(2)}, u32[]{:S(2)}) collective-permute-start(bf16[512,256]{1,0:T(8,128)(2,1)S(1)} %get-tuple-element.51), channel_id=1, source_target_pairs={{0,8},{4,12},{8,0},{12,4},{16,24},{20,28},{24,16},{28,20},{32,40},... | collective-permute-start | bytes 786440 | tf_op jit(solution)/shard_map/ppermute | solution.py:236
  75.9 8.5 %backward.5 = (f32[512,256]{1,0:T(8,128)S(1)}, bf16[256,256]{1,0:T(8,128)(2,1)S(1)}, bf16[256,1024]{1,0:T(8,128)(2,1)}) custom-call(bf16[256,1024]{1,0:T(8,128)(2,1)S(1)} %bitcast.31, bf16[1024,256]{1,0:T(8,128)(2,1)S(1)} %fusion.25.refs_2_.refs_1_, f32[8,1,256]{2,1,0:T(1,128)S(1)} %get-tuple-element.37.refs_2_, f32[8,1,256]{2,1,0:T(1,128)S(1)} %get-tuple-element.38.refs_3_, ...), custom_call_target="tpu_custom_call" | custom-call | flops 3221225472 | bytes 7340032 | tf_op jit(solution)/shard_map/backward/pallas_call | solution.py:200
  84.4 1.8 %collective-permute-done.12 = bf16[512,256]{1,0:T(8,128)(2,1)S(1)} collective-permute-done((bf16[512,256]{1,0:T(8,128)(2,1)S(1)}, bf16[512,256]{1,0:T(8,128)(2,1)S(1)}, u32[]{:S(2)}, u32[]{:S(2)}) %collective-permute-start.12) | collective-permute-done | bytes 262176 | tf_op jit(solution)/shard_map/ppermute | solution.py:236
  86.2 3.4 %collective-permute-done.13 = bf16[512,256]{1,0:T(8,128)(2,1)S(1)} collective-permute-done((bf16[512,256]{1,0:T(8,128)(2,1)S(1)}, bf16[512,256]{1,0:T(8,128)(2,1)S(1)}, u32[]{:S(2)}, u32[]{:S(2)}) %collective-permute-start.13) | collective-permute-done | bytes 262176 | tf_op jit(solution)/shard_map/ppermute | solution.py:236
  89.6 0.0 collective-permute-done.11
  89.6 0.1 fusion.76
  89.8 1.9 %collective-permute-start.14 = (bf16[128,256]{1,0:T(8,128)(2,1)S(1)}, bf16[128,256]{1,0:T(8,128)(2,1)S(1)}, u32[]{:S(2)}, u32[]{:S(2)}) collective-permute-start(bf16[128,256]{1,0:T(8,128)(2,1)S(1)} %get-tuple-element.56), channel_id=1, source_target_pairs={{0,48},{4,52},{8,56},{12,60},{16,0},{20,4},{24,8},{28,12},{32,16},... | collective-permute-start | bytes 196616 | tf_op jit(solution)/shard_map/ppermute | solution.py:233
  91.6 1.1 %collective-permute-start.15 = (bf16[128,256]{1,0:T(8,128)(2,1)S(1)}, bf16[128,256]{1,0:T(8,128)(2,1)S(1)}, u32[]{:S(2)}, u32[]{:S(2)}) collective-permute-start(bf16[128,256]{1,0:T(8,128)(2,1)S(1)} %get-tuple-element.58), channel_id=1, source_target_pairs={{0,16},{4,20},{8,24},{12,28},{16,32},{20,36},{24,40},{28,44},{32,4... | collective-permute-start | bytes 196616 | tf_op jit(solution)/shard_map/ppermute | solution.py:233
  92.8 2.3 %collective-permute-start.16 = (bf16[128,256]{1,0:T(8,128)(2,1)S(1)}, bf16[128,256]{1,0:T(8,128)(2,1)S(1)}, u32[]{:S(2)}, u32[]{:S(2)}) collective-permute-start(bf16[128,256]{1,0:T(8,128)(2,1)S(1)} %get-tuple-element.57), channel_id=1, source_target_pairs={{0,32},{4,36},{8,40},{12,44},{16,48},{20,52},{24,56},{28,60},{32,0... | collective-permute-start | bytes 196616 | tf_op jit(solution)/shard_map/ppermute | solution.py:233
  95.1 0.0 collective-permute-done.9
  95.1 2.3 %fusion.46 = bf16[256,1024]{1,0:T(8,128)(2,1)S(1)} fusion(bf16[1024,256]{1,0:T(8,128)(2,1)S(1)} %get-tuple-element.36, bf16[1024,4096]{1,0:T(8,128)(2,1)} %param.13, s32[]{:T(128)S(6)} %select_n.18, bf16[512,1024]{1,0:T(8,128)(2,1)S(1)} %collective-permute-done.9), kind=kOutput, calls=%fused_computation.26 | convolution fusion | flops 538181632 | bytes 3670020 | tf_op jit(solution)/shard_map/dot_general | solution.py:272
  97.4 2.0 %collective-permute-start.10 = (bf16[256,1024]{1,0:T(8,128)(2,1)S(1)}, bf16[256,1024]{1,0:T(8,128)(2,1)S(1)}, u32[]{:S(2)}, u32[]{:S(2)}) collective-permute-start(bf16[256,1024]{1,0:T(8,128)(2,1)S(1)} %fusion.46), channel_id=1, source_target_pairs={{0,2},{1,3},{2,0},{3,1},{4,6},{5,7},{6,4},{7,5},{8,10},{9,11},{10,... | collective-permute-start | bytes 1572872 | tf_op jit(solution)/shard_map/ppermute | solution.py:242
  99.5 0.7 slice_bitcast_fusion
  100.1 0.0 collective-permute-done.14
  100.1 0.0 collective-permute-done.15
  100.1 1.2 %collective-permute-done.16 = bf16[128,256]{1,0:T(8,128)(2,1)S(1)} collective-permute-done((bf16[128,256]{1,0:T(8,128)(2,1)S(1)}, bf16[128,256]{1,0:T(8,128)(2,1)S(1)}, u32[]{:S(2)}, u32[]{:S(2)}) %collective-permute-start.16) | collective-permute-done | bytes 65568 | tf_op jit(solution)/shard_map/ppermute | solution.py:233
  101.3 0.6 slice_bitcast_fusion.2
  102.0 9.3 %collective-permute-done.10 = bf16[256,1024]{1,0:T(8,128)(2,1)S(1)} collective-permute-done((bf16[256,1024]{1,0:T(8,128)(2,1)S(1)}, bf16[256,1024]{1,0:T(8,128)(2,1)S(1)}, u32[]{:S(2)}, u32[]{:S(2)}) %collective-permute-start.10) | collective-permute-done | bytes 524320 | tf_op jit(solution)/shard_map/ppermute | solution.py:242
  111.2 3.1 %fusion.61 = bf16[1,1,256,1024]{3,2,1,0:T(8,128)(2,1)} fusion(bf16[1024,256]{1,0:T(8,128)(2,1)S(1)} %get-tuple-element.36, bf16[1024,4096]{1,0:T(8,128)(2,1)} %param.13, s32[]{:T(128)S(6)} %select_n.16, bf16[256,1024]{1,0:T(8,128)(2,1)S(1)} %collective-permute-done.10, bf16[512,1024]{1,0:T(8,128)(2,1)S(1)} %collective-permute-done.9), kind=kOutput, calls=%fused_computation.31 | convolution fusion | flops 538705920 | bytes 4194308 | tf_op jit(solution)/shard_map/dot_general | solution.py:272
  (11 shorter events, 0.1 us)
Async XLA Ops:
  0.6 25.1 %copy-start.6 = (bf16[1,128,128]{2,1,0:T(8,128)(2,1)S(1)}, bf16[1,128,128]{2,1,0:T(8,128)(2,1)}, u32[]{:S(2)}) copy-start(bf16[1,128,128]{2,1,0:T(8,128)(2,1)} %param.11) | copy-start | bytes 98308
  0.6 25.1 %copy-start.5 = (bf16[1,128,128]{2,1,0:T(8,128)(2,1)S(1)}, bf16[1,128,128]{2,1,0:T(8,128)(2,1)}, u32[]{:S(2)}) copy-start(bf16[1,128,128]{2,1,0:T(8,128)(2,1)} %param.12) | copy-start | bytes 98308
  0.7 45.3 %collective-permute-start.1 = (bf16[256,1024]{1,0:T(8,128)(2,1)}, bf16[256,1024]{1,0:T(8,128)(2,1)}, u32[]{:S(2)}, u32[]{:S(2)}) collective-permute-start(bf16[256,1024]{1,0:T(8,128)(2,1)} %bitcast.32), channel_id=1, source_target_pairs={{0,2},{1,3},{2,0},{3,1},{4,6},{5,7},{6,4},{7,5},{8,10},{9,11},{10,... | collective-permute-start | bytes 1572872 | tf_op jit(solution)/shard_map/ppermute | solution.py:242
  2.7 46.1 %collective-permute-start = (bf16[256,1024]{1,0:T(8,128)(2,1)}, bf16[256,1024]{1,0:T(8,128)(2,1)}, u32[]{:S(2)}, u32[]{:S(2)}) collective-permute-start(bf16[256,1024]{1,0:T(8,128)(2,1)} %bitcast.33), channel_id=1, source_target_pairs={{0,1},{1,0},{2,3},{3,2},{4,5},{5,4},{6,7},{7,6},{8,9},{9,8},{10,11... | collective-permute-start | bytes 1572872 | tf_op jit(solution)/shard_map/ppermute | solution.py:239
  3.4 20.7 %collective-permute-start.3 = (bf16[128,256]{1,0:T(8,128)(2,1)S(1)}, bf16[128,256]{1,0:T(8,128)(2,1)S(1)}, u32[]{:S(2)}, u32[]{:S(2)}) collective-permute-start(bf16[128,256]{1,0:T(8,128)(2,1)S(1)} %pad_maximum_fusion.3), channel_id=1, source_target_pairs={{0,16},{4,20},{8,24},{12,28},{16,32},{20,36},{24,40},{28,44},{32,4... | collective-permute-start | bytes 196616 | tf_op jit(solution)/shard_map/ppermute | solution.py:233
  6.8 17.3 %collective-permute-start.4 = (bf16[128,256]{1,0:T(8,128)(2,1)S(1)}, bf16[128,256]{1,0:T(8,128)(2,1)S(1)}, u32[]{:S(2)}, u32[]{:S(2)}) collective-permute-start(bf16[128,256]{1,0:T(8,128)(2,1)S(1)} %pad_maximum_fusion.3), channel_id=1, source_target_pairs={{0,48},{4,52},{8,56},{12,60},{16,0},{20,4},{24,8},{28,12},{32,16},... | collective-permute-start | bytes 196616 | tf_op jit(solution)/shard_map/ppermute | solution.py:233
  9.0 16.7 %collective-permute-start.5 = (bf16[128,256]{1,0:T(8,128)(2,1)S(1)}, bf16[128,256]{1,0:T(8,128)(2,1)S(1)}, u32[]{:S(2)}, u32[]{:S(2)}) collective-permute-start(bf16[128,256]{1,0:T(8,128)(2,1)S(1)} %pad_maximum_fusion.3), channel_id=1, source_target_pairs={{0,32},{4,36},{8,40},{12,44},{16,48},{20,52},{24,56},{28,60},{32,0... | collective-permute-start | bytes 196616 | tf_op jit(solution)/shard_map/ppermute | solution.py:233
  13.9 15.1 %copy-start.7 = (bf16[1,1,256,128]{3,2,1,0:T(8,128)(2,1)S(1)}, bf16[1,1,256,128]{3,2,1,0:T(8,128)(2,1)}, u32[]{:S(2)}) copy-start(bf16[1,1,256,128]{3,2,1,0:T(8,128)(2,1)} %param.10) | copy-start | bytes 196612
  13.9 15.1 %copy-start.8 = (bf16[1,1,256,128]{3,2,1,0:T(8,128)(2,1)S(1)}, bf16[1,1,256,128]{3,2,1,0:T(8,128)(2,1)}, u32[]{:S(2)}) copy-start(bf16[1,1,256,128]{3,2,1,0:T(8,128)(2,1)} %param.9) | copy-start | bytes 196612
  13.9 17.0 %copy-start = (bf16[1,1,256,1024]{3,2,1,0:T(8,128)(2,1)S(1)}, bf16[1,1,256,1024]{3,2,1,0:T(8,128)(2,1)}, u32[]{:S(2)}) copy-start(bf16[1,1,256,1024]{3,2,1,0:T(8,128)(2,1)} %param.8) | copy-start | bytes 1572868
  25.8 12.6 %collective-permute-start.7 = (bf16[512,256]{1,0:T(8,128)(2,1)S(1)}, bf16[512,256]{1,0:T(8,128)(2,1)S(1)}, u32[]{:S(2)}, u32[]{:S(2)}) collective-permute-start(bf16[512,256]{1,0:T(8,128)(2,1)S(1)} %pad_maximum_fusion.1.refs_1_.refs_4_), channel_id=1, source_target_pairs={{0,4},{4,8},{8,12},{12,0},{16,20},{20,24},{24,28},{28,16},{32,36},... | collective-permute-start | bytes 786440 | tf_op jit(solution)/shard_map/ppermute | solution.py:236
  27.3 11.0 %collective-permute-start.8 = (bf16[512,256]{1,0:T(8,128)(2,1)S(1)}, bf16[512,256]{1,0:T(8,128)(2,1)S(1)}, u32[]{:S(2)}, u32[]{:S(2)}) collective-permute-start(bf16[512,256]{1,0:T(8,128)(2,1)S(1)} %pad_maximum_fusion.1.refs_1_.refs_4_), channel_id=1, source_target_pairs={{0,12},{4,0},{8,4},{12,8},{16,28},{20,16},{24,20},{28,24},{32,44},... | collective-permute-start | bytes 786440 | tf_op jit(solution)/shard_map/ppermute | solution.py:236
  29.1 22.3 %collective-permute-start.6 = (bf16[512,256]{1,0:T(8,128)(2,1)S(1)}, bf16[512,256]{1,0:T(8,128)(2,1)S(1)}, u32[]{:S(2)}, u32[]{:S(2)}) collective-permute-start(bf16[512,256]{1,0:T(8,128)(2,1)S(1)} %pad_maximum_fusion.1.refs_1_.refs_4_), channel_id=1, source_target_pairs={{0,8},{4,12},{8,0},{12,4},{16,24},{20,28},{24,16},{28,20},{32,40},... | collective-permute-start | bytes 786440 | tf_op jit(solution)/shard_map/ppermute | solution.py:236
  31.0 15.1 %copy-start.3 = (bf16[1024,4096]{1,0:T(8,128)(2,1)S(1)}, bf16[1024,4096]{1,0:T(8,128)(2,1)}, u32[]{:S(2)}) copy-start(bf16[1024,4096]{1,0:T(8,128)(2,1)} %param.13) | copy-start | bytes 25165828
  37.0 1.3 %copy-start.1 = (bf16[8,512,256]{2,1,0:T(8,128)(2,1)}, bf16[8,512,256]{2,1,0:T(8,128)(2,1)S(1)}, u32[]{:S(2)}) copy-start(bf16[8,512,256]{2,1,0:T(8,128)(2,1)S(1)} %get-tuple-element.39.refs_6_) | copy-start | bytes 6291460
  46.0 4.6 %copy-start.2 = (bf16[8,512,256]{2,1,0:T(8,128)(2,1)}, bf16[8,512,256]{2,1,0:T(8,128)(2,1)S(1)}, u32[]{:S(2)}) copy-start(bf16[8,512,256]{2,1,0:T(8,128)(2,1)S(1)} %get-tuple-element.42.refs_6_) | copy-start | bytes 6291460
  46.0 2.7 %copy-start.4 = (f32[1024,256]{1,0:T(8,128)S(1)}, f32[1024,256]{1,0:T(8,128)}, u32[]{:S(2)}) copy-start(f32[1024,256]{1,0:T(8,128)} %fusion.14) | copy-start | bytes 3145732
  46.0 4.6 %collective-permute-start.2 = (bf16[256,1024]{1,0:T(8,128)(2,1)}, bf16[256,1024]{1,0:T(8,128)(2,1)S(1)}, u32[]{:S(2)}, u32[]{:S(2)}) collective-permute-start(bf16[256,1024]{1,0:T(8,128)(2,1)} %collective-permute-done.1), channel_id=1, source_target_pairs={{0,1},{1,0},{2,3},{3,2},{4,5},{5,4},{6,7},{7,6},{8,9},{9,8},{10,11... | collective-permute-start | bytes 1572872 | tf_op jit(solution)/shard_map/ppermute | solution.py:239
  58.0 37.1 %collective-permute-start.9 = (bf16[512,1024]{1,0:T(8,128)(2,1)S(1)}, bf16[512,1024]{1,0:T(8,128)(2,1)S(1)}, u32[]{:S(2)}, u32[]{:S(2)}) collective-permute-start(bf16[512,1024]{1,0:T(8,128)(2,1)S(1)} %pad_maximum_fusion), channel_id=1, source_target_pairs={{0,1},{1,0},{2,3},{3,2},{4,5},{5,4},{6,7},{7,6},{8,9},{9,8},{10,11... | collective-permute-start | bytes 3145736 | tf_op jit(solution)/shard_map/ppermute | solution.py:239
  70.6 15.6 %collective-permute-start.12 = (bf16[512,256]{1,0:T(8,128)(2,1)S(1)}, bf16[512,256]{1,0:T(8,128)(2,1)S(1)}, u32[]{:S(2)}, u32[]{:S(2)}) collective-permute-start(bf16[512,256]{1,0:T(8,128)(2,1)S(1)} %get-tuple-element.52), channel_id=1, source_target_pairs={{0,12},{4,0},{8,4},{12,8},{16,28},{20,16},{24,20},{28,24},{32,44},... | collective-permute-start | bytes 786440 | tf_op jit(solution)/shard_map/ppermute | solution.py:236
  74.4 15.2 %collective-permute-start.13 = (bf16[512,256]{1,0:T(8,128)(2,1)S(1)}, bf16[512,256]{1,0:T(8,128)(2,1)S(1)}, u32[]{:S(2)}, u32[]{:S(2)}) collective-permute-start(bf16[512,256]{1,0:T(8,128)(2,1)S(1)} %get-tuple-element.53), channel_id=1, source_target_pairs={{0,4},{4,8},{8,12},{12,0},{16,20},{20,24},{24,28},{28,16},{32,36},... | collective-permute-start | bytes 786440 | tf_op jit(solution)/shard_map/ppermute | solution.py:236
  74.4 15.2 %collective-permute-start.11 = (bf16[512,256]{1,0:T(8,128)(2,1)S(1)}, bf16[512,256]{1,0:T(8,128)(2,1)S(1)}, u32[]{:S(2)}, u32[]{:S(2)}) collective-permute-start(bf16[512,256]{1,0:T(8,128)(2,1)S(1)} %get-tuple-element.51), channel_id=1, source_target_pairs={{0,8},{4,12},{8,0},{12,4},{16,24},{20,28},{24,16},{28,20},{32,40},... | collective-permute-start | bytes 786440 | tf_op jit(solution)/shard_map/ppermute | solution.py:236
  89.8 10.4 %collective-permute-start.14 = (bf16[128,256]{1,0:T(8,128)(2,1)S(1)}, bf16[128,256]{1,0:T(8,128)(2,1)S(1)}, u32[]{:S(2)}, u32[]{:S(2)}) collective-permute-start(bf16[128,256]{1,0:T(8,128)(2,1)S(1)} %get-tuple-element.56), channel_id=1, source_target_pairs={{0,48},{4,52},{8,56},{12,60},{16,0},{20,4},{24,8},{28,12},{32,16},... | collective-permute-start | bytes 196616 | tf_op jit(solution)/shard_map/ppermute | solution.py:233
  91.6 8.5 %collective-permute-start.15 = (bf16[128,256]{1,0:T(8,128)(2,1)S(1)}, bf16[128,256]{1,0:T(8,128)(2,1)S(1)}, u32[]{:S(2)}, u32[]{:S(2)}) collective-permute-start(bf16[128,256]{1,0:T(8,128)(2,1)S(1)} %get-tuple-element.58), channel_id=1, source_target_pairs={{0,16},{4,20},{8,24},{12,28},{16,32},{20,36},{24,40},{28,44},{32,4... | collective-permute-start | bytes 196616 | tf_op jit(solution)/shard_map/ppermute | solution.py:233
  92.8 8.5 %collective-permute-start.16 = (bf16[128,256]{1,0:T(8,128)(2,1)S(1)}, bf16[128,256]{1,0:T(8,128)(2,1)S(1)}, u32[]{:S(2)}, u32[]{:S(2)}) collective-permute-start(bf16[128,256]{1,0:T(8,128)(2,1)S(1)} %get-tuple-element.57), channel_id=1, source_target_pairs={{0,32},{4,36},{8,40},{12,44},{16,48},{20,52},{24,56},{28,60},{32,0... | collective-permute-start | bytes 196616 | tf_op jit(solution)/shard_map/ppermute | solution.py:233
  97.4 13.8 %collective-permute-start.10 = (bf16[256,1024]{1,0:T(8,128)(2,1)S(1)}, bf16[256,1024]{1,0:T(8,128)(2,1)S(1)}, u32[]{:S(2)}, u32[]{:S(2)}) collective-permute-start(bf16[256,1024]{1,0:T(8,128)(2,1)S(1)} %fusion.46), channel_id=1, source_target_pairs={{0,2},{1,3},{2,0},{3,1},{4,6},{5,7},{6,4},{7,5},{8,10},{9,11},{10,... | collective-permute-start | bytes 1572872 | tf_op jit(solution)/shard_map/ppermute | solution.py:242

commit v2 on v1

v2 whole, which is shorter than its diff:
```python
import functools

import jax
import jax.numpy as jnp
from jax import lax
from jax.experimental import pallas as pl
from jax.experimental.pallas import tpu as pltpu
from jax.sharding import PartitionSpec as P

HD = 128
HEADS = 8
SLOTS = 256
NEG_FILL = -1e30
LOG2E = 1.4426950408889634
SCALE = HD**-0.5
F32 = jnp.float32
BF16 = jnp.bfloat16


def dot_nn(a, b):
    return lax.dot_general(a, b, (((1,), (0,)), ((), ())), preferred_element_type=F32)


def dot_nt(a, b):
    return lax.dot_general(a, b, (((1,), (1,)), ((), ())), preferred_element_type=F32)


def span(i):
    return slice(i * HD, (i + 1) * HD)


def attend(q, tables, causal, weights, scores, turned):
    for table, t in zip(tables, turned):
        t[...] = table[:, HD:].T
    for i in range(HEADS):
        for table, masked, score in zip(tables, causal, scores):
            s = dot_nt(table[:, :HD], q[:, span(i)]) * (SCALE * LOG2E)
            if masked:
                key = lax.broadcasted_iota(jnp.int32, s.shape, 0)
                token = lax.broadcasted_iota(jnp.int32, s.shape, 1)
                s = jnp.where(key <= token, s, NEG_FILL)
            score[i] = s
    stats = []
    for i in range(HEADS):
        top = functools.reduce(
            jnp.maximum, [jnp.max(score[i], axis=0, keepdims=True) for score in scores]
        )
        total = 0.0
        for score, w in zip(scores, weights):
            p = jnp.exp2(score[i] - top)
            total = total + jnp.sum(p, axis=0, keepdims=True)
            w[i] = p.astype(BF16)
        stats.append((top, total))
    return stats


def mix(i, weights, turned):
    return sum(dot_nn(t[...], w[i]) for t, w in zip(turned, weights))


def fwd_kernel(count, causal, *refs):
    q = refs[0]
    tables = refs[1 : 1 + count]
    weights = refs[1 + count : 1 + 2 * count]
    top_ref, total_ref, acc_ref = refs[1 + 2 * count : 4 + 2 * count]
    scores = refs[4 + 2 * count : 4 + 3 * count]
    turned = refs[4 + 3 * count :]
    stats = attend(q, tables, causal, weights, scores, turned)
    for i in range(HEADS):
        top_ref[i], total_ref[i] = stats[i]
        acc_ref[span(i), :] = mix(i, weights, turned)


def merge_kernel(count, earlier, *refs):
    length, q, dout = refs[:3]
    tables = refs[3 : 3 + count]
    at = 3 + count
    old = [refs[at + 3 * i : at + 3 * i + 3] for i in range(earlier)]
    at += 3 * earlier
    weights = refs[at : at + count]
    at += count
    alphas = refs[at : at + earlier + 1]
    delta_ref, mixed_ref = refs[at + earlier + 1 : at + earlier + 3]
    at += earlier + 3
    scores = refs[at : at + count]
    turned = refs[at + count :]
    stats = attend(q, tables, (False,) * count, weights, scores, turned)
    for i in range(HEADS):
        parts = [(t[i], l[i], a[span(i), :]) for t, l, a in old]
        parts.append((*stats[i], mix(i, weights, turned)))
        top = functools.reduce(jnp.maximum, [t for t, _, _ in parts])
        factors = [jnp.exp2(t - top) for t, _, _ in parts]
        total = sum(f * l for f, (_, l, _) in zip(factors, parts))
        live = lax.broadcasted_iota(jnp.int32, top.shape, 1) < length[0, 0]
        inverse = jnp.where(live, 1.0 / total, 0.0)
        mixed = 0.0
        for f, (_, _, acc), alpha in zip(factors, parts, alphas):
            alpha[i] = f * inverse
            mixed = mixed + (f * inverse) * acc
        delta_ref[i] = jnp.sum(mixed * dout[span(i), :].astype(F32), axis=0, keepdims=True)
        mixed_ref[span(i), :] = mixed.astype(BF16)


def bwd_kernel(count, first, last, *refs):
    q, dout, alpha, delta = refs[:4]
    tables = refs[4 : 4 + count]
    weights = refs[4 + count : 4 + 2 * count]
    at = 4 + 2 * count
    if not first:
        dq_in = refs[at]
        at += 1
    grads = refs[at : at + count]
    dq_ref = refs[at + count]
    turned = refs[at + count + 1 : at + 2 * count + 1]
    sums = refs[at + 2 * count + 1 :]
    for table, t in zip(tables, turned):
        t[...] = table[:, :HD].T
    for s in sums:
        s[...] = jnp.zeros_like(s)
    for i in range(HEADS):
        da = (dout[span(i), :].astype(F32) * alpha[i]).astype(BF16)
        shift = delta[i] * alpha[i]
        dq = 0.0 if first else dq_in[span(i), :]
        for table, w, kt, s in zip(tables, weights, turned, sums):
            p = w[i]
            dp = dot_nn(table[:, HD:], da)
            ds = (p.astype(F32) * (dp - shift)).astype(BF16)
            s[:, HD:] += dot_nt(p, da)
            s[:, :HD] += dot_nn(ds, q[:, span(i)])
            dq = dq + dot_nn(kt[...], ds)
        if last:
            dq_ref[:, span(i)] = (dq * SCALE).T.astype(dq_ref.dtype)
        else:
            dq_ref[span(i), :] = dq
    for s, g in zip(sums, grads):
        g[:, :HD] = (s[:, :HD] * SCALE).astype(g.dtype)
        g[:, HD:] = s[:, HD:].astype(g.dtype)


IN_VMEM = pl.BlockSpec(memory_space=pltpu.VMEM)
STAT = pltpu.VMEM((HEADS, 1, SLOTS), F32)
WIDE = pltpu.VMEM((HEADS * HD, SLOTS), F32)
PARAMS = pltpu.CompilerParams(vmem_limit_bytes=20 * 1024 * 1024)


def call(kernel, name, operands, shapes, scratch, cost, specs=None):
    return pl.pallas_call(
        kernel,
        in_specs=specs or [IN_VMEM] * len(operands),
        out_specs=[IN_VMEM] * len(shapes),
        out_shape=shapes,
        scratch_shapes=scratch,
        cost_estimate=cost,
        compiler_params=PARAMS,
        name=name,
    )(*operands)


def weight_shapes(tables):
    return [pltpu.VMEM((HEADS, t.shape[0], SLOTS), BF16) for t in tables]


def score_shapes(tables):
    return [pltpu.VMEM((HEADS, t.shape[0], SLOTS), F32) for t in tables]


def turned_shapes(tables):
    return [pltpu.VMEM((HD, t.shape[0]), BF16) for t in tables]


def cost(tables, dots):
    rows = sum(t.shape[0] for t in tables)
    area = rows * SLOTS * HEADS
    return pl.CostEstimate(flops=dots * area * HD // 16, bytes_accessed=area // 16, transcendentals=0)


def forward(q, tables, causal):
    n = len(tables)
    out = call(
        functools.partial(fwd_kernel, n, causal),
        "forward",
        [q, *tables],
        weight_shapes(tables) + [STAT, STAT, WIDE],
        score_shapes(tables) + turned_shapes(tables),
        cost(tables, 2),
    )
    return out[:n], out[n:]


def forward_merge(length, q, dout, tables, old):
    n = len(tables)
    e = len(old)
    operands = [length, q, dout, *tables, *[x for part in old for x in part]]
    out = call(
        functools.partial(merge_kernel, n, e),
        "forward_merge",
        operands,
        weight_shapes(tables) + [STAT] * (e + 2) + [pltpu.VMEM((HEADS * HD, SLOTS), BF16)],
        score_shapes(tables) + turned_shapes(tables),
        cost(tables, 2),
        [pl.BlockSpec(memory_space=pltpu.SMEM)] + [IN_VMEM] * (len(operands) - 1),
    )
    return out[:n], out[n : n + e + 1], out[n + e + 1], out[n + e + 2]


def backward(q, dout, alpha, delta, tables, weights, kinds, dq, last):
    n = len(tables)
    out = call(
        functools.partial(bwd_kernel, n, dq is None, last),
        "backward",
        [q, dout, alpha, delta, *tables, *weights, *([] if dq is None else [dq])],
        [jax.ShapeDtypeStruct(t.shape, k) for t, k in zip(tables, kinds)]
        + [jax.ShapeDtypeStruct((SLOTS, HEADS * HD), BF16) if last else WIDE],
        turned_shapes(tables) + [pltpu.VMEM(t.shape, F32) for t in tables],
        cost(tables, 4),
    )
    return out[:n], out[n]


def group_shift(dz, dx):
    return [(z * 4 + x, (z + dz) % 4 * 4 + (x + dx) % 4) for z in range(4) for x in range(4)]


def tensor_flip(bits):
    return [(t, t ^ bits) for t in range(4)]


def per_device(
    queries, comp_keys, comp_values, prompt_keys, prompt_values, out_weight, cotangent, lengths
):
    q = queries[0, 0]
    cot = cotangent[0, 0]

    def over_z(a, s):
        return lax.ppermute(a, "group", group_shift(s, 0))

    def over_x(a, s):
        return lax.ppermute(a, "group", group_shift(0, s))

    def to_core(a):
        return lax.ppermute(a, "tensor", tensor_flip(1))

    def to_chip(a):
        return lax.ppermute(a, "tensor", tensor_flip(2))

    own = jnp.concatenate([prompt_keys[0], prompt_values[0]], axis=1)
    comp = jnp.concatenate([comp_keys[0, 0], comp_values[0, 0]], axis=1)
    gathered = [over_z(own, s) for s in (1, 3, 2)]
    chunk0 = jnp.concatenate([own, *gathered], axis=0)
    chunk0, cot = lax.optimization_barrier((chunk0, cot))
    chunk1, chunk3, chunk2 = [over_x(chunk0, s) for s in (1, 3, 2)]

    me = lax.axis_index("tensor")

    def columns(bits):
        return lax.dynamic_slice_in_dim(out_weight, (me ^ bits) * 1024, 1024, 1)

    cot_chip = to_chip(cot)
    cot_core = to_core(cot)
    cot_diag = to_core(cot_chip)
    dout = sum(
        dot_nt(columns(bits), part)
        for bits, part in ((0, cot), (1, cot_core), (2, cot_chip), (3, cot_diag))
    ).astype(BF16)

    w0, part0 = forward(q, [chunk0, comp], (False, True))
    w13, part13 = forward(q, [chunk1, chunk3], (False, False))
    w2, (alpha0, alpha13, alpha2), delta, mixed = forward_merge(
        lengths, q, dout, [chunk2], [part0, part13]
    )

    (g2,), dq = backward(q, dout, alpha2, delta, [chunk2], w2, (BF16,), None, False)
    def partial_out(bits):
        block = lax.dot_general(
            mixed, columns(bits), (((0,), (0,)), ((), ())), preferred_element_type=F32
        )
        return block.astype(BF16)

    other = to_core(jnp.concatenate([partial_out(1), partial_out(3)], axis=0))
    pair_mine = partial_out(0).astype(F32) + other[:SLOTS].astype(F32)
    pair_far = partial_out(2).astype(F32) + other[SLOTS:].astype(F32)
    pair_far, alpha13 = lax.optimization_barrier((pair_far.astype(BF16), alpha13))
    far = to_chip(pair_far)
    (g1,), dq = backward(q, dout, alpha13, delta, [chunk1], w13[:1], (BF16,), dq, False)
    (g3,), dq = backward(q, dout, alpha13, delta, [chunk3], w13[1:], (BF16,), dq, False)

    (g0, gcomp), dq = backward(q, dout, alpha0, delta, [chunk0, comp], w0, (F32, BF16), dq, True)

    back2, back1, back3 = over_x(g2, -2), over_x(g1, -1), over_x(g3, -3)
    rows = g0 + back2.astype(F32) + back1.astype(F32) + back3.astype(F32)
    n = own.shape[0]
    sent, far = lax.optimization_barrier((rows.astype(BF16), far))
    total = rows[:n]
    for i, s in enumerate((1, 3, 2)):
        total = total + over_z(sent[(i + 1) * n : (i + 2) * n], -s).astype(F32)
    total = total.astype(BF16)
    output = (pair_mine + far.astype(F32)).astype(BF16)
    return (
        output[None, None],
        dq[None, None],
        gcomp[None, None, :, :HD],
        gcomp[None, None, :, HD:],
        total[None, :, :HD],
        total[None, :, HD:],
    )


def solution(mesh):
    wide = P("dp", "group", None, "tensor")
    rows = P("dp", "group", "tensor")
    return jax.shard_map(
        per_device,
        mesh=mesh,
        in_specs=(wide, wide, wide, rows, rows, P("tensor", None), wide, P("dp", "group")),
        out_specs=(wide, wide, wide, wide, rows, rows),
        check_vma=False,
    )
```

time: 115 us -> 88.3 us (0.77)
  Pallas kernels: 39.5 us -> 20.3 us
  matrix products: 15.6 us -> 10.2 us
  waiting for transfers between devices: 23.3 us -> 18.8 us
  other arithmetic: 1.04 us -> 2.71 us
    pallas_call x6 -> x7, Pallas kernels: 39.5 us -> 20.3 us  [call(): pl.pallas_call(kernel, in_specs=specs or [IN_VMEM] * len(operands), out_s...]
    ppermute x2, waiting for transfers between devices: 9.26 us -> 5.48 us  [to_chip(): return lax.ppermute(a, 'tensor', tensor_flip(2))]
    dot_general x4, matrix products: 6.94 us -> 3.78 us  [partial_out(): lax.dot_general(mixed, columns(bits), (((0,), (0,)), ((), ())), preferred...]
    dot_general x4, matrix products: 8.64 us -> 6.45 us  [dot_nt(): lax.dot_general(a, b, (((1,), (1,)), ((), ())), preferred_element_type=F32)]
    ppermute x6, starting transfers between devices: 15.8 us -> 17.9 us  [over_z(): return lax.ppermute(a, 'group', group_shift(s, 0))]
    ppermute x2, starting transfers between devices: 4.05 us -> 2.35 us  [to_chip(): return lax.ppermute(a, 'tensor', tensor_flip(2))]
    ppermute x6, waiting for transfers between devices: 8.84 us -> 7.3 us  [over_z(): return lax.ppermute(a, 'group', group_shift(s, 0))]
  transfers between devices with their start and end apart: 17 -> 17, of which waited for: 6 -> 7; matrix products, arithmetic and copies ran while one was open for 12% -> 12% of each run, Pallas kernels for 30% -> 21%
where the time goes in v2:
time: 88.3 us; the launch traced here: 87 us
  starting transfers between devices  31.2 us (35%)
  Pallas kernels  20.3 us (23%)
  waiting for transfers between devices  18.8 us (21%)
  matrix products  10.2 us (12%)
  other arithmetic  2.71 us (3%)
  local copies, waits for them, and re-layouts  2.35 us (3%)
  between operations  1.5 us (2%)
    pallas_call x7, Pallas kernels, call(): pl.pallas_call(kernel, in_specs=specs or [IN_VMEM] * len(operands), out_s...  20.3 us
    ppermute x6, starting transfers between devices, over_z(): return lax.ppermute(a, 'group', group_shift(s, 0))  17.9 us
    ppermute x6, starting transfers between devices, over_x(): return lax.ppermute(a, 'group', group_shift(0, s))  10 us
    ppermute x6, waiting for transfers between devices, over_z(): return lax.ppermute(a, 'group', group_shift(s, 0))  7.3 us
    dot_general x4, matrix products, dot_nt(): lax.dot_general(a, b, (((1,), (1,)), ((), ())), preferred_element_type=F32)  6.45 us
    ppermute x6, waiting for transfers between devices, over_x(): return lax.ppermute(a, 'group', group_shift(0, s))  5.97 us
    ppermute x2, waiting for transfers between devices, to_chip(): return lax.ppermute(a, 'tensor', tensor_flip(2))  5.48 us
    dot_general x4, matrix products, partial_out(): lax.dot_general(mixed, columns(bits), (((0,), (0,)), ((), ())), preferred...  3.78 us
  transfers between devices with their start and end apart: 17, of which 7 were waited for; matrix products, arithmetic and copies ran while one was open for 12% of the time, Pallas kernels for 21%

profile of v2, /device:TPU:8, one launch (start us, length us, event | category | flops | bytes accessed | tf_op | source)
XLA Modules:
  0.0 87.0 jit_solution(16108034560793082993)
XLA Ops:
  0.6 0.8 pad_maximum_fusion.3
  1.4 3.3 %collective-permute-start = (bf16[128,256]{1,0:T(8,128)(2,1)S(1)}, bf16[128,256]{1,0:T(8,128)(2,1)S(1)}, u32[]{:S(2)}, u32[]{:S(2)}) collective-permute-start(bf16[128,256]{1,0:T(8,128)(2,1)S(1)} %pad_maximum_fusion.3), channel_id=1, source_target_pairs={{0,16},{4,20},{8,24},{12,28},{16,32},{20,36},{24,40},{28,44},{32,4... | collective-permute-start | bytes 196616 | tf_op jit(solution)/shard_map/ppermute | solution.py:235
  4.8 3.1 %collective-permute-start.1 = (bf16[128,256]{1,0:T(8,128)(2,1)S(1)}, bf16[128,256]{1,0:T(8,128)(2,1)S(1)}, u32[]{:S(2)}, u32[]{:S(2)}) collective-permute-start(bf16[128,256]{1,0:T(8,128)(2,1)S(1)} %pad_maximum_fusion.3), channel_id=1, source_target_pairs={{0,48},{4,52},{8,56},{12,60},{16,0},{20,4},{24,8},{28,12},{32,16},... | collective-permute-start | bytes 196616 | tf_op jit(solution)/shard_map/ppermute | solution.py:235
  7.9 4.9 %collective-permute-start.2 = (bf16[128,256]{1,0:T(8,128)(2,1)S(1)}, bf16[128,256]{1,0:T(8,128)(2,1)S(1)}, u32[]{:S(2)}, u32[]{:S(2)}) collective-permute-start(bf16[128,256]{1,0:T(8,128)(2,1)S(1)} %pad_maximum_fusion.3), channel_id=1, source_target_pairs={{0,32},{4,36},{8,40},{12,44},{16,48},{20,52},{24,56},{28,60},{32,0... | collective-permute-start | bytes 196616 | tf_op jit(solution)/shard_map/ppermute | solution.py:235
  12.8 0.0 collective-permute-done
  12.8 0.0 collective-permute-done.1
  12.8 4.0 %collective-permute-done.2 = bf16[128,256]{1,0:T(8,128)(2,1)S(1)} collective-permute-done((bf16[128,256]{1,0:T(8,128)(2,1)S(1)}, bf16[128,256]{1,0:T(8,128)(2,1)S(1)}, u32[]{:S(2)}, u32[]{:S(2)}) %collective-permute-start.2) | collective-permute-done | bytes 65568 | tf_op jit(solution)/shard_map/ppermute | solution.py:235
  16.8 0.8 pad_maximum_fusion.1.refs_1_.refs_4_
  17.6 2.3 %collective-permute-start.4 = (bf16[256,1024]{1,0:T(8,128)(2,1)}, bf16[256,1024]{1,0:T(8,128)(2,1)S(1)}, u32[]{:S(2)}, u32[]{:S(2)}) collective-permute-start(bf16[256,1024]{1,0:T(8,128)(2,1)} %bitcast.32), channel_id=1, source_target_pairs={{0,2},{1,3},{2,0},{3,1},{4,6},{5,7},{6,4},{7,5},{8,10},{9,11},{10,... | collective-permute-start | bytes 1572872 | tf_op jit(solution)/shard_map/ppermute | solution.py:244
  20.6 0.9 %pad_maximum_fusion.2.refs_2_.refs_5_ = bf16[256,256]{1,0:T(8,128)(2,1)S(1)} fusion(bf16[256,128]{1,0:T(8,128)(2,1)} %bitcast.39, bf16[256,128]{1,0:T(8,128)(2,1)} %bitcast.40), kind=kLoop, calls=%fused_computation.39 | loop fusion | flops 262144 | bytes 262144 | tf_op jit(solution)/shard_map/concatenate | solution.py:247
  21.5 0.1 collective-permute-start.3
  21.6 1.6 %collective-permute-start.7 = (bf16[512,256]{1,0:T(8,128)(2,1)S(1)}, bf16[512,256]{1,0:T(8,128)(2,1)S(1)}, u32[]{:S(2)}, u32[]{:S(2)}) collective-permute-start(bf16[512,256]{1,0:T(8,128)(2,1)S(1)} %pad_maximum_fusion.1.refs_1_.refs_4_), channel_id=1, source_target_pairs={{0,4},{4,8},{8,12},{12,0},{16,20},{20,24},{24,28},{28,16},{32,36},... | collective-permute-start | bytes 786440 | tf_op jit(solution)/shard_map/ppermute | solution.py:238
  23.1 1.7 %collective-permute-start.8 = (bf16[512,256]{1,0:T(8,128)(2,1)S(1)}, bf16[512,256]{1,0:T(8,128)(2,1)S(1)}, u32[]{:S(2)}, u32[]{:S(2)}) collective-permute-start(bf16[512,256]{1,0:T(8,128)(2,1)S(1)} %pad_maximum_fusion.1.refs_1_.refs_4_), channel_id=1, source_target_pairs={{0,12},{4,0},{8,4},{12,8},{16,28},{20,16},{24,20},{28,24},{32,44},... | collective-permute-start | bytes 786440 | tf_op jit(solution)/shard_map/ppermute | solution.py:238
  24.9 1.8 %collective-permute-start.6 = (bf16[512,256]{1,0:T(8,128)(2,1)S(1)}, bf16[512,256]{1,0:T(8,128)(2,1)S(1)}, u32[]{:S(2)}, u32[]{:S(2)}) collective-permute-start(bf16[512,256]{1,0:T(8,128)(2,1)S(1)} %pad_maximum_fusion.1.refs_1_.refs_4_), channel_id=1, source_target_pairs={{0,8},{4,12},{8,0},{12,4},{16,24},{20,28},{24,16},{28,20},{32,40},... | collective-permute-start | bytes 786440 | tf_op jit(solution)/shard_map/ppermute | solution.py:238
  26.7 0.0 copy-start
  26.7 1.0 %copy-done = bf16[1,1,256,1024]{3,2,1,0:T(8,128)(2,1)S(1)} copy-done((bf16[1,1,256,1024]{3,2,1,0:T(8,128)(2,1)S(1)}, bf16[1,1,256,1024]{3,2,1,0:T(8,128)(2,1)}, u32[]{:S(2)}) %copy-start) | copy-done | bytes 524312
  27.7 2.3 %forward.2 = (bf16[8,512,256]{2,1,0:T(8,128)(2,1)S(1)}, bf16[8,256,256]{2,1,0:T(8,128)(2,1)S(1)}, f32[8,1,256]{2,1,0:T(1,128)S(1)}, f32[8,1,256]{2,1,0:T(1,128)S(1)}, f32[1024,256]{1,0:T(8,128)S(1)}) custom-call(bf16[256,1024]{1,0:T(8,128)(2,1)S(1)} %bitcast.25, bf16[512,256]{1,0:T(8,128)(2,1)S(1)} %pad_maximum_fusion.1.refs_1_.refs_4_, ...), custom_call_target="tpu_custom_call" | custom-call | flops 25165824 | bytes 98304 | tf_op jit(solution)/shard_map/forward/pallas_call | solution.py:147
  30.0 0.0 copy-start.1
  30.1 2.6 %fusion.14 = f32[1024,256]{1,0:T(8,128)S(1)} fusion(bf16[256,1024]{1,0:T(8,128)(2,1)} %bitcast.34, bf16[1024,4096]{1,0:T(8,128)(2,1)} %param.13, s32[]{:T(128)S(6)} %select_n.16), kind=kOutput, calls=%fused_computation.14 | convolution fusion | flops 536870912 | bytes 3670020 | tf_op jit(solution)/shard_map/dot_general | solution.py:25
  32.6 0.0 collective-permute-done.7.refs_1_.refs_4_
  32.6 3.8 %collective-permute-done.8.refs_2_.refs_4_ = bf16[512,256]{1,0:T(8,128)(2,1)S(1)} collective-permute-done((bf16[512,256]{1,0:T(8,128)(2,1)S(1)}, bf16[512,256]{1,0:T(8,128)(2,1)S(1)}, u32[]{:S(2)}, u32[]{:S(2)}) %collective-permute-start.8) | collective-permute-done | bytes 262176 | tf_op jit(solution)/shard_map/ppermute | solution.py:238
  36.4 3.2 %forward.3 = (bf16[8,512,256]{2,1,0:T(8,128)(2,1)S(1)}, bf16[8,512,256]{2,1,0:T(8,128)(2,1)S(1)}, f32[8,1,256]{2,1,0:T(1,128)S(1)}, f32[8,1,256]{2,1,0:T(1,128)S(1)}, f32[1024,256]{1,0:T(8,128)S(1)}) custom-call(bf16[256,1024]{1,0:T(8,128)(2,1)S(1)} %bitcast.26, bf16[512,256]{1,0:T(8,128)(2,1)S(1)} %collective-permute-done.7.refs_1_.refs_4_, ...), custom_call_target="tpu_custom_call" | custom-call | flops 33554432 | bytes 131072 | tf_op jit(solution)/shard_map/forward/pallas_call | solution.py:147
  39.6 0.0 collective-permute-done.4
  39.6 0.3 collective-permute-start.5
  39.9 2.3 %fusion.6 = f32[1024,256]{1,0:T(8,128)S(1)} fusion(bf16[256,1024]{1,0:T(8,128)(2,1)S(1)} %collective-permute-done.4, bf16[1024,4096]{1,0:T(8,128)(2,1)} %param.13, s32[]{:T(128)S(6)} %select_n.18), kind=kOutput, calls=%fused_computation.6 | convolution fusion | flops 536870912 | bytes 3670020 | tf_op jit(solution)/shard_map/dot_general | solution.py:25
  42.3 0.0 collective-permute-done.3
  42.3 0.0 copy-done.1
  42.3 0.7 fusion.19
  43.0 0.0 collective-permute-done.5
  43.1 0.8 fusion.25.refs_2_.refs_1_
  43.8 0.0 collective-permute-done.6.refs_3_.refs_4_
  43.9 2.1 %forward_merge.1 = (bf16[8,512,256]{2,1,0:T(8,128)(2,1)S(1)}, f32[8,1,256]{2,1,0:T(1,128)S(1)}, f32[8,1,256]{2,1,0:T(1,128)S(1)}, f32[8,1,256]{2,1,0:T(1,128)S(1...) custom-call(s32[1,1]{1,0:T(1,128)S(6)} %copy.14.refs_0_, bf16[256,1024]{1,0:T(8,128)(2,1)S(1)} %bitcast.27, ...), custom_call_target="tpu_custom_call" | custom-call | flops 16777216 | bytes 65536 | tf_op jit(solution)/shard_map/forward_merge/pallas_call | solution.py:147
  46.0 0.7 fusion.31
  46.7 0.7 fusion.37
  47.4 0.1 pad_maximum_fusion
  47.5 0.6 collective-permute-start.9
  48.1 2.6 %backward.4 = (bf16[512,256]{1,0:T(8,128)(2,1)S(1)}, f32[1024,256]{1,0:T(8,128)S(1)}) custom-call(bf16[256,1024]{1,0:T(8,128)(2,1)S(1)} %bitcast.28, bf16[1024,256]{1,0:T(8,128)(2,1)S(1)} %fusion.25.refs_2_.refs_1_, f32[8,1,256]{2,1,0:T(1,128)S(1)} %get-tuple-element.54.refs_2_, f32[8,1,256]{2,1,0:T(1,128)S(1)} %get-tuple-element.47.refs_3_, ...), custom_call_target="tpu_custom_call" | custom-call | flops 33554432 | bytes 65536 | tf_op jit(solution)/shard_map/backward/pallas_call | solution.py:147
  50.7 0.3 collective-permute-start.10
  51.0 0.0 collective-permute-done.9
  51.1 0.7 fusion.46
  51.8 2.6 %backward.5 = (bf16[512,256]{1,0:T(8,128)(2,1)S(1)}, f32[1024,256]{1,0:T(8,128)S(1)}) custom-call(bf16[256,1024]{1,0:T(8,128)(2,1)S(1)} %bitcast.29, bf16[1024,256]{1,0:T(8,128)(2,1)S(1)} %fusion.25.refs_2_.refs_1_, f32[8,1,256]{2,1,0:T(1,128)S(1)} %get-tuple-element.51.refs_2_, f32[8,1,256]{2,1,0:T(1,128)S(1)} %get-tuple-element.47.refs_3_, ...), custom_call_target="tpu_custom_call" | custom-call | flops 33554432 | bytes 65536 | tf_op jit(solution)/shard_map/backward/pallas_call | solution.py:147
  54.4 2.6 %backward.6 = (bf16[512,256]{1,0:T(8,128)(2,1)S(1)}, f32[1024,256]{1,0:T(8,128)S(1)}) custom-call(bf16[256,1024]{1,0:T(8,128)(2,1)S(1)} %bitcast.30, bf16[1024,256]{1,0:T(8,128)(2,1)S(1)} %fusion.25.refs_2_.refs_1_, f32[8,1,256]{2,1,0:T(1,128)S(1)} %get-tuple-element.51.refs_2_, f32[8,1,256]{2,1,0:T(1,128)S(1)} %get-tuple-element.47.refs_3_, ...), custom_call_target="tpu_custom_call" | custom-call | flops 33554432 | bytes 65536 | tf_op jit(solution)/shard_map/backward/pallas_call | solution.py:147
  57.1 4.6 %collective-permute-start.12 = (bf16[512,256]{1,0:T(8,128)(2,1)S(1)}, bf16[512,256]{1,0:T(8,128)(2,1)S(1)}, u32[]{:S(2)}, u32[]{:S(2)}) collective-permute-start(bf16[512,256]{1,0:T(8,128)(2,1)S(1)} %get-tuple-element.62), channel_id=1, source_target_pairs={{0,4},{4,8},{8,12},{12,0},{16,20},{20,24},{24,28},{28,16},{32,36},... | collective-permute-start | bytes 786440 | tf_op jit(solution)/shard_map/ppermute | solution.py:238
  61.6 0.0 collective-permute-start.11
  61.6 0.0 collective-permute-start.13
  61.7 4.8 %backward.7 = (f32[512,256]{1,0:T(8,128)S(1)}, bf16[256,256]{1,0:T(8,128)(2,1)S(1)}, bf16[256,1024]{1,0:T(8,128)(2,1)}) custom-call(bf16[256,1024]{1,0:T(8,128)(2,1)S(1)} %bitcast.31, bf16[1024,256]{1,0:T(8,128)(2,1)S(1)} %fusion.25.refs_2_.refs_1_, f32[8,1,256]{2,1,0:T(1,128)S(1)} %get-tuple-element.46.refs_2_, f32[8,1,256]{2,1,0:T(1,128)S(1)} %get-tuple-element.47.refs_3_, ...), custom_call_target="tpu_custom_call" | custom-call | flops 50331648 | bytes 98304 | tf_op jit(solution)/shard_map/backward/pallas_call | solution.py:147
  66.4 0.7 slice_bitcast_fusion
  67.1 0.0 collective-permute-done.10
  67.1 0.2 collective-permute-done.12
  67.3 2.0 %collective-permute-done.11 = bf16[512,256]{1,0:T(8,128)(2,1)S(1)} collective-permute-done((bf16[512,256]{1,0:T(8,128)(2,1)S(1)}, bf16[512,256]{1,0:T(8,128)(2,1)S(1)}, u32[]{:S(2)}, u32[]{:S(2)}) %collective-permute-start.11) | collective-permute-done | bytes 262176 | tf_op jit(solution)/shard_map/ppermute | solution.py:238
  69.3 0.1 fusion.75
  69.5 5.5 %collective-permute-done.13 = bf16[256,1024]{1,0:T(8,128)(2,1)S(1)} collective-permute-done((bf16[256,1024]{1,0:T(8,128)(2,1)S(1)}, bf16[256,1024]{1,0:T(8,128)(2,1)S(1)}, u32[]{:S(2)}, u32[]{:S(2)}) %collective-permute-start.13) | collective-permute-done | bytes 524320 | tf_op jit(solution)/shard_map/ppermute | solution.py:244
  75.0 1.4 %collective-permute-start.14 = (bf16[128,256]{1,0:T(8,128)(2,1)S(1)}, bf16[128,256]{1,0:T(8,128)(2,1)S(1)}, u32[]{:S(2)}, u32[]{:S(2)}) collective-permute-start(bf16[128,256]{1,0:T(8,128)(2,1)S(1)} %get-tuple-element.70), channel_id=1, source_target_pairs={{0,48},{4,52},{8,56},{12,60},{16,0},{20,4},{24,8},{28,12},{32,16},... | collective-permute-start | bytes 196616 | tf_op jit(solution)/shard_map/ppermute | solution.py:235
  76.3 1.6 %collective-permute-start.15 = (bf16[128,256]{1,0:T(8,128)(2,1)S(1)}, bf16[128,256]{1,0:T(8,128)(2,1)S(1)}, u32[]{:S(2)}, u32[]{:S(2)}) collective-permute-start(bf16[128,256]{1,0:T(8,128)(2,1)S(1)} %get-tuple-element.72), channel_id=1, source_target_pairs={{0,16},{4,20},{8,24},{12,28},{16,32},{20,36},{24,40},{28,44},{32,4... | collective-permute-start | bytes 196616 | tf_op jit(solution)/shard_map/ppermute | solution.py:235
  78.0 3.5 %collective-permute-start.16 = (bf16[128,256]{1,0:T(8,128)(2,1)S(1)}, bf16[128,256]{1,0:T(8,128)(2,1)S(1)}, u32[]{:S(2)}, u32[]{:S(2)}) collective-permute-start(bf16[128,256]{1,0:T(8,128)(2,1)S(1)} %get-tuple-element.71), channel_id=1, source_target_pairs={{0,32},{4,36},{8,40},{12,44},{16,48},{20,52},{24,56},{28,60},{32,0... | collective-permute-start | bytes 196616 | tf_op jit(solution)/shard_map/ppermute | solution.py:235
  81.5 1.6 %fusion.61 = bf16[1,1,256,1024]{3,2,1,0:T(8,128)(2,1)} fusion(bf16[1024,256]{1,0:T(8,128)(2,1)S(1)} %get-tuple-element.45, bf16[1024,4096]{1,0:T(8,128)(2,1)S(1)} %copy-done.1, s32[]{:T(128)S(6)} %select_n.16, bf16[256,1024]{1,0:T(8,128)(2,1)S(1)} %collective-permute-done.13, bf16[512,1024]{1,0:T(8,128)(2,1)S(1)} %collective-permute-done.9), kind=kOutput, calls=%fused_computation.31 | convolution fusion | flops 538705920 | bytes 4194308 | tf_op jit(solution)/shard_map/dot_general | solution.py:274
  83.0 0.0 collective-permute-done.14
  83.0 1.6 %collective-permute-done.15 = bf16[128,256]{1,0:T(8,128)(2,1)S(1)} collective-permute-done((bf16[128,256]{1,0:T(8,128)(2,1)S(1)}, bf16[128,256]{1,0:T(8,128)(2,1)S(1)}, u32[]{:S(2)}, u32[]{:S(2)}) %collective-permute-start.15) | collective-permute-done | bytes 65568 | tf_op jit(solution)/shard_map/ppermute | solution.py:235
  84.6 1.7 %collective-permute-done.16 = bf16[128,256]{1,0:T(8,128)(2,1)S(1)} collective-permute-done((bf16[128,256]{1,0:T(8,128)(2,1)S(1)}, bf16[128,256]{1,0:T(8,128)(2,1)S(1)}, u32[]{:S(2)}, u32[]{:S(2)}) %collective-permute-start.16) | collective-permute-done | bytes 65568 | tf_op jit(solution)/shard_map/ppermute | solution.py:235
  86.4 0.6 slice_bitcast_fusion.2
  (2 shorter events, 0.0 us)
Async XLA Ops:
  1.4 11.4 %collective-permute-start = (bf16[128,256]{1,0:T(8,128)(2,1)S(1)}, bf16[128,256]{1,0:T(8,128)(2,1)S(1)}, u32[]{:S(2)}, u32[]{:S(2)}) collective-permute-start(bf16[128,256]{1,0:T(8,128)(2,1)S(1)} %pad_maximum_fusion.3), channel_id=1, source_target_pairs={{0,16},{4,20},{8,24},{12,28},{16,32},{20,36},{24,40},{28,44},{32,4... | collective-permute-start | bytes 196616 | tf_op jit(solution)/shard_map/ppermute | solution.py:235
  4.8 8.1 %collective-permute-start.1 = (bf16[128,256]{1,0:T(8,128)(2,1)S(1)}, bf16[128,256]{1,0:T(8,128)(2,1)S(1)}, u32[]{:S(2)}, u32[]{:S(2)}) collective-permute-start(bf16[128,256]{1,0:T(8,128)(2,1)S(1)} %pad_maximum_fusion.3), channel_id=1, source_target_pairs={{0,48},{4,52},{8,56},{12,60},{16,0},{20,4},{24,8},{28,12},{32,16},... | collective-permute-start | bytes 196616 | tf_op jit(solution)/shard_map/ppermute | solution.py:235
  7.9 8.9 %collective-permute-start.2 = (bf16[128,256]{1,0:T(8,128)(2,1)S(1)}, bf16[128,256]{1,0:T(8,128)(2,1)S(1)}, u32[]{:S(2)}, u32[]{:S(2)}) collective-permute-start(bf16[128,256]{1,0:T(8,128)(2,1)S(1)} %pad_maximum_fusion.3), channel_id=1, source_target_pairs={{0,32},{4,36},{8,40},{12,44},{16,48},{20,52},{24,56},{28,60},{32,0... | collective-permute-start | bytes 196616 | tf_op jit(solution)/shard_map/ppermute | solution.py:235
  17.6 22.0 %collective-permute-start.4 = (bf16[256,1024]{1,0:T(8,128)(2,1)}, bf16[256,1024]{1,0:T(8,128)(2,1)S(1)}, u32[]{:S(2)}, u32[]{:S(2)}) collective-permute-start(bf16[256,1024]{1,0:T(8,128)(2,1)} %bitcast.32), channel_id=1, source_target_pairs={{0,2},{1,3},{2,0},{3,1},{4,6},{5,7},{6,4},{7,5},{8,10},{9,11},{10,... | collective-permute-start | bytes 1572872 | tf_op jit(solution)/shard_map/ppermute | solution.py:244
  21.5 20.8 %collective-permute-start.3 = (bf16[256,1024]{1,0:T(8,128)(2,1)}, bf16[256,1024]{1,0:T(8,128)(2,1)S(1)}, u32[]{:S(2)}, u32[]{:S(2)}) collective-permute-start(bf16[256,1024]{1,0:T(8,128)(2,1)} %bitcast.33), channel_id=1, source_target_pairs={{0,1},{1,0},{2,3},{3,2},{4,5},{5,4},{6,7},{7,6},{8,9},{9,8},{10,11... | collective-permute-start | bytes 1572872 | tf_op jit(solution)/shard_map/ppermute | solution.py:241
  21.6 11.1 %collective-permute-start.7 = (bf16[512,256]{1,0:T(8,128)(2,1)S(1)}, bf16[512,256]{1,0:T(8,128)(2,1)S(1)}, u32[]{:S(2)}, u32[]{:S(2)}) collective-permute-start(bf16[512,256]{1,0:T(8,128)(2,1)S(1)} %pad_maximum_fusion.1.refs_1_.refs_4_), channel_id=1, source_target_pairs={{0,4},{4,8},{8,12},{12,0},{16,20},{20,24},{24,28},{28,16},{32,36},... | collective-permute-start | bytes 786440 | tf_op jit(solution)/shard_map/ppermute | solution.py:238
  23.1 13.3 %collective-permute-start.8 = (bf16[512,256]{1,0:T(8,128)(2,1)S(1)}, bf16[512,256]{1,0:T(8,128)(2,1)S(1)}, u32[]{:S(2)}, u32[]{:S(2)}) collective-permute-start(bf16[512,256]{1,0:T(8,128)(2,1)S(1)} %pad_maximum_fusion.1.refs_1_.refs_4_), channel_id=1, source_target_pairs={{0,12},{4,0},{8,4},{12,8},{16,28},{20,16},{24,20},{28,24},{32,44},... | collective-permute-start | bytes 786440 | tf_op jit(solution)/shard_map/ppermute | solution.py:238
  24.9 19.0 %collective-permute-start.6 = (bf16[512,256]{1,0:T(8,128)(2,1)S(1)}, bf16[512,256]{1,0:T(8,128)(2,1)S(1)}, u32[]{:S(2)}, u32[]{:S(2)}) collective-permute-start(bf16[512,256]{1,0:T(8,128)(2,1)S(1)} %pad_maximum_fusion.1.refs_1_.refs_4_), channel_id=1, source_target_pairs={{0,8},{4,12},{8,0},{12,4},{16,24},{20,28},{24,16},{28,20},{32,40},... | collective-permute-start | bytes 786440 | tf_op jit(solution)/shard_map/ppermute | solution.py:238
  26.7 1.0 %copy-start = (bf16[1,1,256,1024]{3,2,1,0:T(8,128)(2,1)S(1)}, bf16[1,1,256,1024]{3,2,1,0:T(8,128)(2,1)}, u32[]{:S(2)}) copy-start(bf16[1,1,256,1024]{3,2,1,0:T(8,128)(2,1)} %param.8) | copy-start | bytes 1572868
  30.0 12.2 %copy-start.1 = (bf16[1024,4096]{1,0:T(8,128)(2,1)S(1)}, bf16[1024,4096]{1,0:T(8,128)(2,1)}, u32[]{:S(2)}) copy-start(bf16[1024,4096]{1,0:T(8,128)(2,1)} %param.13) | copy-start | bytes 25165828
  39.6 3.4 %collective-permute-start.5 = (bf16[256,1024]{1,0:T(8,128)(2,1)S(1)}, bf16[256,1024]{1,0:T(8,128)(2,1)S(1)}, u32[]{:S(2)}, u32[]{:S(2)}) collective-permute-start(bf16[256,1024]{1,0:T(8,128)(2,1)S(1)} %collective-permute-done.4), channel_id=1, source_target_pairs={{0,1},{1,0},{2,3},{3,2},{4,5},{5,4},{6,7},{7,6},{8,9},{9,8},{10,11... | collective-permute-start | bytes 1572872 | tf_op jit(solution)/shard_map/ppermute | solution.py:241
  47.5 3.5 %collective-permute-start.9 = (bf16[512,1024]{1,0:T(8,128)(2,1)S(1)}, bf16[512,1024]{1,0:T(8,128)(2,1)S(1)}, u32[]{:S(2)}, u32[]{:S(2)}) collective-permute-start(bf16[512,1024]{1,0:T(8,128)(2,1)S(1)} %pad_maximum_fusion), channel_id=1, source_target_pairs={{0,1},{1,0},{2,3},{3,2},{4,5},{5,4},{6,7},{7,6},{8,9},{9,8},{10,11... | collective-permute-start | bytes 3145736 | tf_op jit(solution)/shard_map/ppermute | solution.py:241
  50.7 16.4 %collective-permute-start.10 = (bf16[512,256]{1,0:T(8,128)(2,1)S(1)}, bf16[512,256]{1,0:T(8,128)(2,1)S(1)}, u32[]{:S(2)}, u32[]{:S(2)}) collective-permute-start(bf16[512,256]{1,0:T(8,128)(2,1)S(1)} %get-tuple-element.60), channel_id=1, source_target_pairs={{0,8},{4,12},{8,0},{12,4},{16,24},{20,28},{24,16},{28,20},{32,40},... | collective-permute-start | bytes 786440 | tf_op jit(solution)/shard_map/ppermute | solution.py:238
  57.1 10.2 %collective-permute-start.12 = (bf16[512,256]{1,0:T(8,128)(2,1)S(1)}, bf16[512,256]{1,0:T(8,128)(2,1)S(1)}, u32[]{:S(2)}, u32[]{:S(2)}) collective-permute-start(bf16[512,256]{1,0:T(8,128)(2,1)S(1)} %get-tuple-element.62), channel_id=1, source_target_pairs={{0,4},{4,8},{8,12},{12,0},{16,20},{20,24},{24,28},{28,16},{32,36},... | collective-permute-start | bytes 786440 | tf_op jit(solution)/shard_map/ppermute | solution.py:238
  61.6 7.7 %collective-permute-start.11 = (bf16[512,256]{1,0:T(8,128)(2,1)S(1)}, bf16[512,256]{1,0:T(8,128)(2,1)S(1)}, u32[]{:S(2)}, u32[]{:S(2)}) collective-permute-start(bf16[512,256]{1,0:T(8,128)(2,1)S(1)} %get-tuple-element.61), channel_id=1, source_target_pairs={{0,12},{4,0},{8,4},{12,8},{16,28},{20,16},{24,20},{28,24},{32,44},... | collective-permute-start | bytes 786440 | tf_op jit(solution)/shard_map/ppermute | solution.py:238
  61.6 13.3 %collective-permute-start.13 = (bf16[256,1024]{1,0:T(8,128)(2,1)S(1)}, bf16[256,1024]{1,0:T(8,128)(2,1)S(1)}, u32[]{:S(2)}, u32[]{:S(2)}) collective-permute-start(bf16[256,1024]{1,0:T(8,128)(2,1)S(1)} %fusion.46), channel_id=1, source_target_pairs={{0,2},{1,3},{2,0},{3,1},{4,6},{5,7},{6,4},{7,5},{8,10},{9,11},{10,... | collective-permute-start | bytes 1572872 | tf_op jit(solution)/shard_map/ppermute | solution.py:244
  75.0 8.1 %collective-permute-start.14 = (bf16[128,256]{1,0:T(8,128)(2,1)S(1)}, bf16[128,256]{1,0:T(8,128)(2,1)S(1)}, u32[]{:S(2)}, u32[]{:S(2)}) collective-permute-start(bf16[128,256]{1,0:T(8,128)(2,1)S(1)} %get-tuple-element.70), channel_id=1, source_target_pairs={{0,48},{4,52},{8,56},{12,60},{16,0},{20,4},{24,8},{28,12},{32,16},... | collective-permute-start | bytes 196616 | tf_op jit(solution)/shard_map/ppermute | solution.py:235
  76.3 8.3 %collective-permute-start.15 = (bf16[128,256]{1,0:T(8,128)(2,1)S(1)}, bf16[128,256]{1,0:T(8,128)(2,1)S(1)}, u32[]{:S(2)}, u32[]{:S(2)}) collective-permute-start(bf16[128,256]{1,0:T(8,128)(2,1)S(1)} %get-tuple-element.72), channel_id=1, source_target_pairs={{0,16},{4,20},{8,24},{12,28},{16,32},{20,36},{24,40},{28,44},{32,4... | collective-permute-start | bytes 196616 | tf_op jit(solution)/shard_map/ppermute | solution.py:235
  78.0 8.4 %collective-permute-start.16 = (bf16[128,256]{1,0:T(8,128)(2,1)S(1)}, bf16[128,256]{1,0:T(8,128)(2,1)S(1)}, u32[]{:S(2)}, u32[]{:S(2)}) collective-permute-start(bf16[128,256]{1,0:T(8,128)(2,1)S(1)} %get-tuple-element.71), channel_id=1, source_target_pairs={{0,32},{4,36},{8,40},{12,44},{16,48},{20,52},{24,56},{28,60},{32,0... | collective-permute-start | bytes 196616 | tf_op jit(solution)/shard_map/ppermute | solution.py:235

commit v3 on v2

v3 whole, which is shorter than its diff:
```python
import functools

import jax
import jax.numpy as jnp
from jax import lax
from jax.experimental import pallas as pl
from jax.experimental.pallas import tpu as pltpu
from jax.sharding import PartitionSpec as P

HD = 128
HEADS = 8
SLOTS = 256
NEG_FILL = -1e30
LOG2E = 1.4426950408889634
SCALE = HD**-0.5
F32 = jnp.float32
BF16 = jnp.bfloat16
FIRST_VMEM = 56


def dot_nn(a, b):
    return lax.dot_general(a, b, (((1,), (0,)), ((), ())), preferred_element_type=F32)


def dot_nt(a, b):
    return lax.dot_general(a, b, (((1,), (1,)), ((), ())), preferred_element_type=F32)


def span(i):
    return slice(i * HD, (i + 1) * HD)


def keys(table):
    return table[0][...] if len(table) == 2 else table[0][:, :HD]


def values(table):
    return table[1][...] if len(table) == 2 else table[0][:, HD:]


def regroup(refs, widths):
    refs = iter(refs)
    return [tuple(next(refs) for _ in range(w)) for w in widths]


def attend(q, tables, causal, weights, scores, turned):
    for table, t in zip(tables, turned):
        t[...] = values(table).T
    for i in range(HEADS):
        for table, masked, score in zip(tables, causal, scores):
            s = dot_nt(keys(table), q[:, span(i)]) * (SCALE * LOG2E)
            if masked:
                key = lax.broadcasted_iota(jnp.int32, s.shape, 0)
                token = lax.broadcasted_iota(jnp.int32, s.shape, 1)
                s = jnp.where(key <= token, s, NEG_FILL)
            score[i] = s
    stats = []
    for i in range(HEADS):
        top = functools.reduce(
            jnp.maximum, [jnp.max(score[i], axis=0, keepdims=True) for score in scores]
        )
        total = 0.0
        for score, w in zip(scores, weights):
            p = jnp.exp2(score[i] - top)
            total = total + jnp.sum(p, axis=0, keepdims=True)
            w[i] = p.astype(BF16)
        stats.append((top, total))
    return stats


def mix(i, weights, turned):
    return sum(dot_nn(t[...], w[i]) for t, w in zip(turned, weights))


def fwd_kernel(widths, causal, *refs):
    count = len(widths)
    q = refs[0]
    at = 1 + sum(widths)
    tables = regroup(refs[1:at], widths)
    weights = refs[at : at + count]
    top_ref, total_ref, acc_ref = refs[at + count : at + count + 3]
    scores = refs[at + count + 3 : at + 2 * count + 3]
    turned = refs[at + 2 * count + 3 :]
    stats = attend(q, tables, causal, weights, scores, turned)
    for i in range(HEADS):
        top_ref[i], total_ref[i] = stats[i]
        acc_ref[span(i), :] = mix(i, weights, turned)


def first_kernel(*refs):
    sources = refs[:3]
    w, top_ref, total_ref, acc_ref = refs[3:7]
    q, key, value = held = refs[7:10]
    score, turned, sems = refs[10:]
    copies = [
        pltpu.make_async_copy(source, target, sems.at[i])
        for i, (source, target) in enumerate(zip(sources, held))
    ]
    for copy in copies:
        copy.start()
    for copy in copies:
        copy.wait()
    stats = attend(q, [(key, value)], (True,), [w], [score], [turned])
    for i in range(HEADS):
        top_ref[i], total_ref[i] = stats[i]
        acc_ref[span(i), :] = mix(i, [w], [turned])


def merge_kernel(count, earlier, *refs):
    length, q, dout = refs[:3]
    tables = [(t,) for t in refs[3 : 3 + count]]
    at = 3 + count
    old = [refs[at + 3 * i : at + 3 * i + 3] for i in range(earlier)]
    at += 3 * earlier
    weights = refs[at : at + count]
    at += count
    alphas = refs[at : at + earlier + 1]
    delta_ref, mixed_ref = refs[at + earlier + 1 : at + earlier + 3]
    at += earlier + 3
    scores = refs[at : at + count]
    turned = refs[at + count :]
    stats = attend(q, tables, (False,) * count, weights, scores, turned)
    for i in range(HEADS):
        parts = [(t[i], l[i], a[span(i), :]) for t, l, a in old]
        parts.append((*stats[i], mix(i, weights, turned)))
        top = functools.reduce(jnp.maximum, [t for t, _, _ in parts])
        factors = [jnp.exp2(t - top) for t, _, _ in parts]
        total = sum(f * l for f, (_, l, _) in zip(factors, parts))
        live = lax.broadcasted_iota(jnp.int32, top.shape, 1) < length[0, 0]
        inverse = jnp.where(live, 1.0 / total, 0.0)
        mixed = 0.0
        for f, (_, _, acc), alpha in zip(factors, parts, alphas):
            alpha[i] = f * inverse
            mixed = mixed + (f * inverse) * acc
        delta_ref[i] = jnp.sum(mixed * dout[span(i), :].astype(F32), axis=0, keepdims=True)
        mixed_ref[span(i), :] = mixed.astype(BF16)


def bwd_kernel(widths, first, last, *refs):
    count = len(widths)
    q, dout, delta = refs[:3]
    alphas = refs[3 : 3 + count]
    at = 3 + count
    tables = regroup(refs[at : at + sum(widths)], widths)
    at += sum(widths)
    weights = refs[at : at + count]
    at += count
    if not first:
        dq_in = refs[at]
        at += 1
    grads = regroup(refs[at : at + sum(widths)], widths)
    at += sum(widths)
    dq_ref = refs[at]
    turned = refs[at + 1 : at + count + 1]
    sums = refs[at + count + 1 :]
    for table, t in zip(tables, turned):
        t[...] = keys(table).T
    for s in sums:
        s[...] = jnp.zeros_like(s)
    for i in range(HEADS):
        dq = 0.0 if first else dq_in[span(i), :]
        for table, alpha, w, kt, s in zip(tables, alphas, weights, turned, sums):
            da = (dout[span(i), :].astype(F32) * alpha[i]).astype(BF16)
            shift = delta[i] * alpha[i]
            p = w[i]
            dp = dot_nn(values(table), da)
            ds = (p.astype(F32) * (dp - shift)).astype(BF16)
            s[:, HD:] += dot_nt(p, da)
            s[:, :HD] += dot_nn(ds, q[:, span(i)])
            dq = dq + dot_nn(kt[...], ds)
        if last:
            dq_ref[:, span(i)] = (dq * SCALE).T.astype(dq_ref.dtype)
        else:
            dq_ref[span(i), :] = dq
    for s, g in zip(sums, grads):
        low, high = s[:, :HD] * SCALE, s[:, HD:]
        if len(g) == 2:
            g[0][...], g[1][...] = low.astype(g[0].dtype), high.astype(g[1].dtype)
        else:
            g[0][:, :HD], g[0][:, HD:] = low.astype(g[0].dtype), high.astype(g[0].dtype)


IN_VMEM = pl.BlockSpec(memory_space=pltpu.VMEM)
STAT = pltpu.VMEM((HEADS, 1, SLOTS), F32)
WIDE = pltpu.VMEM((HEADS * HD, SLOTS), F32)
PARAMS = pltpu.CompilerParams(vmem_limit_bytes=20 * 1024 * 1024)


def call(kernel, name, operands, shapes, scratch, cost, specs=None, params=PARAMS):
    return pl.pallas_call(
        kernel,
        in_specs=specs or [IN_VMEM] * len(operands),
        out_specs=[IN_VMEM] * len(shapes),
        out_shape=shapes,
        scratch_shapes=scratch,
        cost_estimate=cost,
        compiler_params=params,
        name=name,
    )(*operands)


def weight_shapes(tables):
    return [pltpu.VMEM((HEADS, t.shape[0], SLOTS), BF16) for (t, *_) in tables]


def score_shapes(tables):
    return [pltpu.VMEM((HEADS, t.shape[0], SLOTS), F32) for (t, *_) in tables]


def turned_shapes(tables):
    return [pltpu.VMEM((HD, t.shape[0]), BF16) for (t, *_) in tables]


def cost(tables, dots, share=16):
    rows = sum(t[0].shape[0] for t in tables)
    area = rows * SLOTS * HEADS
    return pl.CostEstimate(
        flops=int(dots * area * HD / share), bytes_accessed=area // 16, transcendentals=0
    )


def forward(q, tables, causal, share=16):
    n = len(tables)
    out = call(
        functools.partial(fwd_kernel, [len(t) for t in tables], causal),
        "forward",
        [q, *[x for t in tables for x in t]],
        weight_shapes(tables) + [STAT, STAT, WIDE],
        score_shapes(tables) + turned_shapes(tables),
        cost(tables, 2, share),
    )
    return out[:n], out[n:]


def forward_first(*sources):
    tables = [sources[1:3]]
    out = call(
        first_kernel,
        "forward_first",
        sources,
        weight_shapes(tables)
        + [STAT, STAT, WIDE]
        + [pltpu.VMEM(x.shape, x.dtype) for x in sources],
        score_shapes(tables) + turned_shapes(tables) + [pltpu.SemaphoreType.DMA((3,))],
        cost(tables, 2),
        [pl.BlockSpec(memory_space=pl.ANY)] * 3,
        pltpu.CompilerParams(vmem_limit_bytes=FIRST_VMEM * 1024 * 1024),
    )
    return out[:1], out[1:4], out[4:]


def forward_merge(length, q, dout, tables, old):
    n = len(tables)
    e = len(old)
    operands = [length, q, dout, *[t for (t,) in tables], *[x for part in old for x in part]]
    out = call(
        functools.partial(merge_kernel, n, e),
        "forward_merge",
        operands,
        weight_shapes(tables) + [STAT] * (e + 2) + [pltpu.VMEM((HEADS * HD, SLOTS), BF16)],
        score_shapes(tables) + turned_shapes(tables),
        cost(tables, 2),
        [pl.BlockSpec(memory_space=pltpu.SMEM)] + [IN_VMEM] * (len(operands) - 1),
    )
    return out[:n], out[n : n + e + 1], out[n + e + 1], out[n + e + 2]


def backward(q, dout, delta, alphas, tables, weights, kind, dq, last):
    flat = [x for t in tables for x in t]
    kinds = [kind if len(t) == 1 else BF16 for t in tables for _ in t]
    out = call(
        functools.partial(bwd_kernel, [len(t) for t in tables], dq is None, last),
        "backward",
        [q, dout, delta, *alphas, *flat, *weights, *([] if dq is None else [dq])],
        [jax.ShapeDtypeStruct(t.shape, k) for t, k in zip(flat, kinds)]
        + [jax.ShapeDtypeStruct((SLOTS, HEADS * HD), BF16) if last else WIDE],
        turned_shapes(tables) + [pltpu.VMEM((t[0].shape[0], 2 * HD), F32) for t in tables],
        cost(tables, 4),
    )
    return out[:-1], out[-1]


def group_shift(dz, dx):
    return [(z * 4 + x, (z + dz) % 4 * 4 + (x + dx) % 4) for z in range(4) for x in range(4)]


def tensor_flip(bits):
    return [(t, t ^ bits) for t in range(4)]


def per_device(
    queries, comp_keys, comp_values, prompt_keys, prompt_values, out_weight, cotangent, lengths
):
    q = queries[0, 0]
    cot = cotangent[0, 0]

    def over_z(a, s):
        return lax.ppermute(a, "group", group_shift(s, 0))

    def over_x(a, s):
        return lax.ppermute(a, "group", group_shift(0, s))

    def to_core(a):
        return lax.ppermute(a, "tensor", tensor_flip(1))

    def to_chip(a):
        return lax.ppermute(a, "tensor", tensor_flip(2))

    own = jnp.concatenate([prompt_keys[0], prompt_values[0]], axis=1)
    own, comp_k = lax.optimization_barrier((own, comp_keys[0, 0]))
    wc, partc, (q, comp_k, comp_v) = forward_first(q, comp_k, comp_values[0, 0])
    comp = (comp_k, comp_v)
    (topc, totalc, accc), cot_late = lax.optimization_barrier((partc, cot))
    partc = (topc, totalc, accc)
    chunk0 = jnp.concatenate([own] + [over_z(own, s) for s in (1, 3, 2)], axis=0)
    chunk1, chunk3, chunk2 = [over_x(chunk0, s) for s in (1, 3, 2)]

    me = lax.axis_index("tensor")

    def columns(bits):
        return lax.dynamic_slice_in_dim(out_weight, (me ^ bits) * 1024, 1024, 1)

    cot_core = to_core(cot)
    cot_chip = to_chip(cot_late)
    cot_diag = to_core(cot_chip)
    w0, part0 = forward(q, [(chunk0,)], (False,), 0.02)
    part0, cot = lax.optimization_barrier((part0, cot))
    most = sum(
        dot_nt(columns(bits), part) for bits, part in ((0, cot), (1, cot_core), (2, cot_chip))
    )
    most, chunk1 = lax.optimization_barrier((most, chunk1))
    w13, part13 = forward(q, [(chunk1,), (chunk3,)], (False, False))
    dout = (most + dot_nt(columns(3), cot_diag)).astype(BF16)
    w2, (alphac, alpha0, alpha13, alpha2), delta, mixed = forward_merge(
        lengths, q, dout, [(chunk2,)], [partc, part0, part13]
    )
    (g2,), dq = backward(q, dout, delta, [alpha2], [(chunk2,)], w2, BF16, None, False)

    def partial_out(bits):
        block = lax.dot_general(
            mixed, columns(bits), (((0,), (0,)), ((), ())), preferred_element_type=F32
        )
        return block.astype(BF16)

    other = to_core(jnp.concatenate([partial_out(1), partial_out(3)], axis=0))
    other, dq = lax.optimization_barrier((other, dq))
    pair_mine = partial_out(0).astype(F32) + other[:SLOTS].astype(F32)
    pair_far = partial_out(2).astype(F32) + other[SLOTS:].astype(F32)
    pair_far, alpha13 = lax.optimization_barrier((pair_far.astype(BF16), alpha13))
    far = to_chip(pair_far)
    (g1, g3), dq = backward(
        q, dout, delta, [alpha13, alpha13], [(chunk1,), (chunk3,)], w13, BF16, dq, False
    )
    (g0, gck, gcv), dq = backward(
        q, dout, delta, [alpha0, alphac], [(chunk0,), comp], [*w0, *wc], F32, dq, True
    )

    back2, far = lax.optimization_barrier((over_x(g2, -2), far))
    back1, back3 = over_x(g1, -1), over_x(g3, -3)
    rows = g0 + back2.astype(F32) + back1.astype(F32) + back3.astype(F32)
    n = own.shape[0]
    sent = rows.astype(BF16)
    total = rows[:n]
    for i, s in enumerate((1, 3, 2)):
        total = total + over_z(sent[(i + 1) * n : (i + 2) * n], -s).astype(F32)
    total = total.astype(BF16)
    output = (pair_mine + far.astype(F32)).astype(BF16)
    return (
        output[None, None],
        dq[None, None],
        gck[None, None],
        gcv[None, None],
        total[None, :, :HD],
        total[None, :, HD:],
    )


def solution(mesh):
    wide = P("dp", "group", None, "tensor")
    rows = P("dp", "group", "tensor")
    return jax.shard_map(
        per_device,
        mesh=mesh,
        in_specs=(wide, wide, wide, rows, rows, P("tensor", None), wide, P("dp", "group")),
        out_specs=(wide, wide, wide, wide, rows, rows),
        check_vma=False,
    )
```

time: 88.3 us -> 75.5 us (0.86)
  starting transfers between devices: 31.2 us -> 26.5 us
  waiting for transfers between devices: 18.8 us -> 16.2 us
  matrix products: 10.2 us -> 7.8 us
  other arithmetic: 2.71 us -> 1.02 us
  local copies, waits for them, and re-layouts: 2.35 us -> 1.24 us
    ppermute x6, starting transfers between devices: 10 us -> 7.47 us  [over_x(): return lax.ppermute(a, 'group', group_shift(0, s))]
    dot_general x4, matrix products: 6.45 us -> 4.02 us  [dot_nt(): lax.dot_general(a, b, (((1,), (1,)), ((), ())), preferred_element_type=F32)]
    ppermute x6, waiting for transfers between devices: 7.3 us -> 4.97 us  [over_z(): return lax.ppermute(a, 'group', group_shift(s, 0))]
    concatenate x2 -> x0, other arithmetic: 1.68 us -> none  [the longest x1 0.89 us: per_device(): comp = jnp.concatenate([comp_keys[0, 0], comp_values[0, 0]], axis=1)]
    ppermute x6, starting transfers between devices: 17.9 us -> 16.7 us  [over_z(): return lax.ppermute(a, 'group', group_shift(s, 0))]
    ppermute x6, waiting for transfers between devices: 5.97 us -> 4.94 us  [over_x(): return lax.ppermute(a, 'group', group_shift(0, s))]
  transfers between devices with their start and end apart: 17 -> 17, of which waited for: 7 -> 8; matrix products, arithmetic and copies ran while one was open for 12% -> 7% of each run, Pallas kernels for 21% -> 25%
where the time goes in v3:
time: 75.5 us; the launch traced here: 75.1 us
  starting transfers between devices  26.5 us (35%)
  Pallas kernels  20.8 us (28%)
  waiting for transfers between devices  16.2 us (21%)
  matrix products  7.8 us (10%)
  between operations  1.5 us (2%)
  local copies, waits for them, and re-layouts  1.24 us (2%)
  other arithmetic  1.02 us (1%)
    pallas_call x7, Pallas kernels, call(): pl.pallas_call(kernel, in_specs=specs or [IN_VMEM] * len(operands), out_s...  20.8 us
    ppermute x6, starting transfers between devices, over_z(): return lax.ppermute(a, 'group', group_shift(s, 0))  16.7 us
    ppermute x6, starting transfers between devices, over_x(): return lax.ppermute(a, 'group', group_shift(0, s))  7.47 us
    ppermute x2, waiting for transfers between devices, to_chip(): return lax.ppermute(a, 'tensor', tensor_flip(2))  6.32 us
    ppermute x6, waiting for transfers between devices, over_z(): return lax.ppermute(a, 'group', group_shift(s, 0))  4.97 us
    ppermute x6, waiting for transfers between devices, over_x(): return lax.ppermute(a, 'group', group_shift(0, s))  4.94 us
    dot_general x4, matrix products, dot_nt(): lax.dot_general(a, b, (((1,), (1,)), ((), ())), preferred_element_type=F32)  4.02 us
    dot_general x4, matrix products, partial_out(): lax.dot_general(mixed, columns(bits), (((0,), (0,)), ((), ())), preferred...  3.78 us
  transfers between devices with their start and end apart: 17, of which 8 were waited for; matrix products, arithmetic and copies ran while one was open for 7% of the time, Pallas kernels for 25%

profile of v3, /device:TPU:8, one launch (start us, length us, event | category | flops | bytes accessed | tf_op | source)
XLA Modules:
  0.0 75.1 jit_solution(11851237676306437386)
XLA Ops:
  0.6 0.8 %pad_maximum_fusion.1 = bf16[128,256]{1,0:T(8,128)(2,1)S(1)} fusion(bf16[128,128]{1,0:T(8,128)(2,1)} %bitcast.31, bf16[128,128]{1,0:T(8,128)(2,1)} %bitcast.32), kind=kLoop, calls=%fused_computation.38 | loop fusion | flops 131072 | bytes 131072 | tf_op jit(solution)/shard_map/concatenate | solution.py:309
  1.4 7.3 %collective-permute-start.2 = (bf16[128,256]{1,0:T(8,128)(2,1)S(1)}, bf16[128,256]{1,0:T(8,128)(2,1)S(1)}, u32[]{:S(2)}, u32[]{:S(2)}) collective-permute-start(bf16[128,256]{1,0:T(8,128)(2,1)S(1)} %pad_maximum_fusion.1), channel_id=1, source_target_pairs={{0,32},{4,36},{8,40},{12,44},{16,48},{20,52},{24,56},{28,60},{32,0... | collective-permute-start | bytes 196616 | tf_op jit(solution)/shard_map/ppermute | solution.py:298
  8.7 0.0 collective-permute-start.1
  8.7 2.9 %collective-permute-start = (bf16[128,256]{1,0:T(8,128)(2,1)S(1)}, bf16[128,256]{1,0:T(8,128)(2,1)S(1)}, u32[]{:S(2)}, u32[]{:S(2)}) collective-permute-start(bf16[128,256]{1,0:T(8,128)(2,1)S(1)} %pad_maximum_fusion.1), channel_id=1, source_target_pairs={{0,16},{4,20},{8,24},{12,28},{16,32},{20,36},{24,40},{28,44},{32,4... | collective-permute-start | bytes 196616 | tf_op jit(solution)/shard_map/ppermute | solution.py:298
  11.6 0.0 collective-permute-start.3
  11.6 2.0 %forward_first.1 = (bf16[8,256,256]{2,1,0:T(8,128)(2,1)S(1)}, f32[8,1,256]{2,1,0:T(1,128)S(1)}, f32[8,1,256]{2,1,0:T(1,128)S(1)}, f32[1024,256]{1,0:T(8,128)S(1)...) custom-call(bf16[256,1024]{1,0:T(8,128)(2,1)} %bitcast.25, ...), custom_call_target="tpu_custom_call" | custom-call | flops 8388608 | bytes 32768 | tf_op jit(solution)/shard_map/forward_first/pallas_call | solution.py:190
  13.6 1.1 %collective-permute-start.4 = (bf16[256,1024]{1,0:T(8,128)(2,1)}, bf16[256,1024]{1,0:T(8,128)(2,1)}, u32[]{:S(2)}, u32[]{:S(2)}) collective-permute-start(bf16[256,1024]{1,0:T(8,128)(2,1)} %bitcast.27), channel_id=1, source_target_pairs={{0,2},{1,3},{2,0},{3,1},{4,6},{5,7},{6,4},{7,5},{8,10},{9,11},{10,... | collective-permute-start | bytes 1572872 | tf_op jit(solution)/shard_map/ppermute | solution.py:307
  15.4 0.0 slice-start
  15.4 0.0 collective-permute-done
  15.4 0.2 collective-permute-done.1
  15.6 0.0 collective-permute-done.2
  15.6 2.8 %collective-permute-start.8 = (bf16[512,256]{1,0:T(8,128)(2,1)S(1)}, bf16[512,256]{1,0:T(8,128)(2,1)S(1)}, u32[]{:S(2)}, u32[]{:S(2)}) collective-permute-start(bf16[512,256]{1,0:T(8,128)(2,1)S(1)} %constant_dynamic-update-slice_fusion.refs_1_.refs_5_), channel_id=1, source_target_pairs={{0,12},{4,0},{8,4},{12,8},{16,28},{20,16},{24,20},{28,24},{32,44},... | collective-permute-start | bytes 786440 | tf_op jit(solution)/shard_map/ppermute | solution.py:301
  18.5 0.8 %collective-permute-start.7 = (bf16[512,256]{1,0:T(8,128)(2,1)S(1)}, bf16[512,256]{1,0:T(8,128)(2,1)S(1)}, u32[]{:S(2)}, u32[]{:S(2)}) collective-permute-start(bf16[512,256]{1,0:T(8,128)(2,1)S(1)} %constant_dynamic-update-slice_fusion.refs_1_.refs_5_), channel_id=1, source_target_pairs={{0,8},{4,12},{8,0},{12,4},{16,24},{20,28},{24,16},{28,20},{32,40},... | collective-permute-start | bytes 786440 | tf_op jit(solution)/shard_map/ppermute | solution.py:301
  19.3 0.9 %collective-permute-start.5 = (bf16[512,256]{1,0:T(8,128)(2,1)S(1)}, bf16[512,256]{1,0:T(8,128)(2,1)S(1)}, u32[]{:S(2)}, u32[]{:S(2)}) collective-permute-start(bf16[512,256]{1,0:T(8,128)(2,1)S(1)} %constant_dynamic-update-slice_fusion.refs_1_.refs_5_), channel_id=1, source_target_pairs={{0,4},{4,8},{8,12},{12,0},{16,20},{20,24},{24,28},{28,16},{32,36},... | collective-permute-start | bytes 786440 | tf_op jit(solution)/shard_map/ppermute | solution.py:301
  20.2 0.0 slice-start.1
  20.2 0.0 copy-start
  20.2 1.7 %forward.2 = (bf16[8,512,256]{2,1,0:T(8,128)(2,1)S(1)}, f32[8,1,256]{2,1,0:T(1,128)S(1)}, f32[8,1,256]{2,1,0:T(1,128)S(1)}, f32[1024,256]{1,0:T(8,128)S(1)}) custom-call(bf16[256,1024]{1,0:T(8,128)(2,1)S(1)} %get-tuple-element.57.refs_0_.refs_1_, bf16[512,256]{1,0:T(8,128)(2,1)S(1)} %constant_dynamic-update-slice_fusion.refs_1_.refs_5_), custom_call_target="tpu_custom_call" | custom-call | flops 13421772800 | bytes 65536 | tf_op jit(solution)/shard_map/forward/pallas_call | solution.py:190
  21.9 0.0 slice-done
  21.9 0.4 slice-done.1
  22.3 0.1 copy-done
  22.5 0.7 fusion.14
  23.2 5.1 %collective-permute-done.4 = bf16[256,1024]{1,0:T(8,128)(2,1)} collective-permute-done((bf16[256,1024]{1,0:T(8,128)(2,1)}, bf16[256,1024]{1,0:T(8,128)(2,1)}, u32[]{:S(2)}, u32[]{:S(2)}) %collective-permute-start.4) | collective-permute-done | bytes 524320 | tf_op jit(solution)/shard_map/ppermute | solution.py:307
  28.3 0.0 collective-permute-start.6
  28.3 1.8 %fusion.6 = f32[1024,256]{1,0:T(8,128)S(1)} fusion(bf16[256,1024]{1,0:T(8,128)(2,1)} %collective-permute-done.4, bf16[1024,4096]{1,0:T(8,128)(2,1)S(1)} %bitcast.24, s32[]{:T(128)S(6)} %select_n.18), kind=kOutput, calls=%fused_computation.6 | convolution fusion | flops 536870912 | bytes 3670020 | tf_op jit(solution)/shard_map/dot_general | solution.py:26
  30.1 0.0 collective-permute-done.3
  30.1 0.7 fusion.19
  30.9 2.7 %collective-permute-done.5.refs_1_.refs_5_ = bf16[512,256]{1,0:T(8,128)(2,1)S(1)} collective-permute-done((bf16[512,256]{1,0:T(8,128)(2,1)S(1)}, bf16[512,256]{1,0:T(8,128)(2,1)S(1)}, u32[]{:S(2)}, u32[]{:S(2)}) %collective-permute-start.5) | collective-permute-done | bytes 262176 | tf_op jit(solution)/shard_map/ppermute | solution.py:301
  33.6 0.0 collective-permute-done.8.refs_2_.refs_6_
  33.6 3.2 %forward.3 = (bf16[8,512,256]{2,1,0:T(8,128)(2,1)S(1)}, bf16[8,512,256]{2,1,0:T(8,128)(2,1)S(1)}, f32[8,1,256]{2,1,0:T(1,128)S(1)}, f32[8,1,256]{2,1,0:T(1,128)S(1)}, f32[1024,256]{1,0:T(8,128)S(1)}) custom-call(bf16[256,1024]{1,0:T(8,128)(2,1)S(1)} %get-tuple-element.57.refs_0_.refs_1_, bf16[512,256]{1,0:T(8,128)(2,1)S(1)} %collective-permute-done.5.refs_1_.refs_5_, ...), custom_call_target="tpu_custom_call" | custom-call | flops 33554432 | bytes 131072 | tf_op jit(solution)/shard_map/forward/pallas_call | solution.py:190
  36.8 0.0 collective-permute-done.6
  36.8 0.7 fusion.25.refs_2_.refs_1_
  37.6 0.0 collective-permute-done.7.refs_3_.refs_4_
  37.6 2.1 %forward_merge.1 = (bf16[8,512,256]{2,1,0:T(8,128)(2,1)S(1)}, f32[8,1,256]{2,1,0:T(1,128)S(1)}, f32[8,1,256]{2,1,0:T(1,128)S(1)}, f32[8,1,256]{2,1,0:T(1,128)S(1...) custom-call(s32[1,1]{1,0:T(1,128)S(6)} %copy.17.refs_0_, ...), custom_call_target="tpu_custom_call" | custom-call | flops 16777216 | bytes 65536 | tf_op jit(solution)/shard_map/forward_merge/pallas_call | solution.py:190
  39.7 0.7 fusion.37
  40.4 0.7 fusion.31
  41.2 0.1 pad_maximum_fusion
  41.3 0.1 collective-permute-start.9
  41.4 2.6 %backward.3 = (bf16[512,256]{1,0:T(8,128)(2,1)S(1)}, f32[1024,256]{1,0:T(8,128)S(1)}) custom-call(bf16[256,1024]{1,0:T(8,128)(2,1)S(1)} %get-tuple-element.57.refs_0_.refs_1_, bf16[1024,256]{1,0:T(8,128)(2,1)S(1)} %fusion.25.refs_2_.refs_1_, f32[8,1,256]{2,1,0:T(1,128)S(1)} %get-tuple-element.79.refs_2_, f32[8,1,256]{2,1,0:T(1,128)S(1)} %get-tuple-element.80.refs_3_, ...), custom_call_target="tpu_custom_call" | custom-call | flops 33554432 | bytes 65536 | tf_op jit(solution)/shard_map/backward/pallas_call | solution.py:190
  44.0 0.0 collective-permute-done.9
  44.0 0.7 fusion.46
  44.8 1.1 %collective-permute-start.11 = (bf16[256,1024]{1,0:T(8,128)(2,1)S(1)}, bf16[256,1024]{1,0:T(8,128)(2,1)S(1)}, u32[]{:S(2)}, u32[]{:S(2)}) collective-permute-start(bf16[256,1024]{1,0:T(8,128)(2,1)S(1)} %fusion.46), channel_id=1, source_target_pairs={{0,2},{1,3},{2,0},{3,1},{4,6},{5,7},{6,4},{7,5},{8,10},{9,11},{10,... | collective-permute-start | bytes 1572872 | tf_op jit(solution)/shard_map/ppermute | solution.py:307
  45.8 0.8 %collective-permute-start.10 = (bf16[512,256]{1,0:T(8,128)(2,1)S(1)}, bf16[512,256]{1,0:T(8,128)(2,1)S(1)}, u32[]{:S(2)}, u32[]{:S(2)}) collective-permute-start(bf16[512,256]{1,0:T(8,128)(2,1)S(1)} %get-tuple-element.84), channel_id=1, source_target_pairs={{0,8},{4,12},{8,0},{12,4},{16,24},{20,28},{24,16},{28,20},{32,40},... | collective-permute-start | bytes 786440 | tf_op jit(solution)/shard_map/ppermute | solution.py:301
  46.7 4.4 %backward.4 = (bf16[512,256]{1,0:T(8,128)(2,1)S(1)}, bf16[512,256]{1,0:T(8,128)(2,1)S(1)}, f32[1024,256]{1,0:T(8,128)S(1)}) custom-call(bf16[256,1024]{1,0:T(8,128)(2,1)S(1)} %get-tuple-element.57.refs_0_.refs_1_, bf16[1024,256]{1,0:T(8,128)(2,1)S(1)} %fusion.25.refs_2_.refs_1_, f32[8,1,256]{2,1,0:T(1,128)S(1)} %get-tuple-element.79.refs_2_, ...), custom_call_target="tpu_custom_call" | custom-call | flops 67108864 | bytes 131072 | tf_op jit(solution)/shard_map/backward/pallas_call | solution.py:190
  51.1 1.2 %collective-permute-start.12 = (bf16[512,256]{1,0:T(8,128)(2,1)S(1)}, bf16[512,256]{1,0:T(8,128)(2,1)S(1)}, u32[]{:S(2)}, u32[]{:S(2)}) collective-permute-start(bf16[512,256]{1,0:T(8,128)(2,1)S(1)} %get-tuple-element.104), channel_id=1, source_target_pairs={{0,12},{4,0},{8,4},{12,8},{16,28},{20,16},{24,20},{28,24},{32,44},... | collective-permute-start | bytes 786440 | tf_op jit(solution)/shard_map/ppermute | solution.py:301
  52.3 0.9 %collective-permute-start.13 = (bf16[512,256]{1,0:T(8,128)(2,1)S(1)}, bf16[512,256]{1,0:T(8,128)(2,1)S(1)}, u32[]{:S(2)}, u32[]{:S(2)}) collective-permute-start(bf16[512,256]{1,0:T(8,128)(2,1)S(1)} %get-tuple-element.105), channel_id=1, source_target_pairs={{0,4},{4,8},{8,12},{12,0},{16,20},{20,24},{24,28},{28,16},{32,36},... | collective-permute-start | bytes 786440 | tf_op jit(solution)/shard_map/ppermute | solution.py:301
  53.2 4.8 %backward.5 = (f32[512,256]{1,0:T(8,128)S(1)}, bf16[256,128]{1,0:T(8,128)(2,1)}, bf16[256,128]{1,0:T(8,128)(2,1)}, bf16[256,1024]{1,0:T(8,128)(2,1)}) custom-call(bf16[256,1024]{1,0:T(8,128)(2,1)S(1)} %get-tuple-element.57.refs_0_.refs_1_, bf16[1024,256]{1,0:T(8,128)(2,1)S(1)} %fusion.25.refs_2_.refs_1_, f32[8,1,256]{2,1,0:T(1,128)S(1)} %get-tuple-element.79.refs_2_, ...), custom_call_target="tpu_custom_call" | custom-call | flops 50331648 | bytes 98304 | tf_op jit(solution)/shard_map/backward/pallas_call | solution.py:190
  58.0 0.0 collective-permute-done.10
  58.0 1.2 %collective-permute-done.11 = bf16[256,1024]{1,0:T(8,128)(2,1)S(1)} collective-permute-done((bf16[256,1024]{1,0:T(8,128)(2,1)S(1)}, bf16[256,1024]{1,0:T(8,128)(2,1)S(1)}, u32[]{:S(2)}, u32[]{:S(2)}) %collective-permute-start.11) | collective-permute-done | bytes 524320 | tf_op jit(solution)/shard_map/ppermute | solution.py:307
  59.1 0.2 collective-permute-done.12
  59.3 2.1 %collective-permute-done.13 = bf16[512,256]{1,0:T(8,128)(2,1)S(1)} collective-permute-done((bf16[512,256]{1,0:T(8,128)(2,1)S(1)}, bf16[512,256]{1,0:T(8,128)(2,1)S(1)}, u32[]{:S(2)}, u32[]{:S(2)}) %collective-permute-start.13) | collective-permute-done | bytes 262176 | tf_op jit(solution)/shard_map/ppermute | solution.py:301
  61.4 0.1 fusion.75
  61.5 3.0 %collective-permute-start.14 = (bf16[128,256]{1,0:T(8,128)(2,1)S(1)}, bf16[128,256]{1,0:T(8,128)(2,1)S(1)}, u32[]{:S(2)}, u32[]{:S(2)}) collective-permute-start(bf16[128,256]{1,0:T(8,128)(2,1)S(1)} %get-tuple-element.108), channel_id=1, source_target_pairs={{0,48},{4,52},{8,56},{12,60},{16,0},{20,4},{24,8},{28,12},{32,16},... | collective-permute-start | bytes 196616 | tf_op jit(solution)/shard_map/ppermute | solution.py:298
  64.5 3.4 %collective-permute-start.16 = (bf16[128,256]{1,0:T(8,128)(2,1)S(1)}, bf16[128,256]{1,0:T(8,128)(2,1)S(1)}, u32[]{:S(2)}, u32[]{:S(2)}) collective-permute-start(bf16[128,256]{1,0:T(8,128)(2,1)S(1)} %get-tuple-element.109), channel_id=1, source_target_pairs={{0,32},{4,36},{8,40},{12,44},{16,48},{20,52},{24,56},{28,60},{32,0... | collective-permute-start | bytes 196616 | tf_op jit(solution)/shard_map/ppermute | solution.py:298
  67.9 0.2 collective-permute-start.15
  68.0 1.6 %fusion.61 = bf16[1,1,256,1024]{3,2,1,0:T(8,128)(2,1)} fusion(bf16[1024,256]{1,0:T(8,128)(2,1)S(1)} %get-tuple-element.78, bf16[1024,4096]{1,0:T(8,128)(2,1)S(1)} %bitcast.24, s32[]{:T(128)S(6)} %select_n.16, bf16[256,1024]{1,0:T(8,128)(2,1)S(1)} %collective-permute-done.11, bf16[512,1024]{1,0:T(8,128)(2,1)S(1)} %collective-permute-done.9), kind=kOutput, calls=%fused_computation.31 | convolution fusion | flops 538705920 | bytes 4194308 | tf_op jit(solution)/shard_map/dot_general | solution.py:340
  69.6 0.0 collective-permute-done.14
  69.6 4.1 %collective-permute-done.16 = bf16[128,256]{1,0:T(8,128)(2,1)S(1)} collective-permute-done((bf16[128,256]{1,0:T(8,128)(2,1)S(1)}, bf16[128,256]{1,0:T(8,128)(2,1)S(1)}, u32[]{:S(2)}, u32[]{:S(2)}) %collective-permute-start.16) | collective-permute-done | bytes 65568 | tf_op jit(solution)/shard_map/ppermute | solution.py:298
  73.7 0.7 collective-permute-done.15
  74.4 0.6 slice_bitcast_fusion
  (7 shorter events, 0.1 us)
Async XLA Ops:
  1.4 14.2 %collective-permute-start.2 = (bf16[128,256]{1,0:T(8,128)(2,1)S(1)}, bf16[128,256]{1,0:T(8,128)(2,1)S(1)}, u32[]{:S(2)}, u32[]{:S(2)}) collective-permute-start(bf16[128,256]{1,0:T(8,128)(2,1)S(1)} %pad_maximum_fusion.1), channel_id=1, source_target_pairs={{0,32},{4,36},{8,40},{12,44},{16,48},{20,52},{24,56},{28,60},{32,0... | collective-permute-start | bytes 196616 | tf_op jit(solution)/shard_map/ppermute | solution.py:298
  8.7 6.9 %collective-permute-start.1 = (bf16[128,256]{1,0:T(8,128)(2,1)S(1)}, bf16[128,256]{1,0:T(8,128)(2,1)S(1)}, u32[]{:S(2)}, u32[]{:S(2)}) collective-permute-start(bf16[128,256]{1,0:T(8,128)(2,1)S(1)} %pad_maximum_fusion.1), channel_id=1, source_target_pairs={{0,48},{4,52},{8,56},{12,60},{16,0},{20,4},{24,8},{28,12},{32,16},... | collective-permute-start | bytes 196616 | tf_op jit(solution)/shard_map/ppermute | solution.py:298
  8.7 6.7 %collective-permute-start = (bf16[128,256]{1,0:T(8,128)(2,1)S(1)}, bf16[128,256]{1,0:T(8,128)(2,1)S(1)}, u32[]{:S(2)}, u32[]{:S(2)}) collective-permute-start(bf16[128,256]{1,0:T(8,128)(2,1)S(1)} %pad_maximum_fusion.1), channel_id=1, source_target_pairs={{0,16},{4,20},{8,24},{12,28},{16,32},{20,36},{24,40},{28,44},{32,4... | collective-permute-start | bytes 196616 | tf_op jit(solution)/shard_map/ppermute | solution.py:298
  11.6 18.5 %collective-permute-start.3 = (bf16[256,1024]{1,0:T(8,128)(2,1)}, bf16[256,1024]{1,0:T(8,128)(2,1)S(1)}, u32[]{:S(2)}, u32[]{:S(2)}) collective-permute-start(bf16[256,1024]{1,0:T(8,128)(2,1)} %bitcast.26), channel_id=1, source_target_pairs={{0,1},{1,0},{2,3},{3,2},{4,5},{5,4},{6,7},{7,6},{8,9},{9,8},{10,11... | collective-permute-start | bytes 1572872 | tf_op jit(solution)/shard_map/ppermute | solution.py:304
  13.6 14.7 %collective-permute-start.4 = (bf16[256,1024]{1,0:T(8,128)(2,1)}, bf16[256,1024]{1,0:T(8,128)(2,1)}, u32[]{:S(2)}, u32[]{:S(2)}) collective-permute-start(bf16[256,1024]{1,0:T(8,128)(2,1)} %bitcast.27), channel_id=1, source_target_pairs={{0,2},{1,3},{2,0},{3,1},{4,6},{5,7},{6,4},{7,5},{8,10},{9,11},{10,... | collective-permute-start | bytes 1572872 | tf_op jit(solution)/shard_map/ppermute | solution.py:307
  15.4 6.5 %slice-start = ((s8[8388608]{0:T(1024)(128)(4,1)}), s8[4194304]{0:T(1024)(128)(4,1)S(1)}, s32[]{:S(2)}) async-start(s8[8388608]{0:T(1024)(128)(4,1)} %bitcast.23), calls=%async_computation | async-start | bytes 8388608
  15.6 18.0 %collective-permute-start.8 = (bf16[512,256]{1,0:T(8,128)(2,1)S(1)}, bf16[512,256]{1,0:T(8,128)(2,1)S(1)}, u32[]{:S(2)}, u32[]{:S(2)}) collective-permute-start(bf16[512,256]{1,0:T(8,128)(2,1)S(1)} %constant_dynamic-update-slice_fusion.refs_1_.refs_5_), channel_id=1, source_target_pairs={{0,12},{4,0},{8,4},{12,8},{16,28},{20,16},{24,20},{28,24},{32,44},... | collective-permute-start | bytes 786440 | tf_op jit(solution)/shard_map/ppermute | solution.py:301
  18.5 19.1 %collective-permute-start.7 = (bf16[512,256]{1,0:T(8,128)(2,1)S(1)}, bf16[512,256]{1,0:T(8,128)(2,1)S(1)}, u32[]{:S(2)}, u32[]{:S(2)}) collective-permute-start(bf16[512,256]{1,0:T(8,128)(2,1)S(1)} %constant_dynamic-update-slice_fusion.refs_1_.refs_5_), channel_id=1, source_target_pairs={{0,8},{4,12},{8,0},{12,4},{16,24},{20,28},{24,16},{28,20},{32,40},... | collective-permute-start | bytes 786440 | tf_op jit(solution)/shard_map/ppermute | solution.py:301
  19.3 14.3 %collective-permute-start.5 = (bf16[512,256]{1,0:T(8,128)(2,1)S(1)}, bf16[512,256]{1,0:T(8,128)(2,1)S(1)}, u32[]{:S(2)}, u32[]{:S(2)}) collective-permute-start(bf16[512,256]{1,0:T(8,128)(2,1)S(1)} %constant_dynamic-update-slice_fusion.refs_1_.refs_5_), channel_id=1, source_target_pairs={{0,4},{4,8},{8,12},{12,0},{16,20},{20,24},{24,28},{28,16},{32,36},... | collective-permute-start | bytes 786440 | tf_op jit(solution)/shard_map/ppermute | solution.py:301
  20.2 2.2 %slice-start.1 = ((s8[8388608]{0:T(1024)(128)(4,1)}), s8[4194304]{0:T(1024)(128)(4,1)S(1)}, s32[]{:S(2)}) async-start(s8[8388608]{0:T(1024)(128)(4,1)} %bitcast.23), calls=%async_computation.1 | async-start | bytes 8388608
  20.2 2.3 %copy-start = (bf16[1,1,256,1024]{3,2,1,0:T(8,128)(2,1)S(1)}, bf16[1,1,256,1024]{3,2,1,0:T(8,128)(2,1)}, u32[]{:S(2)}) copy-start(bf16[1,1,256,1024]{3,2,1,0:T(8,128)(2,1)} %param.14) | copy-start | bytes 1572868
  28.3 8.5 %collective-permute-start.6 = (bf16[256,1024]{1,0:T(8,128)(2,1)}, bf16[256,1024]{1,0:T(8,128)(2,1)S(1)}, u32[]{:S(2)}, u32[]{:S(2)}) collective-permute-start(bf16[256,1024]{1,0:T(8,128)(2,1)} %collective-permute-done.4), channel_id=1, source_target_pairs={{0,1},{1,0},{2,3},{3,2},{4,5},{5,4},{6,7},{7,6},{8,9},{9,8},{10,11... | collective-permute-start | bytes 1572872 | tf_op jit(solution)/shard_map/ppermute | solution.py:304
  41.3 2.7 %collective-permute-start.9 = (bf16[512,1024]{1,0:T(8,128)(2,1)S(1)}, bf16[512,1024]{1,0:T(8,128)(2,1)S(1)}, u32[]{:S(2)}, u32[]{:S(2)}) collective-permute-start(bf16[512,1024]{1,0:T(8,128)(2,1)S(1)} %pad_maximum_fusion), channel_id=1, source_target_pairs={{0,1},{1,0},{2,3},{3,2},{4,5},{5,4},{6,7},{7,6},{8,9},{9,8},{10,11... | collective-permute-start | bytes 3145736 | tf_op jit(solution)/shard_map/ppermute | solution.py:304
  44.8 14.4 %collective-permute-start.11 = (bf16[256,1024]{1,0:T(8,128)(2,1)S(1)}, bf16[256,1024]{1,0:T(8,128)(2,1)S(1)}, u32[]{:S(2)}, u32[]{:S(2)}) collective-permute-start(bf16[256,1024]{1,0:T(8,128)(2,1)S(1)} %fusion.46), channel_id=1, source_target_pairs={{0,2},{1,3},{2,0},{3,1},{4,6},{5,7},{6,4},{7,5},{8,10},{9,11},{10,... | collective-permute-start | bytes 1572872 | tf_op jit(solution)/shard_map/ppermute | solution.py:307
  45.8 12.1 %collective-permute-start.10 = (bf16[512,256]{1,0:T(8,128)(2,1)S(1)}, bf16[512,256]{1,0:T(8,128)(2,1)S(1)}, u32[]{:S(2)}, u32[]{:S(2)}) collective-permute-start(bf16[512,256]{1,0:T(8,128)(2,1)S(1)} %get-tuple-element.84), channel_id=1, source_target_pairs={{0,8},{4,12},{8,0},{12,4},{16,24},{20,28},{24,16},{28,20},{32,40},... | collective-permute-start | bytes 786440 | tf_op jit(solution)/shard_map/ppermute | solution.py:301
  51.1 8.2 %collective-permute-start.12 = (bf16[512,256]{1,0:T(8,128)(2,1)S(1)}, bf16[512,256]{1,0:T(8,128)(2,1)S(1)}, u32[]{:S(2)}, u32[]{:S(2)}) collective-permute-start(bf16[512,256]{1,0:T(8,128)(2,1)S(1)} %get-tuple-element.104), channel_id=1, source_target_pairs={{0,12},{4,0},{8,4},{12,8},{16,28},{20,16},{24,20},{28,24},{32,44},... | collective-permute-start | bytes 786440 | tf_op jit(solution)/shard_map/ppermute | solution.py:301
  52.3 9.1 %collective-permute-start.13 = (bf16[512,256]{1,0:T(8,128)(2,1)S(1)}, bf16[512,256]{1,0:T(8,128)(2,1)S(1)}, u32[]{:S(2)}, u32[]{:S(2)}) collective-permute-start(bf16[512,256]{1,0:T(8,128)(2,1)S(1)} %get-tuple-element.105), channel_id=1, source_target_pairs={{0,4},{4,8},{8,12},{12,0},{16,20},{20,24},{24,28},{28,16},{32,36},... | collective-permute-start | bytes 786440 | tf_op jit(solution)/shard_map/ppermute | solution.py:301
  61.5 8.1 %collective-permute-start.14 = (bf16[128,256]{1,0:T(8,128)(2,1)S(1)}, bf16[128,256]{1,0:T(8,128)(2,1)S(1)}, u32[]{:S(2)}, u32[]{:S(2)}) collective-permute-start(bf16[128,256]{1,0:T(8,128)(2,1)S(1)} %get-tuple-element.108), channel_id=1, source_target_pairs={{0,48},{4,52},{8,56},{12,60},{16,0},{20,4},{24,8},{28,12},{32,16},... | collective-permute-start | bytes 196616 | tf_op jit(solution)/shard_map/ppermute | solution.py:298
  64.5 9.2 %collective-permute-start.16 = (bf16[128,256]{1,0:T(8,128)(2,1)S(1)}, bf16[128,256]{1,0:T(8,128)(2,1)S(1)}, u32[]{:S(2)}, u32[]{:S(2)}) collective-permute-start(bf16[128,256]{1,0:T(8,128)(2,1)S(1)} %get-tuple-element.109), channel_id=1, source_target_pairs={{0,32},{4,36},{8,40},{12,44},{16,48},{20,52},{24,56},{28,60},{32,0... | collective-permute-start | bytes 196616 | tf_op jit(solution)/shard_map/ppermute | solution.py:298
  67.9 6.5 %collective-permute-start.15 = (bf16[128,256]{1,0:T(8,128)(2,1)S(1)}, bf16[128,256]{1,0:T(8,128)(2,1)S(1)}, u32[]{:S(2)}, u32[]{:S(2)}) collective-permute-start(bf16[128,256]{1,0:T(8,128)(2,1)S(1)} %get-tuple-element.110), channel_id=1, source_target_pairs={{0,16},{4,20},{8,24},{12,28},{16,32},{20,36},{24,40},{28,44},{32,4... | collective-permute-start | bytes 196616 | tf_op jit(solution)/shard_map/ppermute | solution.py:298

commit v4 on v3

--- a/solution.py
+++ b/solution.py
@@ -30,6 +30,10 @@
     return slice(i * HD, (i + 1) * HD)
 
 
+def wide(i):
+    return slice(i * SLOTS, (i + 1) * SLOTS)
+
+
 def keys(table):
     return table[0][...] if len(table) == 2 else table[0][:, :HD]
 
@@ -63,13 +67,13 @@
         for score, w in zip(scores, weights):
             p = jnp.exp2(score[i] - top)
             total = total + jnp.sum(p, axis=0, keepdims=True)
-            w[i] = p.astype(BF16)
+            w[:, wide(i)] = p.astype(BF16)
         stats.append((top, total))
     return stats
 
 
 def mix(i, weights, turned):
-    return sum(dot_nn(t[...], w[i]) for t, w in zip(turned, weights))
+    return sum(dot_nn(t[...], w[:, wide(i)]) for t, w in zip(turned, weights))
 
 
 def fwd_kernel(widths, causal, *refs):
@@ -152,32 +156,32 @@
     at += sum(widths)
     dq_ref = refs[at]
     turned = refs[at + 1 : at + count + 1]
-    sums = refs[at + count + 1 :]
+    slopes = refs[at + count + 1 : at + 2 * count + 1]
+    scaled = refs[at + 2 * count + 1 : at + 3 * count + 1]
+    (rows,) = refs[at + 3 * count + 1 :]
     for table, t in zip(tables, turned):
         t[...] = keys(table).T
-    for s in sums:
-        s[...] = jnp.zeros_like(s)
-    for i in range(HEADS):
-        dq = 0.0 if first else dq_in[span(i), :]
-        for table, alpha, w, kt, s in zip(tables, alphas, weights, turned, sums):
-            da = (dout[span(i), :].astype(F32) * alpha[i]).astype(BF16)
-            shift = delta[i] * alpha[i]
-            p = w[i]
-            dp = dot_nn(values(table), da)
-            ds = (p.astype(F32) * (dp - shift)).astype(BF16)
-            s[:, HD:] += dot_nt(p, da)
-            s[:, :HD] += dot_nn(ds, q[:, span(i)])
-            dq = dq + dot_nn(kt[...], ds)
+    for i in range(HEADS):
+        rows[wide(i), :] = q[:, span(i)]
+        for table, alpha, w, ds, da in zip(tables, alphas, weights, slopes, scaled):
+            da[:, wide(i)] = (dout[span(i), :].astype(F32) * alpha[i]).astype(BF16)
+            dp = dot_nn(values(table), da[:, wide(i)])
+            p = w[:, wide(i)].astype(F32)
+            ds[:, wide(i)] = (p * (dp - delta[i] * alpha[i])).astype(BF16)
+    for w, ds, da, g in zip(weights, slopes, scaled, grads):
+        low, high = dot_nn(ds[...], rows[...]) * SCALE, dot_nt(w[...], da[...])
+        if len(g) == 2:
+            g[0][...], g[1][...] = low.astype(g[0].dtype), high.astype(g[1].dtype)
+        else:
+            g[0][:, :HD], g[0][:, HD:] = low.astype(g[0].dtype), high.astype(g[0].dtype)
+    for i in range(HEADS):
+        dq = sum(dot_nn(kt[...], ds[:, wide(i)]) for kt, ds in zip(turned, slopes))
+        if not first:
+            dq = dq + dq_in[span(i), :]
         if last:
             dq_ref[:, span(i)] = (dq * SCALE).T.astype(dq_ref.dtype)
         else:
             dq_ref[span(i), :] = dq
-    for s, g in zip(sums, grads):
-        low, high = s[:, :HD] * SCALE, s[:, HD:]
-        if len(g) == 2:
-            g[0][...], g[1][...] = low.astype(g[0].dtype), high.astype(g[1].dtype)
-        else:
-            g[0][:, :HD], g[0][:, HD:] = low.astype(g[0].dtype), high.astype(g[0].dtype)
 
 
 IN_VMEM = pl.BlockSpec(memory_space=pltpu.VMEM)
@@ -200,7 +204,7 @@
 
 
 def weight_shapes(tables):
-    return [pltpu.VMEM((HEADS, t.shape[0], SLOTS), BF16) for (t, *_) in tables]
+    return [pltpu.VMEM((t.shape[0], HEADS * SLOTS), BF16) for (t, *_) in tables]
 
 
 def score_shapes(tables):
@@ -274,14 +278,17 @@
         [q, dout, delta, *alphas, *flat, *weights, *([] if dq is None else [dq])],
         [jax.ShapeDtypeStruct(t.shape, k) for t, k in zip(flat, kinds)]
         + [jax.ShapeDtypeStruct((SLOTS, HEADS * HD), BF16) if last else WIDE],
-        turned_shapes(tables) + [pltpu.VMEM((t[0].shape[0], 2 * HD), F32) for t in tables],
+        turned_shapes(tables)
+        + weight_shapes(tables)
+        + [pltpu.VMEM((HD, HEADS * SLOTS), BF16) for _ in tables]
+        + [pltpu.VMEM((HEADS * SLOTS, HD), BF16)],
         cost(tables, 4),
     )
     return out[:-1], out[-1]
 
 
-def group_shift(dz, dx):
-    return [(z * 4 + x, (z + dz) % 4 * 4 + (x + dx) % 4) for z in range(4) for x in range(4)]
+def group_flip(dz, dx):
+    return [(z * 4 + x, (z ^ dz) * 4 + (x ^ dx)) for z in range(4) for x in range(4)]
 
 
 def tensor_flip(bits):
@@ -295,10 +302,10 @@
     cot = cotangent[0, 0]
 
     def over_z(a, s):
-        return lax.ppermute(a, "group", group_shift(s, 0))
+        return lax.ppermute(a, "group", group_flip(s, 0))
 
     def over_x(a, s):
-        return lax.ppermute(a, "group", group_shift(0, s))
+        return lax.ppermute(a, "group", group_flip(0, s))
 
     def to_core(a):
         return lax.ppermute(a, "tensor", tensor_flip(1))
@@ -313,7 +320,8 @@
     (topc, totalc, accc), cot_late = lax.optimization_barrier((partc, cot))
     partc = (topc, totalc, accc)
     chunk0 = jnp.concatenate([own] + [over_z(own, s) for s in (1, 3, 2)], axis=0)
-    chunk1, chunk3, chunk2 = [over_x(chunk0, s) for s in (1, 3, 2)]
+    chunk1, chunk3 = over_x(chunk0, 1), over_x(chunk0, 3)
+    chunk2 = over_x(chunk1, 3)
 
     me = lax.axis_index("tensor")
 
@@ -325,12 +333,10 @@
     cot_diag = to_core(cot_chip)
     w0, part0 = forward(q, [(chunk0,)], (False,), 0.02)
     part0, cot = lax.optimization_barrier((part0, cot))
-    most = sum(
-        dot_nt(columns(bits), part) for bits, part in ((0, cot), (1, cot_core), (2, cot_chip))
-    )
-    most, chunk1 = lax.optimization_barrier((most, chunk1))
+    half = dot_nt(columns(0), cot) + dot_nt(columns(1), cot_core)
+    half, chunk1, chunk3 = lax.optimization_barrier((half, chunk1, chunk3))
     w13, part13 = forward(q, [(chunk1,), (chunk3,)], (False, False))
-    dout = (most + dot_nt(columns(3), cot_diag)).astype(BF16)
+    dout = (half + dot_nt(columns(2), cot_chip) + dot_nt(columns(3), cot_diag)).astype(BF16)
     w2, (alphac, alpha0, alpha13, alpha2), delta, mixed = forward_merge(
         lengths, q, dout, [(chunk2,)], [partc, part0, part13]
     )
@@ -355,23 +361,24 @@
         q, dout, delta, [alpha0, alphac], [(chunk0,), comp], [*w0, *wc], F32, dq, True
     )
 
-    back2, far = lax.optimization_barrier((over_x(g2, -2), far))
-    back1, back3 = over_x(g1, -1), over_x(g3, -3)
+    back2, far = lax.optimization_barrier((over_x(g2, 2), far))
+    back1, back3 = over_x(g1, 1), over_x(g3, 3)
     rows = g0 + back2.astype(F32) + back1.astype(F32) + back3.astype(F32)
     n = own.shape[0]
     sent = rows.astype(BF16)
-    total = rows[:n]
+    shares = [rows[:n]]
     for i, s in enumerate((1, 3, 2)):
-        total = total + over_z(sent[(i + 1) * n : (i + 2) * n], -s).astype(F32)
-    total = total.astype(BF16)
+        shares.append(over_z(sent[(i + 1) * n : (i + 2) * n], s).astype(F32))
+    key_grad = sum(x[:, :HD] for x in shares).astype(BF16)
+    value_grad = sum(x[:, HD:] for x in shares).astype(BF16)
     output = (pair_mine + far.astype(F32)).astype(BF16)
     return (
         output[None, None],
         dq[None, None],
         gck[None, None],
         gcv[None, None],
-        total[None, :, :HD],
-        total[None, :, HD:],
+        key_grad[None],
+        value_grad[None],
     )
 
 

time: 75.5 us -> 73.1 us (0.968)
  starting transfers between devices: 26.5 us -> 24.8 us
  Pallas kernels: 20.8 us -> 19.7 us
    ppermute x12, waiting for transfers between devices: 9.9 us -> 14.9 us  [the longest x6 8.29 us: over_x(): return lax.ppermute(a, 'group', group_flip(0, s))]
    ppermute x2, waiting for transfers between devices: 6.32 us -> 1.47 us  [to_chip(): return lax.ppermute(a, 'tensor', tensor_flip(2))]
    pallas_call x7, Pallas kernels: 20.8 us -> 19.7 us  [call(): pl.pallas_call(kernel, in_specs=specs or [IN_VMEM] * len(operands), out_s...]
    ppermute x12, starting transfers between devices: 24.2 us -> 23.2 us  [the longest x6 15.3 us: over_z(): return lax.ppermute(a, 'group', group_flip(s, 0))]
  transfers between devices with their start and end apart: 17 -> 17, of which waited for: 8 -> 11; matrix products, arithmetic and copies ran while one was open for 7% -> 8% of each run, Pallas kernels for 25% -> 24%
where the time goes in v4:
time: 73.1 us; the launch traced here: 72.8 us
  starting transfers between devices  24.8 us (34%)
  Pallas kernels  19.7 us (27%)
  waiting for transfers between devices  16.8 us (23%)
  matrix products  7.8 us (11%)
  other arithmetic  1.68 us (2%)
  between operations  1.5 us (2%)
    pallas_call x7, Pallas kernels, call(): pl.pallas_call(kernel, in_specs=specs or [IN_VMEM] * len(operands), out_s...  19.7 us
    ppermute x6, starting transfers between devices, over_z(): return lax.ppermute(a, 'group', group_flip(s, 0))  15.3 us
    ppermute x6, waiting for transfers between devices, over_x(): return lax.ppermute(a, 'group', group_flip(0, s))  8.29 us
    ppermute x6, starting transfers between devices, over_x(): return lax.ppermute(a, 'group', group_flip(0, s))  7.9 us
    ppermute x6, waiting for transfers between devices, over_z(): return lax.ppermute(a, 'group', group_flip(s, 0))  6.57 us
    dot_general x4, matrix products, dot_nt(): lax.dot_general(a, b, (((1,), (1,)), ((), ())), preferred_element_type=F32)  4.04 us
    dot_general x4, matrix products, partial_out(): lax.dot_general(mixed, columns(bits), (((0,), (0,)), ((), ())), preferred...  3.76 us
    ppermute x2, starting transfers between devices, to_chip(): return lax.ppermute(a, 'tensor', tensor_flip(2))  1.48 us
  transfers between devices with their start and end apart: 17, of which 11 were waited for; matrix products, arithmetic and copies ran while one was open for 8% of the time, Pallas kernels for 24%

profile of v4, /device:TPU:8, one launch (start us, length us, event | category | flops | bytes accessed | tf_op | source)
XLA Modules:
  0.0 72.8 jit_solution(8484680240639786741)
XLA Ops:
  0.6 0.8 %pad_maximum_fusion.1 = bf16[128,256]{1,0:T(8,128)(2,1)S(1)} fusion(bf16[128,128]{1,0:T(8,128)(2,1)} %bitcast.31, bf16[128,128]{1,0:T(8,128)(2,1)} %bitcast.32), kind=kLoop, calls=%fused_computation.41 | loop fusion | flops 131072 | bytes 131072 | tf_op jit(solution)/shard_map/concatenate | solution.py:316
  1.4 7.3 %collective-permute-start.2 = (bf16[128,256]{1,0:T(8,128)(2,1)S(1)}, bf16[128,256]{1,0:T(8,128)(2,1)S(1)}, u32[]{:S(2)}, u32[]{:S(2)}) collective-permute-start(bf16[128,256]{1,0:T(8,128)(2,1)S(1)} %pad_maximum_fusion.1), channel_id=1, source_target_pairs={{0,32},{4,36},{8,40},{12,44},{16,48},{20,52},{24,56},{28,60},{32,0... | collective-permute-start | bytes 196616 | tf_op jit(solution)/shard_map/ppermute | solution.py:305
  8.7 0.0 collective-permute-start.1
  8.7 1.5 %collective-permute-start = (bf16[128,256]{1,0:T(8,128)(2,1)S(1)}, bf16[128,256]{1,0:T(8,128)(2,1)S(1)}, u32[]{:S(2)}, u32[]{:S(2)}) collective-permute-start(bf16[128,256]{1,0:T(8,128)(2,1)S(1)} %pad_maximum_fusion.1), channel_id=1, source_target_pairs={{0,16},{4,20},{8,24},{12,28},{16,0},{20,4},{24,8},{28,12},{32,48},... | collective-permute-start | bytes 196616 | tf_op jit(solution)/shard_map/ppermute | solution.py:305
  10.2 0.0 collective-permute-start.3
  10.2 2.0 %forward_first.1 = (bf16[256,2048]{1,0:T(8,128)(2,1)S(1)}, f32[8,1,256]{2,1,0:T(1,128)S(1)}, f32[8,1,256]{2,1,0:T(1,128)S(1)}, f32[1024,256]{1,0:T(8,128)S(1)}, ...) custom-call(bf16[256,1024]{1,0:T(8,128)(2,1)} %bitcast.25, ...), custom_call_target="tpu_custom_call" | custom-call | flops 8388608 | bytes 32768 | tf_op jit(solution)/shard_map/forward_first/pallas_call | solution.py:194
  12.2 1.1 %collective-permute-start.6 = (bf16[256,1024]{1,0:T(8,128)(2,1)}, bf16[256,1024]{1,0:T(8,128)(2,1)}, u32[]{:S(2)}, u32[]{:S(2)}) collective-permute-start(bf16[256,1024]{1,0:T(8,128)(2,1)} %bitcast.27), channel_id=1, source_target_pairs={{0,2},{1,3},{2,0},{3,1},{4,6},{5,7},{6,4},{7,5},{8,10},{9,11},{10,... | collective-permute-start | bytes 1572872 | tf_op jit(solution)/shard_map/ppermute | solution.py:314
  14.0 0.0 slice-start
  14.0 1.7 %collective-permute-done = bf16[128,256]{1,0:T(8,128)(2,1)S(1)} collective-permute-done((bf16[128,256]{1,0:T(8,128)(2,1)S(1)}, bf16[128,256]{1,0:T(8,128)(2,1)S(1)}, u32[]{:S(2)}, u32[]{:S(2)}) %collective-permute-start) | collective-permute-done | bytes 65568 | tf_op jit(solution)/shard_map/ppermute | solution.py:305
  15.7 0.1 collective-permute-done.1
  15.8 0.0 collective-permute-done.2
  15.8 2.8 %collective-permute-start.5 = (bf16[512,256]{1,0:T(8,128)(2,1)S(1)}, bf16[512,256]{1,0:T(8,128)(2,1)S(1)}, u32[]{:S(2)}, u32[]{:S(2)}) collective-permute-start(bf16[512,256]{1,0:T(8,128)(2,1)S(1)} %constant_dynamic-update-slice_fusion.refs_1_.refs_5_), channel_id=1, source_target_pairs={{0,12},{4,8},{8,4},{12,0},{16,28},{20,24},{24,20},{28,16},{32,44},... | collective-permute-start | bytes 786440 | tf_op jit(solution)/shard_map/ppermute | solution.py:308
  18.6 0.2 collective-permute-start.4
  18.9 0.0 slice-start.1
  18.9 0.0 copy-start
  18.9 1.8 %forward.2 = (bf16[512,2048]{1,0:T(8,128)(2,1)S(1)}, f32[8,1,256]{2,1,0:T(1,128)S(1)}, f32[8,1,256]{2,1,0:T(1,128)S(1)}, f32[1024,256]{1,0:T(8,128)S(1)}) custom-call(bf16[256,1024]{1,0:T(8,128)(2,1)S(1)} %get-tuple-element.58.refs_0_.refs_1_, bf16[512,256]{1,0:T(8,128)(2,1)S(1)} %constant_dynamic-update-slice_fusion.refs_1_.refs_5_), custom_call_target="tpu_custom_call" | custom-call | flops 13421772800 | bytes 65536 | tf_op jit(solution)/shard_map/forward/pallas_call | solution.py:194
  20.7 0.0 slice-done
  20.7 0.3 slice-done.1
  21.1 0.1 copy-done
  21.2 0.7 %fusion.14 = f32[1024,256]{1,0:T(8,128)S(1)} fusion(bf16[256,1024]{1,0:T(8,128)(2,1)S(1)} %bitcast.28, bf16[1024,4096]{1,0:T(8,128)(2,1)S(1)} %bitcast.24, s32[]{:T(128)S(6)} %select_n.16), kind=kOutput, calls=%fused_computation.14 | convolution fusion | flops 536870912 | bytes 3670020 | tf_op jit(solution)/shard_map/dot_general | solution.py:26
  21.9 4.5 %collective-permute-done.4.refs_1_.refs_5_ = bf16[512,256]{1,0:T(8,128)(2,1)S(1)} collective-permute-done((bf16[512,256]{1,0:T(8,128)(2,1)S(1)}, bf16[512,256]{1,0:T(8,128)(2,1)S(1)}, u32[]{:S(2)}, u32[]{:S(2)}) %collective-permute-start.4) | collective-permute-done | bytes 262176 | tf_op jit(solution)/shard_map/ppermute | solution.py:308
  26.4 0.5 collective-permute-start.8
  26.9 0.2 collective-permute-done.6
  27.1 0.0 collective-permute-start.7
  27.1 0.0 collective-permute-done.3
  27.1 0.8 %fusion.16 = f32[1024,256]{1,0:T(8,128)S(1)} fusion(f32[1024,256]{1,0:T(8,128)S(1)} %fusion.14, bf16[256,1024]{1,0:T(8,128)(2,1)S(1)} %collective-permute-done.3, bf16[1024,4096]{1,0:T(8,128)(2,1)S(1)} %bitcast.24, s32[]{:T(128)S(6)} %select_n.17), kind=kOutput, calls=%fused_computation.16 | convolution fusion | flops 537133056 | bytes 4718596 | tf_op jit(solution)/shard_map/dot_general | solution.py:26
  27.9 0.0 collective-permute-done.5.refs_2_.refs_6_
  27.9 3.5 %forward.3 = (bf16[512,2048]{1,0:T(8,128)(2,1)S(1)}, bf16[512,2048]{1,0:T(8,128)(2,1)S(1)}, f32[8,1,256]{2,1,0:T(1,128)S(1)}, f32[8,1,256]{2,1,0:T(1,128)S(1)}, f32[1024,256]{1,0:T(8,128)S(1)}) custom-call(bf16[256,1024]{1,0:T(8,128)(2,1)S(1)} %get-tuple-element.58.refs_0_.refs_1_, bf16[512,256]{1,0:T(8,128)(2,1)S(1)} %collective-permute-done.4.refs_1_.refs_5_, ...), custom_call_target="tpu_custom_call" | custom-call | flops 33554432 | bytes 131072 | tf_op jit(solution)/shard_map/forward/pallas_call | solution.py:194
  31.4 1.8 %fusion.6 = f32[1024,256]{1,0:T(8,128)S(1)} fusion(bf16[256,1024]{1,0:T(8,128)(2,1)} %collective-permute-done.6, bf16[1024,4096]{1,0:T(8,128)(2,1)S(1)} %bitcast.24, s32[]{:T(128)S(6)} %select_n.18), kind=kOutput, calls=%fused_computation.6 | convolution fusion | flops 536870912 | bytes 3670020 | tf_op jit(solution)/shard_map/dot_general | solution.py:26
  33.2 0.0 collective-permute-done.7
  33.2 0.7 %fusion.22.refs_2_.refs_1_ = bf16[1024,256]{1,0:T(8,128)(2,1)S(1)} fusion(bf16[256,1024]{1,0:T(8,128)(2,1)S(1)} %collective-permute-done.7, bf16[1024,4096]{1,0:T(8,128)(2,1)S(1)} %bitcast.24, s32[]{:T(128)S(6)} %select_n.19, f32[1024,256]{1,0:T(8,128)S(1)} %fusion.16, f32[1024,256]{1,0:T(8,128)S(1)} %fusion.6), kind=kOutput, calls=%fused_computation.18 | convolution fusion | flops 537657344 | bytes 5242884 | tf_op jit(solution)/shard_map/dot_general | solution.py:26
  33.9 0.7 %collective-permute-done.8.refs_3_.refs_4_ = bf16[512,256]{1,0:T(8,128)(2,1)S(1)} collective-permute-done((bf16[512,256]{1,0:T(8,128)(2,1)S(1)}, bf16[512,256]{1,0:T(8,128)(2,1)S(1)}, u32[]{:S(2)}, u32[]{:S(2)}) %collective-permute-start.8) | collective-permute-done | bytes 262176 | tf_op jit(solution)/shard_map/ppermute | solution.py:308
  34.7 2.2 %forward_merge.1 = (bf16[512,2048]{1,0:T(8,128)(2,1)S(1)}, f32[8,1,256]{2,1,0:T(1,128)S(1)}, f32[8,1,256]{2,1,0:T(1,128)S(1)}, f32[8,1,256]{2,1,0:T(1,128)S(1)},...) custom-call(s32[1,1]{1,0:T(1,128)S(6)} %copy.17.refs_0_, ...), custom_call_target="tpu_custom_call" | custom-call | flops 16777216 | bytes 65536 | tf_op jit(solution)/shard_map/forward_merge/pallas_call | solution.py:194
  36.9 0.7 %fusion.34 = bf16[256,1024]{1,0:T(8,128)(2,1)S(1)} fusion(bf16[1024,256]{1,0:T(8,128)(2,1)S(1)} %get-tuple-element.80, bf16[1024,4096]{1,0:T(8,128)(2,1)S(1)} %bitcast.24, s32[]{:T(128)S(6)} %select_n.19), kind=kOutput, calls=%fused_computation.22 | convolution fusion | flops 537133056 | bytes 3145732 | tf_op jit(solution)/shard_map/dot_general | solution.py:346
  37.6 0.7 %fusion.28 = bf16[256,1024]{1,0:T(8,128)(2,1)S(1)} fusion(bf16[1024,256]{1,0:T(8,128)(2,1)S(1)} %get-tuple-element.80, bf16[1024,4096]{1,0:T(8,128)(2,1)S(1)} %bitcast.24, s32[]{:T(128)S(6)} %select_n.17), kind=kOutput, calls=%fused_computation.20 | convolution fusion | flops 537133056 | bytes 3145732 | tf_op jit(solution)/shard_map/dot_general | solution.py:346
  38.4 0.1 pad_maximum_fusion
  38.5 0.1 collective-permute-start.9
  38.6 2.1 %backward.3 = (bf16[512,256]{1,0:T(8,128)(2,1)S(1)}, f32[1024,256]{1,0:T(8,128)S(1)}) custom-call(bf16[256,1024]{1,0:T(8,128)(2,1)S(1)} %get-tuple-element.58.refs_0_.refs_1_, bf16[1024,256]{1,0:T(8,128)(2,1)S(1)} %fusion.22.refs_2_.refs_1_, f32[8,1,256]{2,1,0:T(1,128)S(1)} %get-tuple-element.81.refs_2_, f32[8,1,256]{2,1,0:T(1,128)S(1)} %get-tuple-element.82.refs_3_, ...), custom_call_target="tpu_custom_call" | custom-call | flops 33554432 | bytes 65536 | tf_op jit(solution)/shard_map/backward/pallas_call | solution.py:194
  40.7 0.5 collective-permute-done.9
  41.2 0.7 %fusion.43 = bf16[256,1024]{1,0:T(8,128)(2,1)S(1)} fusion(bf16[1024,256]{1,0:T(8,128)(2,1)S(1)} %get-tuple-element.80, bf16[1024,4096]{1,0:T(8,128)(2,1)S(1)} %bitcast.24, s32[]{:T(128)S(6)} %select_n.18, bf16[512,1024]{1,0:T(8,128)(2,1)S(1)} %collective-permute-done.9), kind=kOutput, calls=%fused_computation.25 | convolution fusion | flops 538181632 | bytes 3670020 | tf_op jit(solution)/shard_map/dot_general | solution.py:346
  41.9 0.4 collective-permute-start.11
  42.3 3.0 %collective-permute-start.10 = (bf16[512,256]{1,0:T(8,128)(2,1)S(1)}, bf16[512,256]{1,0:T(8,128)(2,1)S(1)}, u32[]{:S(2)}, u32[]{:S(2)}) collective-permute-start(bf16[512,256]{1,0:T(8,128)(2,1)S(1)} %get-tuple-element.86), channel_id=1, source_target_pairs={{0,8},{4,12},{8,0},{12,4},{16,24},{20,28},{24,16},{28,20},{32,40},... | collective-permute-start | bytes 786440 | tf_op jit(solution)/shard_map/ppermute | solution.py:308
  45.3 4.1 %backward.4 = (bf16[512,256]{1,0:T(8,128)(2,1)S(1)}, bf16[512,256]{1,0:T(8,128)(2,1)S(1)}, f32[1024,256]{1,0:T(8,128)S(1)}) custom-call(bf16[256,1024]{1,0:T(8,128)(2,1)S(1)} %get-tuple-element.58.refs_0_.refs_1_, bf16[1024,256]{1,0:T(8,128)(2,1)S(1)} %fusion.22.refs_2_.refs_1_, f32[8,1,256]{2,1,0:T(1,128)S(1)} %get-tuple-element.81.refs_2_, ...), custom_call_target="tpu_custom_call" | custom-call | flops 67108864 | bytes 131072 | tf_op jit(solution)/shard_map/backward/pallas_call | solution.py:194
  49.4 0.7 collective-permute-start.12
  50.1 0.7 collective-permute-start.13
  50.7 4.0 %backward.5 = (f32[512,256]{1,0:T(8,128)S(1)}, bf16[256,128]{1,0:T(8,128)(2,1)}, bf16[256,128]{1,0:T(8,128)(2,1)}, bf16[256,1024]{1,0:T(8,128)(2,1)}) custom-call(bf16[256,1024]{1,0:T(8,128)(2,1)S(1)} %get-tuple-element.58.refs_0_.refs_1_, bf16[1024,256]{1,0:T(8,128)(2,1)S(1)} %fusion.22.refs_2_.refs_1_, f32[8,1,256]{2,1,0:T(1,128)S(1)} %get-tuple-element.81.refs_2_, ...), custom_call_target="tpu_custom_call" | custom-call | flops 50331648 | bytes 98304 | tf_op jit(solution)/shard_map/backward/pallas_call | solution.py:194
  54.7 0.0 collective-permute-done.10
  54.7 1.3 %collective-permute-done.11 = bf16[256,1024]{1,0:T(8,128)(2,1)S(1)} collective-permute-done((bf16[256,1024]{1,0:T(8,128)(2,1)S(1)}, bf16[256,1024]{1,0:T(8,128)(2,1)S(1)}, u32[]{:S(2)}, u32[]{:S(2)}) %collective-permute-start.11) | collective-permute-done | bytes 524320 | tf_op jit(solution)/shard_map/ppermute | solution.py:314
  56.0 1.8 %collective-permute-done.12 = bf16[512,256]{1,0:T(8,128)(2,1)S(1)} collective-permute-done((bf16[512,256]{1,0:T(8,128)(2,1)S(1)}, bf16[512,256]{1,0:T(8,128)(2,1)S(1)}, u32[]{:S(2)}, u32[]{:S(2)}) %collective-permute-start.12) | collective-permute-done | bytes 262176 | tf_op jit(solution)/shard_map/ppermute | solution.py:308
  57.8 1.2 %collective-permute-done.13 = bf16[512,256]{1,0:T(8,128)(2,1)S(1)} collective-permute-done((bf16[512,256]{1,0:T(8,128)(2,1)S(1)}, bf16[512,256]{1,0:T(8,128)(2,1)S(1)}, u32[]{:S(2)}, u32[]{:S(2)}) %collective-permute-start.13) | collective-permute-done | bytes 262176 | tf_op jit(solution)/shard_map/ppermute | solution.py:308
  59.0 0.1 fusion.73
  59.2 2.1 %collective-permute-start.14 = (bf16[128,256]{1,0:T(8,128)(2,1)S(1)}, bf16[128,256]{1,0:T(8,128)(2,1)S(1)}, u32[]{:S(2)}, u32[]{:S(2)}) collective-permute-start(bf16[128,256]{1,0:T(8,128)(2,1)S(1)} %get-tuple-element.112), channel_id=1, source_target_pairs={{0,16},{4,20},{8,24},{12,28},{16,0},{20,4},{24,8},{28,12},{32,48},... | collective-permute-start | bytes 196616 | tf_op jit(solution)/shard_map/ppermute | solution.py:305
  61.3 4.5 %collective-permute-start.16 = (bf16[128,256]{1,0:T(8,128)(2,1)S(1)}, bf16[128,256]{1,0:T(8,128)(2,1)S(1)}, u32[]{:S(2)}, u32[]{:S(2)}) collective-permute-start(bf16[128,256]{1,0:T(8,128)(2,1)S(1)} %get-tuple-element.113), channel_id=1, source_target_pairs={{0,32},{4,36},{8,40},{12,44},{16,48},{20,52},{24,56},{28,60},{32,0... | collective-permute-start | bytes 196616 | tf_op jit(solution)/shard_map/ppermute | solution.py:305
  65.8 0.0 collective-permute-start.15
  65.8 1.6 %fusion.58 = bf16[1,1,256,1024]{3,2,1,0:T(8,128)(2,1)} fusion(bf16[1024,256]{1,0:T(8,128)(2,1)S(1)} %get-tuple-element.80, bf16[1024,4096]{1,0:T(8,128)(2,1)S(1)} %bitcast.24, s32[]{:T(128)S(6)} %select_n.16, bf16[256,1024]{1,0:T(8,128)(2,1)S(1)} %collective-permute-done.11, bf16[512,1024]{1,0:T(8,128)(2,1)S(1)} %collective-permute-done.9), kind=kOutput, calls=%fused_computation.30 | convolution fusion | flops 538705920 | bytes 4194308 | tf_op jit(solution)/shard_map/dot_general | solution.py:346
  67.3 0.0 collective-permute-done.14
  67.3 3.3 %collective-permute-done.16 = bf16[128,256]{1,0:T(8,128)(2,1)S(1)} collective-permute-done((bf16[128,256]{1,0:T(8,128)(2,1)S(1)}, bf16[128,256]{1,0:T(8,128)(2,1)S(1)}, u32[]{:S(2)}, u32[]{:S(2)}) %collective-permute-start.16) | collective-permute-done | bytes 65568 | tf_op jit(solution)/shard_map/ppermute | solution.py:305
  70.6 1.5 %collective-permute-done.15 = bf16[128,256]{1,0:T(8,128)(2,1)S(1)} collective-permute-done((bf16[128,256]{1,0:T(8,128)(2,1)S(1)}, bf16[128,256]{1,0:T(8,128)(2,1)S(1)}, u32[]{:S(2)}, u32[]{:S(2)}) %collective-permute-start.15) | collective-permute-done | bytes 65568 | tf_op jit(solution)/shard_map/ppermute | solution.py:305
  72.2 0.7 fusion.64
  (9 shorter events, 0.1 us)
Async XLA Ops:
  1.4 14.4 %collective-permute-start.2 = (bf16[128,256]{1,0:T(8,128)(2,1)S(1)}, bf16[128,256]{1,0:T(8,128)(2,1)S(1)}, u32[]{:S(2)}, u32[]{:S(2)}) collective-permute-start(bf16[128,256]{1,0:T(8,128)(2,1)S(1)} %pad_maximum_fusion.1), channel_id=1, source_target_pairs={{0,32},{4,36},{8,40},{12,44},{16,48},{20,52},{24,56},{28,60},{32,0... | collective-permute-start | bytes 196616 | tf_op jit(solution)/shard_map/ppermute | solution.py:305
  8.7 7.1 %collective-permute-start.1 = (bf16[128,256]{1,0:T(8,128)(2,1)S(1)}, bf16[128,256]{1,0:T(8,128)(2,1)S(1)}, u32[]{:S(2)}, u32[]{:S(2)}) collective-permute-start(bf16[128,256]{1,0:T(8,128)(2,1)S(1)} %pad_maximum_fusion.1), channel_id=1, source_target_pairs={{0,48},{4,52},{8,56},{12,60},{16,32},{20,36},{24,40},{28,44},{32,1... | collective-permute-start | bytes 196616 | tf_op jit(solution)/shard_map/ppermute | solution.py:305
  8.7 7.0 %collective-permute-start = (bf16[128,256]{1,0:T(8,128)(2,1)S(1)}, bf16[128,256]{1,0:T(8,128)(2,1)S(1)}, u32[]{:S(2)}, u32[]{:S(2)}) collective-permute-start(bf16[128,256]{1,0:T(8,128)(2,1)S(1)} %pad_maximum_fusion.1), channel_id=1, source_target_pairs={{0,16},{4,20},{8,24},{12,28},{16,0},{20,4},{24,8},{28,12},{32,48},... | collective-permute-start | bytes 196616 | tf_op jit(solution)/shard_map/ppermute | solution.py:305
  10.2 17.0 %collective-permute-start.3 = (bf16[256,1024]{1,0:T(8,128)(2,1)}, bf16[256,1024]{1,0:T(8,128)(2,1)S(1)}, u32[]{:S(2)}, u32[]{:S(2)}) collective-permute-start(bf16[256,1024]{1,0:T(8,128)(2,1)} %bitcast.26), channel_id=1, source_target_pairs={{0,1},{1,0},{2,3},{3,2},{4,5},{5,4},{6,7},{7,6},{8,9},{9,8},{10,11... | collective-permute-start | bytes 1572872 | tf_op jit(solution)/shard_map/ppermute | solution.py:311
  12.2 14.9 %collective-permute-start.6 = (bf16[256,1024]{1,0:T(8,128)(2,1)}, bf16[256,1024]{1,0:T(8,128)(2,1)}, u32[]{:S(2)}, u32[]{:S(2)}) collective-permute-start(bf16[256,1024]{1,0:T(8,128)(2,1)} %bitcast.27), channel_id=1, source_target_pairs={{0,2},{1,3},{2,0},{3,1},{4,6},{5,7},{6,4},{7,5},{8,10},{9,11},{10,... | collective-permute-start | bytes 1572872 | tf_op jit(solution)/shard_map/ppermute | solution.py:314
  14.0 6.8 %slice-start = ((s8[8388608]{0:T(1024)(128)(4,1)}), s8[4194304]{0:T(1024)(128)(4,1)S(1)}, s32[]{:S(2)}) async-start(s8[8388608]{0:T(1024)(128)(4,1)} %bitcast.23), calls=%async_computation | async-start | bytes 8388608
  15.8 12.1 %collective-permute-start.5 = (bf16[512,256]{1,0:T(8,128)(2,1)S(1)}, bf16[512,256]{1,0:T(8,128)(2,1)S(1)}, u32[]{:S(2)}, u32[]{:S(2)}) collective-permute-start(bf16[512,256]{1,0:T(8,128)(2,1)S(1)} %constant_dynamic-update-slice_fusion.refs_1_.refs_5_), channel_id=1, source_target_pairs={{0,12},{4,8},{8,4},{12,0},{16,28},{20,24},{24,20},{28,16},{32,44},... | collective-permute-start | bytes 786440 | tf_op jit(solution)/shard_map/ppermute | solution.py:308
  18.6 7.8 %collective-permute-start.4 = (bf16[512,256]{1,0:T(8,128)(2,1)S(1)}, bf16[512,256]{1,0:T(8,128)(2,1)S(1)}, u32[]{:S(2)}, u32[]{:S(2)}) collective-permute-start(bf16[512,256]{1,0:T(8,128)(2,1)S(1)} %constant_dynamic-update-slice_fusion.refs_1_.refs_5_), channel_id=1, source_target_pairs={{0,4},{4,0},{8,12},{12,8},{16,20},{20,16},{24,28},{28,24},{32,36},... | collective-permute-start | bytes 786440 | tf_op jit(solution)/shard_map/ppermute | solution.py:308
  18.9 2.2 %slice-start.1 = ((s8[8388608]{0:T(1024)(128)(4,1)}), s8[4194304]{0:T(1024)(128)(4,1)S(1)}, s32[]{:S(2)}) async-start(s8[8388608]{0:T(1024)(128)(4,1)} %bitcast.23), calls=%async_computation.1 | async-start | bytes 8388608
  18.9 2.3 %copy-start = (bf16[1,1,256,1024]{3,2,1,0:T(8,128)(2,1)S(1)}, bf16[1,1,256,1024]{3,2,1,0:T(8,128)(2,1)}, u32[]{:S(2)}) copy-start(bf16[1,1,256,1024]{3,2,1,0:T(8,128)(2,1)} %param.14) | copy-start | bytes 1572868
  26.4 8.2 %collective-permute-start.8 = (bf16[512,256]{1,0:T(8,128)(2,1)S(1)}, bf16[512,256]{1,0:T(8,128)(2,1)S(1)}, u32[]{:S(2)}, u32[]{:S(2)}) collective-permute-start(bf16[512,256]{1,0:T(8,128)(2,1)S(1)} %collective-permute-done.4.refs_1_.refs_5_), channel_id=1, source_target_pairs={{0,12},{4,8},{8,4},{12,0},{16,28},{20,24},{24,20},{28,16},{32,44},... | collective-permute-start | bytes 786440 | tf_op jit(solution)/shard_map/ppermute | solution.py:308
  27.1 6.0 %collective-permute-start.7 = (bf16[256,1024]{1,0:T(8,128)(2,1)}, bf16[256,1024]{1,0:T(8,128)(2,1)S(1)}, u32[]{:S(2)}, u32[]{:S(2)}) collective-permute-start(bf16[256,1024]{1,0:T(8,128)(2,1)} %collective-permute-done.6), channel_id=1, source_target_pairs={{0,1},{1,0},{2,3},{3,2},{4,5},{5,4},{6,7},{7,6},{8,9},{9,8},{10,11... | collective-permute-start | bytes 1572872 | tf_op jit(solution)/shard_map/ppermute | solution.py:311
  38.5 2.7 %collective-permute-start.9 = (bf16[512,1024]{1,0:T(8,128)(2,1)S(1)}, bf16[512,1024]{1,0:T(8,128)(2,1)S(1)}, u32[]{:S(2)}, u32[]{:S(2)}) collective-permute-start(bf16[512,1024]{1,0:T(8,128)(2,1)S(1)} %pad_maximum_fusion), channel_id=1, source_target_pairs={{0,1},{1,0},{2,3},{3,2},{4,5},{5,4},{6,7},{7,6},{8,9},{9,8},{10,11... | collective-permute-start | bytes 3145736 | tf_op jit(solution)/shard_map/ppermute | solution.py:311
  41.9 14.1 %collective-permute-start.11 = (bf16[256,1024]{1,0:T(8,128)(2,1)S(1)}, bf16[256,1024]{1,0:T(8,128)(2,1)S(1)}, u32[]{:S(2)}, u32[]{:S(2)}) collective-permute-start(bf16[256,1024]{1,0:T(8,128)(2,1)S(1)} %fusion.43), channel_id=1, source_target_pairs={{0,2},{1,3},{2,0},{3,1},{4,6},{5,7},{6,4},{7,5},{8,10},{9,11},{10,... | collective-permute-start | bytes 1572872 | tf_op jit(solution)/shard_map/ppermute | solution.py:314
  42.3 12.4 %collective-permute-start.10 = (bf16[512,256]{1,0:T(8,128)(2,1)S(1)}, bf16[512,256]{1,0:T(8,128)(2,1)S(1)}, u32[]{:S(2)}, u32[]{:S(2)}) collective-permute-start(bf16[512,256]{1,0:T(8,128)(2,1)S(1)} %get-tuple-element.86), channel_id=1, source_target_pairs={{0,8},{4,12},{8,0},{12,4},{16,24},{20,28},{24,16},{28,20},{32,40},... | collective-permute-start | bytes 786440 | tf_op jit(solution)/shard_map/ppermute | solution.py:308
  49.4 8.4 %collective-permute-start.12 = (bf16[512,256]{1,0:T(8,128)(2,1)S(1)}, bf16[512,256]{1,0:T(8,128)(2,1)S(1)}, u32[]{:S(2)}, u32[]{:S(2)}) collective-permute-start(bf16[512,256]{1,0:T(8,128)(2,1)S(1)} %get-tuple-element.106), channel_id=1, source_target_pairs={{0,4},{4,0},{8,12},{12,8},{16,20},{20,16},{24,28},{28,24},{32,36},... | collective-permute-start | bytes 786440 | tf_op jit(solution)/shard_map/ppermute | solution.py:308
  50.1 8.9 %collective-permute-start.13 = (bf16[512,256]{1,0:T(8,128)(2,1)S(1)}, bf16[512,256]{1,0:T(8,128)(2,1)S(1)}, u32[]{:S(2)}, u32[]{:S(2)}) collective-permute-start(bf16[512,256]{1,0:T(8,128)(2,1)S(1)} %get-tuple-element.107), channel_id=1, source_target_pairs={{0,12},{4,8},{8,4},{12,0},{16,28},{20,24},{24,20},{28,16},{32,44},... | collective-permute-start | bytes 786440 | tf_op jit(solution)/shard_map/ppermute | solution.py:308
  59.2 8.1 %collective-permute-start.14 = (bf16[128,256]{1,0:T(8,128)(2,1)S(1)}, bf16[128,256]{1,0:T(8,128)(2,1)S(1)}, u32[]{:S(2)}, u32[]{:S(2)}) collective-permute-start(bf16[128,256]{1,0:T(8,128)(2,1)S(1)} %get-tuple-element.112), channel_id=1, source_target_pairs={{0,16},{4,20},{8,24},{12,28},{16,0},{20,4},{24,8},{28,12},{32,48},... | collective-permute-start | bytes 196616 | tf_op jit(solution)/shard_map/ppermute | solution.py:305
  61.3 9.4 %collective-permute-start.16 = (bf16[128,256]{1,0:T(8,128)(2,1)S(1)}, bf16[128,256]{1,0:T(8,128)(2,1)S(1)}, u32[]{:S(2)}, u32[]{:S(2)}) collective-permute-start(bf16[128,256]{1,0:T(8,128)(2,1)S(1)} %get-tuple-element.113), channel_id=1, source_target_pairs={{0,32},{4,36},{8,40},{12,44},{16,48},{20,52},{24,56},{28,60},{32,0... | collective-permute-start | bytes 196616 | tf_op jit(solution)/shard_map/ppermute | solution.py:305
  65.8 6.4 %collective-permute-start.15 = (bf16[128,256]{1,0:T(8,128)(2,1)S(1)}, bf16[128,256]{1,0:T(8,128)(2,1)S(1)}, u32[]{:S(2)}, u32[]{:S(2)}) collective-permute-start(bf16[128,256]{1,0:T(8,128)(2,1)S(1)} %get-tuple-element.114), channel_id=1, source_target_pairs={{0,48},{4,52},{8,56},{12,60},{16,32},{20,36},{24,40},{28,44},{32,1... | collective-permute-start | bytes 196616 | tf_op jit(solution)/shard_map/ppermute | solution.py:305

commit v5 on v4

--- a/solution.py
+++ b/solution.py
@@ -15,7 +15,7 @@
 SCALE = HD**-0.5
 F32 = jnp.float32
 BF16 = jnp.bfloat16
-FIRST_VMEM = 56
+FETCH_VMEM = 56
 
 
 def dot_nn(a, b):
@@ -91,11 +91,8 @@
         acc_ref[span(i), :] = mix(i, weights, turned)
 
 
-def first_kernel(*refs):
-    sources = refs[:3]
-    w, top_ref, total_ref, acc_ref = refs[3:7]
-    q, key, value = held = refs[7:10]
-    score, turned, sems = refs[10:]
+def fetch_kernel(*refs):
+    sources, held, sems = refs[:3], refs[3:6], refs[6]
     copies = [
         pltpu.make_async_copy(source, target, sems.at[i])
         for i, (source, target) in enumerate(zip(sources, held))
@@ -104,10 +101,6 @@
         copy.start()
     for copy in copies:
         copy.wait()
-    stats = attend(q, [(key, value)], (True,), [w], [score], [turned])
-    for i in range(HEADS):
-        top_ref[i], total_ref[i] = stats[i]
-        acc_ref[span(i), :] = mix(i, [w], [turned])
 
 
 def merge_kernel(count, earlier, *refs):
@@ -236,21 +229,17 @@
     return out[:n], out[n:]
 
 
-def forward_first(*sources):
-    tables = [sources[1:3]]
-    out = call(
-        first_kernel,
-        "forward_first",
+def fetch(*sources):
+    return call(
+        fetch_kernel,
+        "fetch",
         sources,
-        weight_shapes(tables)
-        + [STAT, STAT, WIDE]
-        + [pltpu.VMEM(x.shape, x.dtype) for x in sources],
-        score_shapes(tables) + turned_shapes(tables) + [pltpu.SemaphoreType.DMA((3,))],
-        cost(tables, 2),
+        [pltpu.VMEM(x.shape, x.dtype) for x in sources],
+        [pltpu.SemaphoreType.DMA((3,))],
+        pl.CostEstimate(flops=10**6, bytes_accessed=10**5, transcendentals=0),
         [pl.BlockSpec(memory_space=pl.ANY)] * 3,
-        pltpu.CompilerParams(vmem_limit_bytes=FIRST_VMEM * 1024 * 1024),
-    )
-    return out[:1], out[1:4], out[4:]
+        pltpu.CompilerParams(vmem_limit_bytes=FETCH_VMEM * 1024 * 1024),
+    )
 
 
 def forward_merge(length, q, dout, tables, old):
@@ -315,10 +304,9 @@
 
     own = jnp.concatenate([prompt_keys[0], prompt_values[0]], axis=1)
     own, comp_k = lax.optimization_barrier((own, comp_keys[0, 0]))
-    wc, partc, (q, comp_k, comp_v) = forward_first(q, comp_k, comp_values[0, 0])
+    q, comp_k, comp_v = fetch(q, comp_k, comp_values[0, 0])
     comp = (comp_k, comp_v)
-    (topc, totalc, accc), cot_late = lax.optimization_barrier((partc, cot))
-    partc = (topc, totalc, accc)
+    q, cot_late = lax.optimization_barrier((q, cot))
     chunk0 = jnp.concatenate([own] + [over_z(own, s) for s in (1, 3, 2)], axis=0)
     chunk1, chunk3 = over_x(chunk0, 1), over_x(chunk0, 3)
     chunk2 = over_x(chunk1, 3)
@@ -331,14 +319,14 @@
     cot_core = to_core(cot)
     cot_chip = to_chip(cot_late)
     cot_diag = to_core(cot_chip)
-    w0, part0 = forward(q, [(chunk0,)], (False,), 0.02)
+    w0, part0 = forward(q, [(chunk0,), comp], (False, True), 0.02)
     part0, cot = lax.optimization_barrier((part0, cot))
     half = dot_nt(columns(0), cot) + dot_nt(columns(1), cot_core)
     half, chunk1, chunk3 = lax.optimization_barrier((half, chunk1, chunk3))
     w13, part13 = forward(q, [(chunk1,), (chunk3,)], (False, False))
     dout = (half + dot_nt(columns(2), cot_chip) + dot_nt(columns(3), cot_diag)).astype(BF16)
-    w2, (alphac, alpha0, alpha13, alpha2), delta, mixed = forward_merge(
-        lengths, q, dout, [(chunk2,)], [partc, part0, part13]
+    w2, (alpha0, alpha13, alpha2), delta, mixed = forward_merge(
+        lengths, q, dout, [(chunk2,)], [part0, part13]
     )
     (g2,), dq = backward(q, dout, delta, [alpha2], [(chunk2,)], w2, BF16, None, False)
 
@@ -358,7 +346,7 @@
         q, dout, delta, [alpha13, alpha13], [(chunk1,), (chunk3,)], w13, BF16, dq, False
     )
     (g0, gck, gcv), dq = backward(
-        q, dout, delta, [alpha0, alphac], [(chunk0,), comp], [*w0, *wc], F32, dq, True
+        q, dout, delta, [alpha0, alpha0], [(chunk0,), comp], w0, F32, dq, True
     )
 
     back2, far = lax.optimization_barrier((over_x(g2, 2), far))

time: 73.1 us -> 70.9 us (0.970)
  matrix products: 7.8 us -> 6.75 us
  waiting for transfers between devices: 16.8 us -> 15.9 us
    dot_general x4, matrix products: 4.04 us -> 2.98 us  [dot_nt(): lax.dot_general(a, b, (((1,), (1,)), ((), ())), preferred_element_type=F32)]
    ppermute x6, waiting for transfers between devices: 8.29 us -> 7.38 us  [over_x(): return lax.ppermute(a, 'group', group_flip(0, s))]
  transfers between devices with their start and end apart: 17 -> 17, of which waited for: 11 -> 11; matrix products, arithmetic and copies ran while one was open for 8% -> 6% of each run, Pallas kernels for 24% -> 24%
where the time goes in v5:
time: 70.9 us; the launch traced here: 70.7 us
  starting transfers between devices  24.7 us (35%)
  Pallas kernels  19.4 us (27%)
  waiting for transfers between devices  15.9 us (22%)
  matrix products  6.75 us (10%)
  other arithmetic  1.71 us (2%)
  between operations  1.49 us (2%)
  local copies, waits for them, and re-layouts  0.9 us (1%)
    pallas_call x7, Pallas kernels, call(): pl.pallas_call(kernel, in_specs=specs or [IN_VMEM] * len(operands), out_s...  19.4 us
    ppermute x6, starting transfers between devices, over_z(): return lax.ppermute(a, 'group', group_flip(s, 0))  15.3 us
    ppermute x6, starting transfers between devices, over_x(): return lax.ppermute(a, 'group', group_flip(0, s))  8.03 us
    ppermute x6, waiting for transfers between devices, over_x(): return lax.ppermute(a, 'group', group_flip(0, s))  7.38 us
    ppermute x6, waiting for transfers between devices, over_z(): return lax.ppermute(a, 'group', group_flip(s, 0))  6.47 us
    dot_general x4, matrix products, partial_out(): lax.dot_general(mixed, columns(bits), (((0,), (0,)), ((), ())), preferred...  3.78 us
    dot_general x4, matrix products, dot_nt(): lax.dot_general(a, b, (((1,), (1,)), ((), ())), preferred_element_type=F32)  2.98 us
    ppermute x2, waiting for transfers between devices, to_chip(): return lax.ppermute(a, 'tensor', tensor_flip(2))  1.5 us
  transfers between devices with their start and end apart: 17, of which 11 were waited for; matrix products, arithmetic and copies ran while one was open for 6% of the time, Pallas kernels for 24%

profile of v5, /device:TPU:8, one launch (start us, length us, event | category | flops | bytes accessed | tf_op | source)
XLA Modules:
  0.0 70.7 jit_solution(6742101315810765588)
XLA Ops:
  0.6 0.8 %pad_maximum_fusion.1 = bf16[128,256]{1,0:T(8,128)(2,1)S(1)} fusion(bf16[128,128]{1,0:T(8,128)(2,1)} %bitcast.29, bf16[128,128]{1,0:T(8,128)(2,1)} %bitcast.30), kind=kLoop, calls=%fused_computation.41 | loop fusion | flops 131072 | bytes 131072 | tf_op jit(solution)/shard_map/concatenate | solution.py:305
  1.4 7.3 %collective-permute-start.2 = (bf16[128,256]{1,0:T(8,128)(2,1)S(1)}, bf16[128,256]{1,0:T(8,128)(2,1)S(1)}, u32[]{:S(2)}, u32[]{:S(2)}) collective-permute-start(bf16[128,256]{1,0:T(8,128)(2,1)S(1)} %pad_maximum_fusion.1), channel_id=1, source_target_pairs={{0,32},{4,36},{8,40},{12,44},{16,48},{20,52},{24,56},{28,60},{32,0... | collective-permute-start | bytes 196616 | tf_op jit(solution)/shard_map/ppermute | solution.py:294
  8.7 0.0 collective-permute-start.1
  8.7 1.5 %collective-permute-start = (bf16[128,256]{1,0:T(8,128)(2,1)S(1)}, bf16[128,256]{1,0:T(8,128)(2,1)S(1)}, u32[]{:S(2)}, u32[]{:S(2)}) collective-permute-start(bf16[128,256]{1,0:T(8,128)(2,1)S(1)} %pad_maximum_fusion.1), channel_id=1, source_target_pairs={{0,16},{4,20},{8,24},{12,28},{16,0},{20,4},{24,8},{28,12},{32,48},... | collective-permute-start | bytes 196616 | tf_op jit(solution)/shard_map/ppermute | solution.py:294
  10.2 0.0 collective-permute-start.3
  10.2 1.1 %fetch.1 = (bf16[256,1024]{1,0:T(8,128)(2,1)S(1)}, bf16[256,128]{1,0:T(8,128)(2,1)S(1)}, bf16[256,128]{1,0:T(8,128)(2,1)S(1)}) custom-call(bf16[256,1024]{1,0:T(8,128)(2,1)} %bitcast.23, bf16[256,128]{1,0:T(8,128)(2,1)} %bitcast.27, bf16[256,128]{1,0:T(8,128)(2,1)} %bitcast.28), custom_call_target="tpu_custom_call" | custom-call | flops 1000000 | bytes 100000 | tf_op jit(solution)/shard_map/fetch/pallas_call | solution.py:187
  11.2 1.1 %collective-permute-start.6 = (bf16[256,1024]{1,0:T(8,128)(2,1)}, bf16[256,1024]{1,0:T(8,128)(2,1)S(1)}, u32[]{:S(2)}, u32[]{:S(2)}) collective-permute-start(bf16[256,1024]{1,0:T(8,128)(2,1)} %bitcast.25), channel_id=1, source_target_pairs={{0,2},{1,3},{2,0},{3,1},{4,6},{5,7},{6,4},{7,5},{8,10},{9,11},{10,... | collective-permute-start | bytes 1572872 | tf_op jit(solution)/shard_map/ppermute | solution.py:303
  13.0 2.7 %collective-permute-done = bf16[128,256]{1,0:T(8,128)(2,1)S(1)} collective-permute-done((bf16[128,256]{1,0:T(8,128)(2,1)S(1)}, bf16[128,256]{1,0:T(8,128)(2,1)S(1)}, u32[]{:S(2)}, u32[]{:S(2)}) %collective-permute-start) | collective-permute-done | bytes 65568 | tf_op jit(solution)/shard_map/ppermute | solution.py:294
  15.7 0.1 collective-permute-done.1
  15.8 0.0 collective-permute-done.2
  15.8 2.8 %collective-permute-start.5 = (bf16[512,256]{1,0:T(8,128)(2,1)S(1)}, bf16[512,256]{1,0:T(8,128)(2,1)S(1)}, u32[]{:S(2)}, u32[]{:S(2)}) collective-permute-start(bf16[512,256]{1,0:T(8,128)(2,1)S(1)} %constant_dynamic-update-slice_fusion.refs_1_.refs_5_), channel_id=1, source_target_pairs={{0,12},{4,8},{8,4},{12,0},{16,28},{20,24},{24,20},{28,16},{32,44},... | collective-permute-start | bytes 786440 | tf_op jit(solution)/shard_map/ppermute | solution.py:297
  18.6 0.2 collective-permute-start.4
  18.9 0.0 copy-start
  18.9 0.0 copy-start.1
  18.9 2.6 %forward.2 = (bf16[512,2048]{1,0:T(8,128)(2,1)S(1)}, bf16[256,2048]{1,0:T(8,128)(2,1)S(1)}, f32[8,1,256]{2,1,0:T(1,128)S(1)}, f32[8,1,256]{2,1,0:T(1,128)S(1)}, f32[1024,256]{1,0:T(8,128)S(1)}) custom-call(bf16[256,1024]{1,0:T(8,128)(2,1)S(1)} %get-tuple-element.53.refs_0_.refs_1_, bf16[512,256]{1,0:T(8,128)(2,1)S(1)} %constant_dynamic-update-slice_fusion.refs_1_.refs_5_, ...), custom_call_target="tpu_custom_call" | custom-call | flops 20132659200 | bytes 98304 | tf_op jit(solution)/shard_map/forward/pallas_call | solution.py:187
  21.4 0.8 %copy-done = bf16[1024,4096]{1,0:T(8,128)(2,1)S(1)} copy-done((bf16[1024,4096]{1,0:T(8,128)(2,1)S(1)}, bf16[1024,4096]{1,0:T(8,128)(2,1)}, u32[]{:S(2)}) %copy-start) | copy-done | bytes 8388632
  22.2 0.0 copy-done.1
  22.3 0.7 %fusion.14 = f32[1024,256]{1,0:T(8,128)S(1)} fusion(bf16[256,1024]{1,0:T(8,128)(2,1)S(1)} %bitcast.26, bf16[1024,4096]{1,0:T(8,128)(2,1)S(1)} %copy-done, s32[]{:T(128)S(6)} %select_n.16), kind=kOutput, calls=%fused_computation.14 | convolution fusion | flops 536870912 | bytes 3670020 | tf_op jit(solution)/shard_map/dot_general | solution.py:26
  23.0 3.4 %collective-permute-done.4.refs_1_.refs_5_ = bf16[512,256]{1,0:T(8,128)(2,1)S(1)} collective-permute-done((bf16[512,256]{1,0:T(8,128)(2,1)S(1)}, bf16[512,256]{1,0:T(8,128)(2,1)S(1)}, u32[]{:S(2)}, u32[]{:S(2)}) %collective-permute-start.4) | collective-permute-done | bytes 262176 | tf_op jit(solution)/shard_map/ppermute | solution.py:297
  26.4 0.5 collective-permute-start.8
  26.9 0.1 collective-permute-done.6
  27.0 0.0 collective-permute-start.7
  27.0 0.0 collective-permute-done.3
  27.0 0.7 %fusion.16 = f32[1024,256]{1,0:T(8,128)S(1)} fusion(f32[1024,256]{1,0:T(8,128)S(1)} %fusion.14, bf16[256,1024]{1,0:T(8,128)(2,1)S(1)} %collective-permute-done.3, bf16[1024,4096]{1,0:T(8,128)(2,1)S(1)} %copy-done, s32[]{:T(128)S(6)} %select_n.17), kind=kOutput, calls=%fused_computation.16 | convolution fusion | flops 537133056 | bytes 4718596 | tf_op jit(solution)/shard_map/dot_general | solution.py:26
  27.8 0.0 collective-permute-done.5.refs_2_.refs_6_
  27.8 3.5 %forward.3 = (bf16[512,2048]{1,0:T(8,128)(2,1)S(1)}, bf16[512,2048]{1,0:T(8,128)(2,1)S(1)}, f32[8,1,256]{2,1,0:T(1,128)S(1)}, f32[8,1,256]{2,1,0:T(1,128)S(1)}, f32[1024,256]{1,0:T(8,128)S(1)}) custom-call(bf16[256,1024]{1,0:T(8,128)(2,1)S(1)} %get-tuple-element.53.refs_0_.refs_1_, bf16[512,256]{1,0:T(8,128)(2,1)S(1)} %collective-permute-done.4.refs_1_.refs_5_, ...), custom_call_target="tpu_custom_call" | custom-call | flops 33554432 | bytes 131072 | tf_op jit(solution)/shard_map/forward/pallas_call | solution.py:187
  31.2 0.7 %fusion.6 = f32[1024,256]{1,0:T(8,128)S(1)} fusion(bf16[256,1024]{1,0:T(8,128)(2,1)S(1)} %collective-permute-done.6, bf16[1024,4096]{1,0:T(8,128)(2,1)S(1)} %copy-done, s32[]{:T(128)S(6)} %select_n.18), kind=kOutput, calls=%fused_computation.6 | convolution fusion | flops 536870912 | bytes 3670020 | tf_op jit(solution)/shard_map/dot_general | solution.py:26
  32.0 0.0 collective-permute-done.7
  32.0 0.7 %fusion.22.refs_2_.refs_1_ = bf16[1024,256]{1,0:T(8,128)(2,1)S(1)} fusion(bf16[256,1024]{1,0:T(8,128)(2,1)S(1)} %collective-permute-done.7, bf16[1024,4096]{1,0:T(8,128)(2,1)S(1)} %copy-done, s32[]{:T(128)S(6)} %select_n.19, f32[1024,256]{1,0:T(8,128)S(1)} %fusion.16, f32[1024,256]{1,0:T(8,128)S(1)} %fusion.6), kind=kOutput, calls=%fused_computation.18 | convolution fusion | flops 537657344 | bytes 5242884 | tf_op jit(solution)/shard_map/dot_general | solution.py:26
  32.8 1.8 %collective-permute-done.8.refs_3_.refs_4_ = bf16[512,256]{1,0:T(8,128)(2,1)S(1)} collective-permute-done((bf16[512,256]{1,0:T(8,128)(2,1)S(1)}, bf16[512,256]{1,0:T(8,128)(2,1)S(1)}, u32[]{:S(2)}, u32[]{:S(2)}) %collective-permute-start.8) | collective-permute-done | bytes 262176 | tf_op jit(solution)/shard_map/ppermute | solution.py:297
  34.6 2.1 %forward_merge.1 = (bf16[512,2048]{1,0:T(8,128)(2,1)S(1)}, f32[8,1,256]{2,1,0:T(1,128)S(1)}, f32[8,1,256]{2,1,0:T(1,128)S(1)}, f32[8,1,256]{2,1,0:T(1,128)S(1)},...) custom-call(s32[1,1]{1,0:T(1,128)S(6)} %copy.17.refs_0_, ...), custom_call_target="tpu_custom_call" | custom-call | flops 16777216 | bytes 65536 | tf_op jit(solution)/shard_map/forward_merge/pallas_call | solution.py:187
  36.7 0.7 %fusion.34 = bf16[256,1024]{1,0:T(8,128)(2,1)S(1)} fusion(bf16[1024,256]{1,0:T(8,128)(2,1)S(1)} %get-tuple-element.71, bf16[1024,4096]{1,0:T(8,128)(2,1)S(1)} %copy-done, s32[]{:T(128)S(6)} %select_n.19), kind=kOutput, calls=%fused_computation.22 | convolution fusion | flops 537133056 | bytes 3145732 | tf_op jit(solution)/shard_map/dot_general | solution.py:334
  37.4 0.7 %fusion.28 = bf16[256,1024]{1,0:T(8,128)(2,1)S(1)} fusion(bf16[1024,256]{1,0:T(8,128)(2,1)S(1)} %get-tuple-element.71, bf16[1024,4096]{1,0:T(8,128)(2,1)S(1)} %copy-done, s32[]{:T(128)S(6)} %select_n.17), kind=kOutput, calls=%fused_computation.20 | convolution fusion | flops 537133056 | bytes 3145732 | tf_op jit(solution)/shard_map/dot_general | solution.py:334
  38.2 0.1 pad_maximum_fusion
  38.3 0.1 collective-permute-start.9
  38.4 2.1 %backward.3 = (bf16[512,256]{1,0:T(8,128)(2,1)S(1)}, f32[1024,256]{1,0:T(8,128)S(1)}) custom-call(bf16[256,1024]{1,0:T(8,128)(2,1)S(1)} %get-tuple-element.53.refs_0_.refs_1_, bf16[1024,256]{1,0:T(8,128)(2,1)S(1)} %fusion.22.refs_2_.refs_1_, f32[8,1,256]{2,1,0:T(1,128)S(1)} %get-tuple-element.72.refs_2_, f32[8,1,256]{2,1,0:T(1,128)S(1)} %get-tuple-element.73.refs_3_, ...), custom_call_target="tpu_custom_call" | custom-call | flops 33554432 | bytes 65536 | tf_op jit(solution)/shard_map/backward/pallas_call | solution.py:187
  40.5 0.5 collective-permute-done.9
  41.0 0.7 %fusion.43 = bf16[256,1024]{1,0:T(8,128)(2,1)S(1)} fusion(bf16[1024,256]{1,0:T(8,128)(2,1)S(1)} %get-tuple-element.71, bf16[1024,4096]{1,0:T(8,128)(2,1)S(1)} %copy-done, s32[]{:T(128)S(6)} %select_n.18, bf16[512,1024]{1,0:T(8,128)(2,1)S(1)} %collective-permute-done.9), kind=kOutput, calls=%fused_computation.25 | convolution fusion | flops 538181632 | bytes 3670020 | tf_op jit(solution)/shard_map/dot_general | solution.py:334
  41.7 0.1 collective-permute-start.11
  41.8 2.0 %collective-permute-start.10 = (bf16[512,256]{1,0:T(8,128)(2,1)S(1)}, bf16[512,256]{1,0:T(8,128)(2,1)S(1)}, u32[]{:S(2)}, u32[]{:S(2)}) collective-permute-start(bf16[512,256]{1,0:T(8,128)(2,1)S(1)} %get-tuple-element.77), channel_id=1, source_target_pairs={{0,8},{4,12},{8,0},{12,4},{16,24},{20,28},{24,16},{28,20},{32,40},... | collective-permute-start | bytes 786440 | tf_op jit(solution)/shard_map/ppermute | solution.py:297
  43.8 4.1 %backward.4 = (bf16[512,256]{1,0:T(8,128)(2,1)S(1)}, bf16[512,256]{1,0:T(8,128)(2,1)S(1)}, f32[1024,256]{1,0:T(8,128)S(1)}) custom-call(bf16[256,1024]{1,0:T(8,128)(2,1)S(1)} %get-tuple-element.53.refs_0_.refs_1_, bf16[1024,256]{1,0:T(8,128)(2,1)S(1)} %fusion.22.refs_2_.refs_1_, f32[8,1,256]{2,1,0:T(1,128)S(1)} %get-tuple-element.72.refs_2_, ...), custom_call_target="tpu_custom_call" | custom-call | flops 67108864 | bytes 131072 | tf_op jit(solution)/shard_map/backward/pallas_call | solution.py:187
  47.9 0.7 collective-permute-start.12
  48.6 1.8 %collective-permute-start.13 = (bf16[512,256]{1,0:T(8,128)(2,1)S(1)}, bf16[512,256]{1,0:T(8,128)(2,1)S(1)}, u32[]{:S(2)}, u32[]{:S(2)}) collective-permute-start(bf16[512,256]{1,0:T(8,128)(2,1)S(1)} %get-tuple-element.95), channel_id=1, source_target_pairs={{0,12},{4,8},{8,4},{12,0},{16,28},{20,24},{24,20},{28,16},{32,44},... | collective-permute-start | bytes 786440 | tf_op jit(solution)/shard_map/ppermute | solution.py:297
  50.4 4.0 %backward.5 = (f32[512,256]{1,0:T(8,128)S(1)}, bf16[256,128]{1,0:T(8,128)(2,1)}, bf16[256,128]{1,0:T(8,128)(2,1)}, bf16[256,1024]{1,0:T(8,128)(2,1)}) custom-call(bf16[256,1024]{1,0:T(8,128)(2,1)S(1)} %get-tuple-element.53.refs_0_.refs_1_, bf16[1024,256]{1,0:T(8,128)(2,1)S(1)} %fusion.22.refs_2_.refs_1_, f32[8,1,256]{2,1,0:T(1,128)S(1)} %get-tuple-element.72.refs_2_, ...), custom_call_target="tpu_custom_call" | custom-call | flops 50331648 | bytes 98304 | tf_op jit(solution)/shard_map/backward/pallas_call | solution.py:187
  54.4 0.0 collective-permute-done.10
  54.4 1.4 %collective-permute-done.11 = bf16[256,1024]{1,0:T(8,128)(2,1)S(1)} collective-permute-done((bf16[256,1024]{1,0:T(8,128)(2,1)S(1)}, bf16[256,1024]{1,0:T(8,128)(2,1)S(1)}, u32[]{:S(2)}, u32[]{:S(2)}) %collective-permute-start.11) | collective-permute-done | bytes 524320 | tf_op jit(solution)/shard_map/ppermute | solution.py:303
  55.8 0.5 collective-permute-done.12
  56.3 1.7 %collective-permute-done.13 = bf16[512,256]{1,0:T(8,128)(2,1)S(1)} collective-permute-done((bf16[512,256]{1,0:T(8,128)(2,1)S(1)}, bf16[512,256]{1,0:T(8,128)(2,1)S(1)}, u32[]{:S(2)}, u32[]{:S(2)}) %collective-permute-start.13) | collective-permute-done | bytes 262176 | tf_op jit(solution)/shard_map/ppermute | solution.py:297
  58.0 0.2 fusion.73
  58.2 1.7 %collective-permute-start.14 = (bf16[128,256]{1,0:T(8,128)(2,1)S(1)}, bf16[128,256]{1,0:T(8,128)(2,1)S(1)}, u32[]{:S(2)}, u32[]{:S(2)}) collective-permute-start(bf16[128,256]{1,0:T(8,128)(2,1)S(1)} %get-tuple-element.100), channel_id=1, source_target_pairs={{0,16},{4,20},{8,24},{12,28},{16,0},{20,4},{24,8},{28,12},{32,48},... | collective-permute-start | bytes 196616 | tf_op jit(solution)/shard_map/ppermute | solution.py:294
  59.8 3.8 %collective-permute-start.16 = (bf16[128,256]{1,0:T(8,128)(2,1)S(1)}, bf16[128,256]{1,0:T(8,128)(2,1)S(1)}, u32[]{:S(2)}, u32[]{:S(2)}) collective-permute-start(bf16[128,256]{1,0:T(8,128)(2,1)S(1)} %get-tuple-element.101), channel_id=1, source_target_pairs={{0,32},{4,36},{8,40},{12,44},{16,48},{20,52},{24,56},{28,60},{32,0... | collective-permute-start | bytes 196616 | tf_op jit(solution)/shard_map/ppermute | solution.py:294
  63.7 1.1 %collective-permute-start.15 = (bf16[128,256]{1,0:T(8,128)(2,1)S(1)}, bf16[128,256]{1,0:T(8,128)(2,1)S(1)}, u32[]{:S(2)}, u32[]{:S(2)}) collective-permute-start(bf16[128,256]{1,0:T(8,128)(2,1)S(1)} %get-tuple-element.102), channel_id=1, source_target_pairs={{0,48},{4,52},{8,56},{12,60},{16,32},{20,36},{24,40},{28,44},{32,1... | collective-permute-start | bytes 196616 | tf_op jit(solution)/shard_map/ppermute | solution.py:294
  64.7 1.6 %fusion.58 = bf16[1,1,256,1024]{3,2,1,0:T(8,128)(2,1)} fusion(bf16[1024,256]{1,0:T(8,128)(2,1)S(1)} %get-tuple-element.71, bf16[1024,4096]{1,0:T(8,128)(2,1)S(1)} %copy-done, s32[]{:T(128)S(6)} %select_n.16, bf16[256,1024]{1,0:T(8,128)(2,1)S(1)} %collective-permute-done.11, bf16[512,1024]{1,0:T(8,128)(2,1)S(1)} %collective-permute-done.9), kind=kOutput, calls=%fused_computation.30 | convolution fusion | flops 538705920 | bytes 4194308 | tf_op jit(solution)/shard_map/dot_general | solution.py:334
  66.3 0.0 collective-permute-done.14
  66.3 2.4 %collective-permute-done.16 = bf16[128,256]{1,0:T(8,128)(2,1)S(1)} collective-permute-done((bf16[128,256]{1,0:T(8,128)(2,1)S(1)}, bf16[128,256]{1,0:T(8,128)(2,1)S(1)}, u32[]{:S(2)}, u32[]{:S(2)}) %collective-permute-start.16) | collective-permute-done | bytes 65568 | tf_op jit(solution)/shard_map/ppermute | solution.py:294
  68.8 1.3 %collective-permute-done.15 = bf16[128,256]{1,0:T(8,128)(2,1)S(1)} collective-permute-done((bf16[128,256]{1,0:T(8,128)(2,1)S(1)}, bf16[128,256]{1,0:T(8,128)(2,1)S(1)}, u32[]{:S(2)}, u32[]{:S(2)}) %collective-permute-start.15) | collective-permute-done | bytes 65568 | tf_op jit(solution)/shard_map/ppermute | solution.py:294
  70.1 0.7 fusion.64
  (8 shorter events, 0.1 us)
Async XLA Ops:
  1.4 14.4 %collective-permute-start.2 = (bf16[128,256]{1,0:T(8,128)(2,1)S(1)}, bf16[128,256]{1,0:T(8,128)(2,1)S(1)}, u32[]{:S(2)}, u32[]{:S(2)}) collective-permute-start(bf16[128,256]{1,0:T(8,128)(2,1)S(1)} %pad_maximum_fusion.1), channel_id=1, source_target_pairs={{0,32},{4,36},{8,40},{12,44},{16,48},{20,52},{24,56},{28,60},{32,0... | collective-permute-start | bytes 196616 | tf_op jit(solution)/shard_map/ppermute | solution.py:294
  8.7 7.1 %collective-permute-start.1 = (bf16[128,256]{1,0:T(8,128)(2,1)S(1)}, bf16[128,256]{1,0:T(8,128)(2,1)S(1)}, u32[]{:S(2)}, u32[]{:S(2)}) collective-permute-start(bf16[128,256]{1,0:T(8,128)(2,1)S(1)} %pad_maximum_fusion.1), channel_id=1, source_target_pairs={{0,48},{4,52},{8,56},{12,60},{16,32},{20,36},{24,40},{28,44},{32,1... | collective-permute-start | bytes 196616 | tf_op jit(solution)/shard_map/ppermute | solution.py:294
  8.7 7.0 %collective-permute-start = (bf16[128,256]{1,0:T(8,128)(2,1)S(1)}, bf16[128,256]{1,0:T(8,128)(2,1)S(1)}, u32[]{:S(2)}, u32[]{:S(2)}) collective-permute-start(bf16[128,256]{1,0:T(8,128)(2,1)S(1)} %pad_maximum_fusion.1), channel_id=1, source_target_pairs={{0,16},{4,20},{8,24},{12,28},{16,0},{20,4},{24,8},{28,12},{32,48},... | collective-permute-start | bytes 196616 | tf_op jit(solution)/shard_map/ppermute | solution.py:294
  10.2 16.9 %collective-permute-start.3 = (bf16[256,1024]{1,0:T(8,128)(2,1)}, bf16[256,1024]{1,0:T(8,128)(2,1)S(1)}, u32[]{:S(2)}, u32[]{:S(2)}) collective-permute-start(bf16[256,1024]{1,0:T(8,128)(2,1)} %bitcast.24), channel_id=1, source_target_pairs={{0,1},{1,0},{2,3},{3,2},{4,5},{5,4},{6,7},{7,6},{8,9},{9,8},{10,11... | collective-permute-start | bytes 1572872 | tf_op jit(solution)/shard_map/ppermute | solution.py:300
  11.2 15.8 %collective-permute-start.6 = (bf16[256,1024]{1,0:T(8,128)(2,1)}, bf16[256,1024]{1,0:T(8,128)(2,1)S(1)}, u32[]{:S(2)}, u32[]{:S(2)}) collective-permute-start(bf16[256,1024]{1,0:T(8,128)(2,1)} %bitcast.25), channel_id=1, source_target_pairs={{0,2},{1,3},{2,0},{3,1},{4,6},{5,7},{6,4},{7,5},{8,10},{9,11},{10,... | collective-permute-start | bytes 1572872 | tf_op jit(solution)/shard_map/ppermute | solution.py:303
  15.8 12.0 %collective-permute-start.5 = (bf16[512,256]{1,0:T(8,128)(2,1)S(1)}, bf16[512,256]{1,0:T(8,128)(2,1)S(1)}, u32[]{:S(2)}, u32[]{:S(2)}) collective-permute-start(bf16[512,256]{1,0:T(8,128)(2,1)S(1)} %constant_dynamic-update-slice_fusion.refs_1_.refs_5_), channel_id=1, source_target_pairs={{0,12},{4,8},{8,4},{12,0},{16,28},{20,24},{24,20},{28,16},{32,44},... | collective-permute-start | bytes 786440 | tf_op jit(solution)/shard_map/ppermute | solution.py:297
  18.6 7.8 %collective-permute-start.4 = (bf16[512,256]{1,0:T(8,128)(2,1)S(1)}, bf16[512,256]{1,0:T(8,128)(2,1)S(1)}, u32[]{:S(2)}, u32[]{:S(2)}) collective-permute-start(bf16[512,256]{1,0:T(8,128)(2,1)S(1)} %constant_dynamic-update-slice_fusion.refs_1_.refs_5_), channel_id=1, source_target_pairs={{0,4},{4,0},{8,12},{12,8},{16,20},{20,16},{24,28},{28,24},{32,36},... | collective-permute-start | bytes 786440 | tf_op jit(solution)/shard_map/ppermute | solution.py:297
  18.9 3.4 %copy-start = (bf16[1024,4096]{1,0:T(8,128)(2,1)S(1)}, bf16[1024,4096]{1,0:T(8,128)(2,1)}, u32[]{:S(2)}) copy-start(bf16[1024,4096]{1,0:T(8,128)(2,1)} %param.13) | copy-start | bytes 25165828
  18.9 3.4 %copy-start.1 = (bf16[1,1,256,1024]{3,2,1,0:T(8,128)(2,1)S(1)}, bf16[1,1,256,1024]{3,2,1,0:T(8,128)(2,1)}, u32[]{:S(2)}) copy-start(bf16[1,1,256,1024]{3,2,1,0:T(8,128)(2,1)} %param.14) | copy-start | bytes 1572868
  26.4 8.1 %collective-permute-start.8 = (bf16[512,256]{1,0:T(8,128)(2,1)S(1)}, bf16[512,256]{1,0:T(8,128)(2,1)S(1)}, u32[]{:S(2)}, u32[]{:S(2)}) collective-permute-start(bf16[512,256]{1,0:T(8,128)(2,1)S(1)} %collective-permute-done.4.refs_1_.refs_5_), channel_id=1, source_target_pairs={{0,12},{4,8},{8,4},{12,0},{16,28},{20,24},{24,20},{28,16},{32,44},... | collective-permute-start | bytes 786440 | tf_op jit(solution)/shard_map/ppermute | solution.py:297
  27.0 5.0 %collective-permute-start.7 = (bf16[256,1024]{1,0:T(8,128)(2,1)S(1)}, bf16[256,1024]{1,0:T(8,128)(2,1)S(1)}, u32[]{:S(2)}, u32[]{:S(2)}) collective-permute-start(bf16[256,1024]{1,0:T(8,128)(2,1)S(1)} %collective-permute-done.6), channel_id=1, source_target_pairs={{0,1},{1,0},{2,3},{3,2},{4,5},{5,4},{6,7},{7,6},{8,9},{9,8},{10,11... | collective-permute-start | bytes 1572872 | tf_op jit(solution)/shard_map/ppermute | solution.py:300
  38.3 2.7 %collective-permute-start.9 = (bf16[512,1024]{1,0:T(8,128)(2,1)S(1)}, bf16[512,1024]{1,0:T(8,128)(2,1)S(1)}, u32[]{:S(2)}, u32[]{:S(2)}) collective-permute-start(bf16[512,1024]{1,0:T(8,128)(2,1)S(1)} %pad_maximum_fusion), channel_id=1, source_target_pairs={{0,1},{1,0},{2,3},{3,2},{4,5},{5,4},{6,7},{7,6},{8,9},{9,8},{10,11... | collective-permute-start | bytes 3145736 | tf_op jit(solution)/shard_map/ppermute | solution.py:300
  41.7 14.1 %collective-permute-start.11 = (bf16[256,1024]{1,0:T(8,128)(2,1)S(1)}, bf16[256,1024]{1,0:T(8,128)(2,1)S(1)}, u32[]{:S(2)}, u32[]{:S(2)}) collective-permute-start(bf16[256,1024]{1,0:T(8,128)(2,1)S(1)} %fusion.43), channel_id=1, source_target_pairs={{0,2},{1,3},{2,0},{3,1},{4,6},{5,7},{6,4},{7,5},{8,10},{9,11},{10,... | collective-permute-start | bytes 1572872 | tf_op jit(solution)/shard_map/ppermute | solution.py:303
  41.8 12.5 %collective-permute-start.10 = (bf16[512,256]{1,0:T(8,128)(2,1)S(1)}, bf16[512,256]{1,0:T(8,128)(2,1)S(1)}, u32[]{:S(2)}, u32[]{:S(2)}) collective-permute-start(bf16[512,256]{1,0:T(8,128)(2,1)S(1)} %get-tuple-element.77), channel_id=1, source_target_pairs={{0,8},{4,12},{8,0},{12,4},{16,24},{20,28},{24,16},{28,20},{32,40},... | collective-permute-start | bytes 786440 | tf_op jit(solution)/shard_map/ppermute | solution.py:297
  47.9 8.4 %collective-permute-start.12 = (bf16[512,256]{1,0:T(8,128)(2,1)S(1)}, bf16[512,256]{1,0:T(8,128)(2,1)S(1)}, u32[]{:S(2)}, u32[]{:S(2)}) collective-permute-start(bf16[512,256]{1,0:T(8,128)(2,1)S(1)} %get-tuple-element.94), channel_id=1, source_target_pairs={{0,4},{4,0},{8,12},{12,8},{16,20},{20,16},{24,28},{28,24},{32,36},... | collective-permute-start | bytes 786440 | tf_op jit(solution)/shard_map/ppermute | solution.py:297
  48.6 9.4 %collective-permute-start.13 = (bf16[512,256]{1,0:T(8,128)(2,1)S(1)}, bf16[512,256]{1,0:T(8,128)(2,1)S(1)}, u32[]{:S(2)}, u32[]{:S(2)}) collective-permute-start(bf16[512,256]{1,0:T(8,128)(2,1)S(1)} %get-tuple-element.95), channel_id=1, source_target_pairs={{0,12},{4,8},{8,4},{12,0},{16,28},{20,24},{24,20},{28,16},{32,44},... | collective-permute-start | bytes 786440 | tf_op jit(solution)/shard_map/ppermute | solution.py:297
  58.2 8.1 %collective-permute-start.14 = (bf16[128,256]{1,0:T(8,128)(2,1)S(1)}, bf16[128,256]{1,0:T(8,128)(2,1)S(1)}, u32[]{:S(2)}, u32[]{:S(2)}) collective-permute-start(bf16[128,256]{1,0:T(8,128)(2,1)S(1)} %get-tuple-element.100), channel_id=1, source_target_pairs={{0,16},{4,20},{8,24},{12,28},{16,0},{20,4},{24,8},{28,12},{32,48},... | collective-permute-start | bytes 196616 | tf_op jit(solution)/shard_map/ppermute | solution.py:294
  59.8 8.9 %collective-permute-start.16 = (bf16[128,256]{1,0:T(8,128)(2,1)S(1)}, bf16[128,256]{1,0:T(8,128)(2,1)S(1)}, u32[]{:S(2)}, u32[]{:S(2)}) collective-permute-start(bf16[128,256]{1,0:T(8,128)(2,1)S(1)} %get-tuple-element.101), channel_id=1, source_target_pairs={{0,32},{4,36},{8,40},{12,44},{16,48},{20,52},{24,56},{28,60},{32,0... | collective-permute-start | bytes 196616 | tf_op jit(solution)/shard_map/ppermute | solution.py:294
  63.7 6.4 %collective-permute-start.15 = (bf16[128,256]{1,0:T(8,128)(2,1)S(1)}, bf16[128,256]{1,0:T(8,128)(2,1)S(1)}, u32[]{:S(2)}, u32[]{:S(2)}) collective-permute-start(bf16[128,256]{1,0:T(8,128)(2,1)S(1)} %get-tuple-element.102), channel_id=1, source_target_pairs={{0,48},{4,52},{8,56},{12,60},{16,32},{20,36},{24,40},{28,44},{32,1... | collective-permute-start | bytes 196616 | tf_op jit(solution)/shard_map/ppermute | solution.py:294

commit v6 on v5

--- a/solution.py
+++ b/solution.py
@@ -133,7 +133,7 @@
         mixed_ref[span(i), :] = mixed.astype(BF16)
 
 
-def bwd_kernel(widths, first, last, *refs):
+def bwd_kernel(widths, first, last, joined, *refs):
     count = len(widths)
     q, dout, delta = refs[:3]
     alphas = refs[3 : 3 + count]
@@ -145,8 +145,13 @@
     if not first:
         dq_in = refs[at]
         at += 1
-    grads = regroup(refs[at : at + sum(widths)], widths)
-    at += sum(widths)
+    if joined:
+        n = tables[0][0].shape[0]
+        grads = [(refs[at].at[i * n : (i + 1) * n],) for i in range(count)]
+        at += 1
+    else:
+        grads = regroup(refs[at : at + sum(widths)], widths)
+        at += sum(widths)
     dq_ref = refs[at]
     turned = refs[at + 1 : at + count + 1]
     slopes = refs[at + count + 1 : at + 2 * count + 1]
@@ -258,14 +263,17 @@
     return out[:n], out[n : n + e + 1], out[n + e + 1], out[n + e + 2]
 
 
-def backward(q, dout, delta, alphas, tables, weights, kind, dq, last):
+def backward(q, dout, delta, alphas, tables, weights, kind, dq, last, joined=False):
     flat = [x for t in tables for x in t]
+    shapes = [t.shape for t in flat]
+    if joined:
+        shapes = [(sum(t.shape[0] for t in flat), flat[0].shape[1])]
     kinds = [kind if len(t) == 1 else BF16 for t in tables for _ in t]
     out = call(
-        functools.partial(bwd_kernel, [len(t) for t in tables], dq is None, last),
+        functools.partial(bwd_kernel, [len(t) for t in tables], dq is None, last, joined),
         "backward",
         [q, dout, delta, *alphas, *flat, *weights, *([] if dq is None else [dq])],
-        [jax.ShapeDtypeStruct(t.shape, k) for t, k in zip(flat, kinds)]
+        [jax.ShapeDtypeStruct(shape, k) for shape, k in zip(shapes, kinds)]
         + [jax.ShapeDtypeStruct((SLOTS, HEADS * HD), BF16) if last else WIDE],
         turned_shapes(tables)
         + weight_shapes(tables)
@@ -309,7 +317,8 @@
     q, cot_late = lax.optimization_barrier((q, cot))
     chunk0 = jnp.concatenate([own] + [over_z(own, s) for s in (1, 3, 2)], axis=0)
     chunk1, chunk3 = over_x(chunk0, 1), over_x(chunk0, 3)
-    chunk2 = over_x(chunk1, 3)
+    middle = chunk0.shape[0] // 2
+    halves = [(over_x(chunk1[:middle], 3),), (over_x(chunk3[middle:], 1),)]
 
     me = lax.axis_index("tensor")
 
@@ -319,16 +328,16 @@
     cot_core = to_core(cot)
     cot_chip = to_chip(cot_late)
     cot_diag = to_core(cot_chip)
-    w0, part0 = forward(q, [(chunk0,), comp], (False, True), 0.02)
+    w0, part0 = forward(q, [(chunk0,), comp], (False, True), 0.03)
     part0, cot = lax.optimization_barrier((part0, cot))
     half = dot_nt(columns(0), cot) + dot_nt(columns(1), cot_core)
     half, chunk1, chunk3 = lax.optimization_barrier((half, chunk1, chunk3))
     w13, part13 = forward(q, [(chunk1,), (chunk3,)], (False, False))
     dout = (half + dot_nt(columns(2), cot_chip) + dot_nt(columns(3), cot_diag)).astype(BF16)
     w2, (alpha0, alpha13, alpha2), delta, mixed = forward_merge(
-        lengths, q, dout, [(chunk2,)], [part0, part13]
-    )
-    (g2,), dq = backward(q, dout, delta, [alpha2], [(chunk2,)], w2, BF16, None, False)
+        lengths, q, dout, halves, [part0, part13]
+    )
+    (g2,), dq = backward(q, dout, delta, [alpha2, alpha2], halves, w2, BF16, None, False, True)
 
     def partial_out(bits):
         block = lax.dot_general(

time: 70.9 us -> 71.5 us (level)
  starting transfers between devices: 24.7 us -> 26.9 us
  waiting for transfers between devices: 15.9 us -> 15 us
  local copies, waits for them, and re-layouts: 0.9 us -> 0.07 us
    ppermute x6 -> x7, starting transfers between devices: 8.03 us -> 9.72 us  [over_x(): return lax.ppermute(a, 'group', group_flip(0, s))]
    ppermute x6 -> x7, waiting for transfers between devices: 7.38 us -> 5.84 us  [over_x(): return lax.ppermute(a, 'group', group_flip(0, s))]
    ppermute x6, waiting for transfers between devices: 6.47 us -> 7.5 us  [over_z(): return lax.ppermute(a, 'group', group_flip(s, 0))]
    unnamed x7 -> x9, local copies, waits for them, and re-layouts: 0.88 us -> 0.03 us
  transfers between devices with their start and end apart: 17 -> 18, of which waited for: 11 -> 9; matrix products, arithmetic and copies ran while one was open for 6% -> 6% of each run, Pallas kernels for 24% -> 24%
where the time goes in v6:
time: 71.5 us; the launch traced here: 71.3 us
  starting transfers between devices  26.9 us (38%)
  Pallas kernels  19.4 us (27%)
  waiting for transfers between devices  15 us (21%)
  matrix products  6.76 us (9%)
  other arithmetic  1.66 us (2%)
  between operations  1.53 us (2%)
    pallas_call x7, Pallas kernels, call(): pl.pallas_call(kernel, in_specs=specs or [IN_VMEM] * len(operands), out_s...  19.4 us
    ppermute x6, starting transfers between devices, over_z(): return lax.ppermute(a, 'group', group_flip(s, 0))  15.4 us
    ppermute x7, starting transfers between devices, over_x(): return lax.ppermute(a, 'group', group_flip(0, s))  9.72 us
    ppermute x6, waiting for transfers between devices, over_z(): return lax.ppermute(a, 'group', group_flip(s, 0))  7.5 us
    ppermute x7, waiting for transfers between devices, over_x(): return lax.ppermute(a, 'group', group_flip(0, s))  5.84 us
    dot_general x4, matrix products, partial_out(): lax.dot_general(mixed, columns(bits), (((0,), (0,)), ((), ())), preferred...  3.77 us
    dot_general x4, matrix products, dot_nt(): lax.dot_general(a, b, (((1,), (1,)), ((), ())), preferred_element_type=F32)  2.99 us
    ppermute x2, waiting for transfers between devices, to_chip(): return lax.ppermute(a, 'tensor', tensor_flip(2))  1.57 us
  transfers between devices with their start and end apart: 18, of which 9 were waited for; matrix products, arithmetic and copies ran while one was open for 6% of the time, Pallas kernels for 24%

profile of v6, /device:TPU:8, one launch (start us, length us, event | category | flops | bytes accessed | tf_op | source)
XLA Modules:
  0.0 71.3 jit_solution(2793240079707202114)
XLA Ops:
  0.6 0.8 %pad_maximum_fusion.1 = bf16[128,256]{1,0:T(8,128)(2,1)S(1)} fusion(bf16[128,128]{1,0:T(8,128)(2,1)} %bitcast.31, bf16[128,128]{1,0:T(8,128)(2,1)} %bitcast.32), kind=kLoop, calls=%fused_computation.41 | loop fusion | flops 131072 | bytes 131072 | tf_op jit(solution)/shard_map/concatenate | solution.py:313
  1.4 7.3 %collective-permute-start.2 = (bf16[128,256]{1,0:T(8,128)(2,1)S(1)}, bf16[128,256]{1,0:T(8,128)(2,1)S(1)}, u32[]{:S(2)}, u32[]{:S(2)}) collective-permute-start(bf16[128,256]{1,0:T(8,128)(2,1)S(1)} %pad_maximum_fusion.1), channel_id=1, source_target_pairs={{0,32},{4,36},{8,40},{12,44},{16,48},{20,52},{24,56},{28,60},{32,0... | collective-permute-start | bytes 196616 | tf_op jit(solution)/shard_map/ppermute | solution.py:302
  8.7 0.0 collective-permute-start.1
  8.7 1.5 %collective-permute-start = (bf16[128,256]{1,0:T(8,128)(2,1)S(1)}, bf16[128,256]{1,0:T(8,128)(2,1)S(1)}, u32[]{:S(2)}, u32[]{:S(2)}) collective-permute-start(bf16[128,256]{1,0:T(8,128)(2,1)S(1)} %pad_maximum_fusion.1), channel_id=1, source_target_pairs={{0,16},{4,20},{8,24},{12,28},{16,0},{20,4},{24,8},{28,12},{32,48},... | collective-permute-start | bytes 196616 | tf_op jit(solution)/shard_map/ppermute | solution.py:302
  10.2 0.0 collective-permute-start.3
  10.2 1.1 %fetch.1 = (bf16[256,1024]{1,0:T(8,128)(2,1)S(1)}, bf16[256,128]{1,0:T(8,128)(2,1)S(1)}, bf16[256,128]{1,0:T(8,128)(2,1)S(1)}) custom-call(bf16[256,1024]{1,0:T(8,128)(2,1)} %bitcast.25, bf16[256,128]{1,0:T(8,128)(2,1)} %bitcast.29, bf16[256,128]{1,0:T(8,128)(2,1)} %bitcast.30), custom_call_target="tpu_custom_call" | custom-call | flops 1000000 | bytes 100000 | tf_op jit(solution)/shard_map/fetch/pallas_call | solution.py:192
  11.2 1.1 %collective-permute-start.6 = (bf16[256,1024]{1,0:T(8,128)(2,1)}, bf16[256,1024]{1,0:T(8,128)(2,1)S(1)}, u32[]{:S(2)}, u32[]{:S(2)}) collective-permute-start(bf16[256,1024]{1,0:T(8,128)(2,1)} %bitcast.27), channel_id=1, source_target_pairs={{0,2},{1,3},{2,0},{3,1},{4,6},{5,7},{6,4},{7,5},{8,10},{9,11},{10,... | collective-permute-start | bytes 1572872 | tf_op jit(solution)/shard_map/ppermute | solution.py:311
  13.0 0.0 slice-start
  13.0 2.7 %collective-permute-done = bf16[128,256]{1,0:T(8,128)(2,1)S(1)} collective-permute-done((bf16[128,256]{1,0:T(8,128)(2,1)S(1)}, bf16[128,256]{1,0:T(8,128)(2,1)S(1)}, u32[]{:S(2)}, u32[]{:S(2)}) %collective-permute-start) | collective-permute-done | bytes 65568 | tf_op jit(solution)/shard_map/ppermute | solution.py:302
  15.7 0.1 collective-permute-done.1
  15.8 0.0 collective-permute-done.2
  15.8 2.8 %collective-permute-start.5 = (bf16[512,256]{1,0:T(8,128)(2,1)S(1)}, bf16[512,256]{1,0:T(8,128)(2,1)S(1)}, u32[]{:S(2)}, u32[]{:S(2)}) collective-permute-start(bf16[512,256]{1,0:T(8,128)(2,1)S(1)} %constant_dynamic-update-slice_fusion.refs_1_.refs_5_), channel_id=1, source_target_pairs={{0,12},{4,8},{8,4},{12,0},{16,28},{20,24},{24,20},{28,16},{32,44},... | collective-permute-start | bytes 786440 | tf_op jit(solution)/shard_map/ppermute | solution.py:305
  18.6 0.2 collective-permute-start.4
  18.9 0.0 slice-start.1
  18.9 0.0 copy-start
  18.9 2.6 %forward.2 = (bf16[512,2048]{1,0:T(8,128)(2,1)S(1)}, bf16[256,2048]{1,0:T(8,128)(2,1)S(1)}, f32[8,1,256]{2,1,0:T(1,128)S(1)}, f32[8,1,256]{2,1,0:T(1,128)S(1)}, f32[1024,256]{1,0:T(8,128)S(1)}) custom-call(bf16[256,1024]{1,0:T(8,128)(2,1)S(1)} %get-tuple-element.54.refs_0_.refs_1_, bf16[512,256]{1,0:T(8,128)(2,1)S(1)} %constant_dynamic-update-slice_fusion.refs_1_.refs_5_, ...), custom_call_target="tpu_custom_call" | custom-call | flops 13421772800 | bytes 98304 | tf_op jit(solution)/shard_map/forward/pallas_call | solution.py:192
  21.4 0.0 slice-done
  21.4 0.0 slice-done.1
  21.5 0.0 copy-done
  21.5 0.7 %fusion.14 = f32[1024,256]{1,0:T(8,128)S(1)} fusion(bf16[256,1024]{1,0:T(8,128)(2,1)S(1)} %bitcast.28, bf16[1024,4096]{1,0:T(8,128)(2,1)S(1)} %bitcast.24, s32[]{:T(128)S(6)} %select_n.16), kind=kOutput, calls=%fused_computation.14 | convolution fusion | flops 536870912 | bytes 3670020 | tf_op jit(solution)/shard_map/dot_general | solution.py:26
  22.2 3.0 %collective-permute-done.5.refs_2_.refs_6_ = bf16[512,256]{1,0:T(8,128)(2,1)S(1)} collective-permute-done((bf16[512,256]{1,0:T(8,128)(2,1)S(1)}, bf16[512,256]{1,0:T(8,128)(2,1)S(1)}, u32[]{:S(2)}, u32[]{:S(2)}) %collective-permute-start.5) | collective-permute-done | bytes 262176 | tf_op jit(solution)/shard_map/ppermute | solution.py:305
  25.2 0.4 collective-permute-start.9
  25.6 0.9 %collective-permute-done.4.refs_1_.refs_5_ = bf16[512,256]{1,0:T(8,128)(2,1)S(1)} collective-permute-done((bf16[512,256]{1,0:T(8,128)(2,1)S(1)}, bf16[512,256]{1,0:T(8,128)(2,1)S(1)}, u32[]{:S(2)}, u32[]{:S(2)}) %collective-permute-start.4) | collective-permute-done | bytes 262176 | tf_op jit(solution)/shard_map/ppermute | solution.py:305
  26.5 1.7 %collective-permute-start.8 = (bf16[256,256]{1,0:T(8,128)(2,1)S(1)}, bf16[256,256]{1,0:T(8,128)(2,1)S(1)}, u32[]{:S(2)}, u32[]{:S(2)}) collective-permute-start(bf16[256,256]{1,0:T(8,128)(2,1)S(1)} %slice.63), channel_id=1, source_target_pairs={{0,12},{4,8},{8,4},{12,0},{16,28},{20,24},{24,20},{28,16},{32,44},... | collective-permute-start | bytes 393224 | tf_op jit(solution)/shard_map/ppermute | solution.py:305
  28.2 0.0 collective-permute-done.6
  28.2 0.0 collective-permute-start.7
  28.2 0.0 collective-permute-done.3
  28.2 0.7 %fusion.16 = f32[1024,256]{1,0:T(8,128)S(1)} fusion(f32[1024,256]{1,0:T(8,128)S(1)} %fusion.14, bf16[256,1024]{1,0:T(8,128)(2,1)S(1)} %collective-permute-done.3, bf16[1024,4096]{1,0:T(8,128)(2,1)S(1)} %bitcast.24, s32[]{:T(128)S(6)} %select_n.17), kind=kOutput, calls=%fused_computation.16 | convolution fusion | flops 537133056 | bytes 4718596 | tf_op jit(solution)/shard_map/dot_general | solution.py:26
  28.9 3.4 %forward.3 = (bf16[512,2048]{1,0:T(8,128)(2,1)S(1)}, bf16[512,2048]{1,0:T(8,128)(2,1)S(1)}, f32[8,1,256]{2,1,0:T(1,128)S(1)}, f32[8,1,256]{2,1,0:T(1,128)S(1)}, f32[1024,256]{1,0:T(8,128)S(1)}) custom-call(bf16[256,1024]{1,0:T(8,128)(2,1)S(1)} %get-tuple-element.54.refs_0_.refs_1_, bf16[512,256]{1,0:T(8,128)(2,1)S(1)} %collective-permute-done.4.refs_1_.refs_5_, ...), custom_call_target="tpu_custom_call" | custom-call | flops 33554432 | bytes 131072 | tf_op jit(solution)/shard_map/forward/pallas_call | solution.py:192
  32.4 0.7 %fusion.6 = f32[1024,256]{1,0:T(8,128)S(1)} fusion(bf16[256,1024]{1,0:T(8,128)(2,1)S(1)} %collective-permute-done.6, bf16[1024,4096]{1,0:T(8,128)(2,1)S(1)} %bitcast.24, s32[]{:T(128)S(6)} %select_n.18), kind=kOutput, calls=%fused_computation.6 | convolution fusion | flops 536870912 | bytes 3670020 | tf_op jit(solution)/shard_map/dot_general | solution.py:26
  33.1 0.0 collective-permute-done.7
  33.1 0.7 %fusion.22.refs_2_.refs_1_ = bf16[1024,256]{1,0:T(8,128)(2,1)S(1)} fusion(bf16[256,1024]{1,0:T(8,128)(2,1)S(1)} %collective-permute-done.7, bf16[1024,4096]{1,0:T(8,128)(2,1)S(1)} %bitcast.24, s32[]{:T(128)S(6)} %select_n.19, f32[1024,256]{1,0:T(8,128)S(1)} %fusion.16, f32[1024,256]{1,0:T(8,128)S(1)} %fusion.6), kind=kOutput, calls=%fused_computation.18 | convolution fusion | flops 537657344 | bytes 5242884 | tf_op jit(solution)/shard_map/dot_general | solution.py:26
  33.9 0.0 collective-permute-done.9.refs_4_.refs_6_
  33.9 0.0 collective-permute-done.8.refs_3_.refs_5_
  33.9 2.1 %forward_merge.1 = (bf16[256,2048]{1,0:T(8,128)(2,1)S(1)}, bf16[256,2048]{1,0:T(8,128)(2,1)S(1)}, f32[8,1,256]{2,1,0:T(1,128)S(1)}, f32[8,1,256]{2,1,0:T(1,128)S...) custom-call(s32[1,1]{1,0:T(1,128)S(6)} %copy.17.refs_0_, ...), custom_call_target="tpu_custom_call" | custom-call | flops 16777216 | bytes 65536 | tf_op jit(solution)/shard_map/forward_merge/pallas_call | solution.py:192
  36.0 0.7 %fusion.34 = bf16[256,1024]{1,0:T(8,128)(2,1)S(1)} fusion(bf16[1024,256]{1,0:T(8,128)(2,1)S(1)} %get-tuple-element.72, bf16[1024,4096]{1,0:T(8,128)(2,1)S(1)} %bitcast.24, s32[]{:T(128)S(6)} %select_n.19), kind=kOutput, calls=%fused_computation.22 | convolution fusion | flops 537133056 | bytes 3145732 | tf_op jit(solution)/shard_map/dot_general | solution.py:343
  36.8 0.7 %fusion.28 = bf16[256,1024]{1,0:T(8,128)(2,1)S(1)} fusion(bf16[1024,256]{1,0:T(8,128)(2,1)S(1)} %get-tuple-element.72, bf16[1024,4096]{1,0:T(8,128)(2,1)S(1)} %bitcast.24, s32[]{:T(128)S(6)} %select_n.17), kind=kOutput, calls=%fused_computation.20 | convolution fusion | flops 537133056 | bytes 3145732 | tf_op jit(solution)/shard_map/dot_general | solution.py:343
  37.5 0.1 pad_maximum_fusion
  37.6 0.6 collective-permute-start.10
  38.2 2.2 %backward.3 = (bf16[512,256]{1,0:T(8,128)(2,1)S(1)}, f32[1024,256]{1,0:T(8,128)S(1)}) custom-call(bf16[256,1024]{1,0:T(8,128)(2,1)S(1)} %get-tuple-element.54.refs_0_.refs_1_, bf16[1024,256]{1,0:T(8,128)(2,1)S(1)} %fusion.22.refs_2_.refs_1_, f32[8,1,256]{2,1,0:T(1,128)S(1)} %get-tuple-element.73.refs_2_, f32[8,1,256]{2,1,0:T(1,128)S(1)} %get-tuple-element.74.refs_3_.refs_4_, ...), custom_call_target="tpu_custom_call" | custom-call | flops 33554432 | bytes 65536 | tf_op jit(solution)/shard_map/backward/pallas_call | solution.py:192
  40.4 0.0 collective-permute-done.10
  40.5 0.7 %fusion.43 = bf16[256,1024]{1,0:T(8,128)(2,1)S(1)} fusion(bf16[1024,256]{1,0:T(8,128)(2,1)S(1)} %get-tuple-element.72, bf16[1024,4096]{1,0:T(8,128)(2,1)S(1)} %bitcast.24, s32[]{:T(128)S(6)} %select_n.18, bf16[512,1024]{1,0:T(8,128)(2,1)S(1)} %collective-permute-done.10), kind=kOutput, calls=%fused_computation.25 | convolution fusion | flops 538181632 | bytes 3670020 | tf_op jit(solution)/shard_map/dot_general | solution.py:343
  41.2 0.1 collective-permute-start.12
  41.3 2.5 %collective-permute-start.11 = (bf16[512,256]{1,0:T(8,128)(2,1)S(1)}, bf16[512,256]{1,0:T(8,128)(2,1)S(1)}, u32[]{:S(2)}, u32[]{:S(2)}) collective-permute-start(bf16[512,256]{1,0:T(8,128)(2,1)S(1)} %get-tuple-element.79), channel_id=1, source_target_pairs={{0,8},{4,12},{8,0},{12,4},{16,24},{20,28},{24,16},{28,20},{32,40},... | collective-permute-start | bytes 786440 | tf_op jit(solution)/shard_map/ppermute | solution.py:305
  43.8 4.1 %backward.4 = (bf16[512,256]{1,0:T(8,128)(2,1)S(1)}, bf16[512,256]{1,0:T(8,128)(2,1)S(1)}, f32[1024,256]{1,0:T(8,128)S(1)}) custom-call(bf16[256,1024]{1,0:T(8,128)(2,1)S(1)} %get-tuple-element.54.refs_0_.refs_1_, bf16[1024,256]{1,0:T(8,128)(2,1)S(1)} %fusion.22.refs_2_.refs_1_, f32[8,1,256]{2,1,0:T(1,128)S(1)} %get-tuple-element.73.refs_2_, ...), custom_call_target="tpu_custom_call" | custom-call | flops 67108864 | bytes 131072 | tf_op jit(solution)/shard_map/backward/pallas_call | solution.py:192
  47.8 0.7 collective-permute-start.13
  48.5 1.4 %collective-permute-start.14 = (bf16[512,256]{1,0:T(8,128)(2,1)S(1)}, bf16[512,256]{1,0:T(8,128)(2,1)S(1)}, u32[]{:S(2)}, u32[]{:S(2)}) collective-permute-start(bf16[512,256]{1,0:T(8,128)(2,1)S(1)} %get-tuple-element.97), channel_id=1, source_target_pairs={{0,12},{4,8},{8,4},{12,0},{16,28},{20,24},{24,20},{28,16},{32,44},... | collective-permute-start | bytes 786440 | tf_op jit(solution)/shard_map/ppermute | solution.py:305
  49.9 4.0 %backward.5 = (f32[512,256]{1,0:T(8,128)S(1)}, bf16[256,128]{1,0:T(8,128)(2,1)}, bf16[256,128]{1,0:T(8,128)(2,1)}, bf16[256,1024]{1,0:T(8,128)(2,1)}) custom-call(bf16[256,1024]{1,0:T(8,128)(2,1)S(1)} %get-tuple-element.54.refs_0_.refs_1_, bf16[1024,256]{1,0:T(8,128)(2,1)S(1)} %fusion.22.refs_2_.refs_1_, f32[8,1,256]{2,1,0:T(1,128)S(1)} %get-tuple-element.73.refs_2_, ...), custom_call_target="tpu_custom_call" | custom-call | flops 50331648 | bytes 98304 | tf_op jit(solution)/shard_map/backward/pallas_call | solution.py:192
  53.9 0.0 collective-permute-done.11
  53.9 1.6 %collective-permute-done.12 = bf16[256,1024]{1,0:T(8,128)(2,1)S(1)} collective-permute-done((bf16[256,1024]{1,0:T(8,128)(2,1)S(1)}, bf16[256,1024]{1,0:T(8,128)(2,1)S(1)}, u32[]{:S(2)}, u32[]{:S(2)}) %collective-permute-start.12) | collective-permute-done | bytes 524320 | tf_op jit(solution)/shard_map/ppermute | solution.py:311
  55.5 0.8 %collective-permute-done.13 = bf16[512,256]{1,0:T(8,128)(2,1)S(1)} collective-permute-done((bf16[512,256]{1,0:T(8,128)(2,1)S(1)}, bf16[512,256]{1,0:T(8,128)(2,1)S(1)}, u32[]{:S(2)}, u32[]{:S(2)}) %collective-permute-start.13) | collective-permute-done | bytes 262176 | tf_op jit(solution)/shard_map/ppermute | solution.py:305
  56.3 1.2 %collective-permute-done.14 = bf16[512,256]{1,0:T(8,128)(2,1)S(1)} collective-permute-done((bf16[512,256]{1,0:T(8,128)(2,1)S(1)}, bf16[512,256]{1,0:T(8,128)(2,1)S(1)}, u32[]{:S(2)}, u32[]{:S(2)}) %collective-permute-start.14) | collective-permute-done | bytes 262176 | tf_op jit(solution)/shard_map/ppermute | solution.py:305
  57.5 0.1 fusion.73
  57.6 1.9 %collective-permute-start.15 = (bf16[128,256]{1,0:T(8,128)(2,1)S(1)}, bf16[128,256]{1,0:T(8,128)(2,1)S(1)}, u32[]{:S(2)}, u32[]{:S(2)}) collective-permute-start(bf16[128,256]{1,0:T(8,128)(2,1)S(1)} %get-tuple-element.102), channel_id=1, source_target_pairs={{0,16},{4,20},{8,24},{12,28},{16,0},{20,4},{24,8},{28,12},{32,48},... | collective-permute-start | bytes 196616 | tf_op jit(solution)/shard_map/ppermute | solution.py:302
  59.6 4.7 %collective-permute-start.17 = (bf16[128,256]{1,0:T(8,128)(2,1)S(1)}, bf16[128,256]{1,0:T(8,128)(2,1)S(1)}, u32[]{:S(2)}, u32[]{:S(2)}) collective-permute-start(bf16[128,256]{1,0:T(8,128)(2,1)S(1)} %get-tuple-element.103), channel_id=1, source_target_pairs={{0,32},{4,36},{8,40},{12,44},{16,48},{20,52},{24,56},{28,60},{32,0... | collective-permute-start | bytes 196616 | tf_op jit(solution)/shard_map/ppermute | solution.py:302
  64.2 0.0 collective-permute-start.16
  64.2 1.6 %fusion.58 = bf16[1,1,256,1024]{3,2,1,0:T(8,128)(2,1)} fusion(bf16[1024,256]{1,0:T(8,128)(2,1)S(1)} %get-tuple-element.72, bf16[1024,4096]{1,0:T(8,128)(2,1)S(1)} %bitcast.24, s32[]{:T(128)S(6)} %select_n.16, bf16[256,1024]{1,0:T(8,128)(2,1)S(1)} %collective-permute-done.12, bf16[512,1024]{1,0:T(8,128)(2,1)S(1)} %collective-permute-done.10), kind=kOutput, calls=%fused_computation.30 | convolution fusion | flops 538705920 | bytes 4194308 | tf_op jit(solution)/shard_map/dot_general | solution.py:343
  65.8 0.0 collective-permute-done.15
  65.8 2.9 %collective-permute-done.17 = bf16[128,256]{1,0:T(8,128)(2,1)S(1)} collective-permute-done((bf16[128,256]{1,0:T(8,128)(2,1)S(1)}, bf16[128,256]{1,0:T(8,128)(2,1)S(1)}, u32[]{:S(2)}, u32[]{:S(2)}) %collective-permute-start.17) | collective-permute-done | bytes 65568 | tf_op jit(solution)/shard_map/ppermute | solution.py:302
  68.7 1.9 %collective-permute-done.16 = bf16[128,256]{1,0:T(8,128)(2,1)S(1)} collective-permute-done((bf16[128,256]{1,0:T(8,128)(2,1)S(1)}, bf16[128,256]{1,0:T(8,128)(2,1)S(1)}, u32[]{:S(2)}, u32[]{:S(2)}) %collective-permute-start.16) | collective-permute-done | bytes 65568 | tf_op jit(solution)/shard_map/ppermute | solution.py:302
  70.6 0.7 fusion.64
  (11 shorter events, 0.1 us)
Async XLA Ops:
  1.4 14.4 %collective-permute-start.2 = (bf16[128,256]{1,0:T(8,128)(2,1)S(1)}, bf16[128,256]{1,0:T(8,128)(2,1)S(1)}, u32[]{:S(2)}, u32[]{:S(2)}) collective-permute-start(bf16[128,256]{1,0:T(8,128)(2,1)S(1)} %pad_maximum_fusion.1), channel_id=1, source_target_pairs={{0,32},{4,36},{8,40},{12,44},{16,48},{20,52},{24,56},{28,60},{32,0... | collective-permute-start | bytes 196616 | tf_op jit(solution)/shard_map/ppermute | solution.py:302
  8.7 7.1 %collective-permute-start.1 = (bf16[128,256]{1,0:T(8,128)(2,1)S(1)}, bf16[128,256]{1,0:T(8,128)(2,1)S(1)}, u32[]{:S(2)}, u32[]{:S(2)}) collective-permute-start(bf16[128,256]{1,0:T(8,128)(2,1)S(1)} %pad_maximum_fusion.1), channel_id=1, source_target_pairs={{0,48},{4,52},{8,56},{12,60},{16,32},{20,36},{24,40},{28,44},{32,1... | collective-permute-start | bytes 196616 | tf_op jit(solution)/shard_map/ppermute | solution.py:302
  8.7 7.0 %collective-permute-start = (bf16[128,256]{1,0:T(8,128)(2,1)S(1)}, bf16[128,256]{1,0:T(8,128)(2,1)S(1)}, u32[]{:S(2)}, u32[]{:S(2)}) collective-permute-start(bf16[128,256]{1,0:T(8,128)(2,1)S(1)} %pad_maximum_fusion.1), channel_id=1, source_target_pairs={{0,16},{4,20},{8,24},{12,28},{16,0},{20,4},{24,8},{28,12},{32,48},... | collective-permute-start | bytes 196616 | tf_op jit(solution)/shard_map/ppermute | solution.py:302
  10.2 18.0 %collective-permute-start.3 = (bf16[256,1024]{1,0:T(8,128)(2,1)}, bf16[256,1024]{1,0:T(8,128)(2,1)S(1)}, u32[]{:S(2)}, u32[]{:S(2)}) collective-permute-start(bf16[256,1024]{1,0:T(8,128)(2,1)} %bitcast.26), channel_id=1, source_target_pairs={{0,1},{1,0},{2,3},{3,2},{4,5},{5,4},{6,7},{7,6},{8,9},{9,8},{10,11... | collective-permute-start | bytes 1572872 | tf_op jit(solution)/shard_map/ppermute | solution.py:308
  11.2 16.9 %collective-permute-start.6 = (bf16[256,1024]{1,0:T(8,128)(2,1)}, bf16[256,1024]{1,0:T(8,128)(2,1)S(1)}, u32[]{:S(2)}, u32[]{:S(2)}) collective-permute-start(bf16[256,1024]{1,0:T(8,128)(2,1)} %bitcast.27), channel_id=1, source_target_pairs={{0,2},{1,3},{2,0},{3,1},{4,6},{5,7},{6,4},{7,5},{8,10},{9,11},{10,... | collective-permute-start | bytes 1572872 | tf_op jit(solution)/shard_map/ppermute | solution.py:311
  13.0 8.4 %slice-start = ((s8[8388608]{0:T(1024)(128)(4,1)}), s8[4194304]{0:T(1024)(128)(4,1)S(1)}, s32[]{:S(2)}) async-start(s8[8388608]{0:T(1024)(128)(4,1)} %bitcast.23), calls=%async_computation | async-start | bytes 8388608
  15.8 9.4 %collective-permute-start.5 = (bf16[512,256]{1,0:T(8,128)(2,1)S(1)}, bf16[512,256]{1,0:T(8,128)(2,1)S(1)}, u32[]{:S(2)}, u32[]{:S(2)}) collective-permute-start(bf16[512,256]{1,0:T(8,128)(2,1)S(1)} %constant_dynamic-update-slice_fusion.refs_1_.refs_5_), channel_id=1, source_target_pairs={{0,12},{4,8},{8,4},{12,0},{16,28},{20,24},{24,20},{28,16},{32,44},... | collective-permute-start | bytes 786440 | tf_op jit(solution)/shard_map/ppermute | solution.py:305
  18.6 7.8 %collective-permute-start.4 = (bf16[512,256]{1,0:T(8,128)(2,1)S(1)}, bf16[512,256]{1,0:T(8,128)(2,1)S(1)}, u32[]{:S(2)}, u32[]{:S(2)}) collective-permute-start(bf16[512,256]{1,0:T(8,128)(2,1)S(1)} %constant_dynamic-update-slice_fusion.refs_1_.refs_5_), channel_id=1, source_target_pairs={{0,4},{4,0},{8,12},{12,8},{16,20},{20,16},{24,28},{28,24},{32,36},... | collective-permute-start | bytes 786440 | tf_op jit(solution)/shard_map/ppermute | solution.py:305
  18.9 2.6 %slice-start.1 = ((s8[8388608]{0:T(1024)(128)(4,1)}), s8[4194304]{0:T(1024)(128)(4,1)S(1)}, s32[]{:S(2)}) async-start(s8[8388608]{0:T(1024)(128)(4,1)} %bitcast.23), calls=%async_computation.1 | async-start | bytes 8388608
  18.9 2.6 %copy-start = (bf16[1,1,256,1024]{3,2,1,0:T(8,128)(2,1)S(1)}, bf16[1,1,256,1024]{3,2,1,0:T(8,128)(2,1)}, u32[]{:S(2)}) copy-start(bf16[1,1,256,1024]{3,2,1,0:T(8,128)(2,1)} %param.14) | copy-start | bytes 1572868
  25.2 8.7 %collective-permute-start.9 = (bf16[256,256]{1,0:T(8,128)(2,1)S(1)}, bf16[256,256]{1,0:T(8,128)(2,1)S(1)}, u32[]{:S(2)}, u32[]{:S(2)}) collective-permute-start(bf16[256,256]{1,0:T(8,128)(2,1)S(1)} %slice.64), channel_id=1, source_target_pairs={{0,4},{4,0},{8,12},{12,8},{16,20},{20,16},{24,28},{28,24},{32,36},... | collective-permute-start | bytes 393224 | tf_op jit(solution)/shard_map/ppermute | solution.py:305
  26.5 7.5 %collective-permute-start.8 = (bf16[256,256]{1,0:T(8,128)(2,1)S(1)}, bf16[256,256]{1,0:T(8,128)(2,1)S(1)}, u32[]{:S(2)}, u32[]{:S(2)}) collective-permute-start(bf16[256,256]{1,0:T(8,128)(2,1)S(1)} %slice.63), channel_id=1, source_target_pairs={{0,12},{4,8},{8,4},{12,0},{16,28},{20,24},{24,20},{28,16},{32,44},... | collective-permute-start | bytes 393224 | tf_op jit(solution)/shard_map/ppermute | solution.py:305
  28.2 5.0 %collective-permute-start.7 = (bf16[256,1024]{1,0:T(8,128)(2,1)S(1)}, bf16[256,1024]{1,0:T(8,128)(2,1)S(1)}, u32[]{:S(2)}, u32[]{:S(2)}) collective-permute-start(bf16[256,1024]{1,0:T(8,128)(2,1)S(1)} %collective-permute-done.6), channel_id=1, source_target_pairs={{0,1},{1,0},{2,3},{3,2},{4,5},{5,4},{6,7},{7,6},{8,9},{9,8},{10,11... | collective-permute-start | bytes 1572872 | tf_op jit(solution)/shard_map/ppermute | solution.py:308
  37.6 2.9 %collective-permute-start.10 = (bf16[512,1024]{1,0:T(8,128)(2,1)S(1)}, bf16[512,1024]{1,0:T(8,128)(2,1)S(1)}, u32[]{:S(2)}, u32[]{:S(2)}) collective-permute-start(bf16[512,1024]{1,0:T(8,128)(2,1)S(1)} %pad_maximum_fusion), channel_id=1, source_target_pairs={{0,1},{1,0},{2,3},{3,2},{4,5},{5,4},{6,7},{7,6},{8,9},{9,8},{10,11... | collective-permute-start | bytes 3145736 | tf_op jit(solution)/shard_map/ppermute | solution.py:308
  41.2 14.3 %collective-permute-start.12 = (bf16[256,1024]{1,0:T(8,128)(2,1)S(1)}, bf16[256,1024]{1,0:T(8,128)(2,1)S(1)}, u32[]{:S(2)}, u32[]{:S(2)}) collective-permute-start(bf16[256,1024]{1,0:T(8,128)(2,1)S(1)} %fusion.43), channel_id=1, source_target_pairs={{0,2},{1,3},{2,0},{3,1},{4,6},{5,7},{6,4},{7,5},{8,10},{9,11},{10,... | collective-permute-start | bytes 1572872 | tf_op jit(solution)/shard_map/ppermute | solution.py:311
  41.3 12.6 %collective-permute-start.11 = (bf16[512,256]{1,0:T(8,128)(2,1)S(1)}, bf16[512,256]{1,0:T(8,128)(2,1)S(1)}, u32[]{:S(2)}, u32[]{:S(2)}) collective-permute-start(bf16[512,256]{1,0:T(8,128)(2,1)S(1)} %get-tuple-element.79), channel_id=1, source_target_pairs={{0,8},{4,12},{8,0},{12,4},{16,24},{20,28},{24,16},{28,20},{32,40},... | collective-permute-start | bytes 786440 | tf_op jit(solution)/shard_map/ppermute | solution.py:305
  47.8 8.4 %collective-permute-start.13 = (bf16[512,256]{1,0:T(8,128)(2,1)S(1)}, bf16[512,256]{1,0:T(8,128)(2,1)S(1)}, u32[]{:S(2)}, u32[]{:S(2)}) collective-permute-start(bf16[512,256]{1,0:T(8,128)(2,1)S(1)} %get-tuple-element.96), channel_id=1, source_target_pairs={{0,4},{4,0},{8,12},{12,8},{16,20},{20,16},{24,28},{28,24},{32,36},... | collective-permute-start | bytes 786440 | tf_op jit(solution)/shard_map/ppermute | solution.py:305
  48.5 9.0 %collective-permute-start.14 = (bf16[512,256]{1,0:T(8,128)(2,1)S(1)}, bf16[512,256]{1,0:T(8,128)(2,1)S(1)}, u32[]{:S(2)}, u32[]{:S(2)}) collective-permute-start(bf16[512,256]{1,0:T(8,128)(2,1)S(1)} %get-tuple-element.97), channel_id=1, source_target_pairs={{0,12},{4,8},{8,4},{12,0},{16,28},{20,24},{24,20},{28,16},{32,44},... | collective-permute-start | bytes 786440 | tf_op jit(solution)/shard_map/ppermute | solution.py:305
  57.6 8.2 %collective-permute-start.15 = (bf16[128,256]{1,0:T(8,128)(2,1)S(1)}, bf16[128,256]{1,0:T(8,128)(2,1)S(1)}, u32[]{:S(2)}, u32[]{:S(2)}) collective-permute-start(bf16[128,256]{1,0:T(8,128)(2,1)S(1)} %get-tuple-element.102), channel_id=1, source_target_pairs={{0,16},{4,20},{8,24},{12,28},{16,0},{20,4},{24,8},{28,12},{32,48},... | collective-permute-start | bytes 196616 | tf_op jit(solution)/shard_map/ppermute | solution.py:302
  59.6 9.2 %collective-permute-start.17 = (bf16[128,256]{1,0:T(8,128)(2,1)S(1)}, bf16[128,256]{1,0:T(8,128)(2,1)S(1)}, u32[]{:S(2)}, u32[]{:S(2)}) collective-permute-start(bf16[128,256]{1,0:T(8,128)(2,1)S(1)} %get-tuple-element.103), channel_id=1, source_target_pairs={{0,32},{4,36},{8,40},{12,44},{16,48},{20,52},{24,56},{28,60},{32,0... | collective-permute-start | bytes 196616 | tf_op jit(solution)/shard_map/ppermute | solution.py:302
  64.2 6.4 %collective-permute-start.16 = (bf16[128,256]{1,0:T(8,128)(2,1)S(1)}, bf16[128,256]{1,0:T(8,128)(2,1)S(1)}, u32[]{:S(2)}, u32[]{:S(2)}) collective-permute-start(bf16[128,256]{1,0:T(8,128)(2,1)S(1)} %get-tuple-element.104), channel_id=1, source_target_pairs={{0,48},{4,52},{8,56},{12,60},{16,32},{20,36},{24,40},{28,44},{32,1... | collective-permute-start | bytes 196616 | tf_op jit(solution)/shard_map/ppermute | solution.py:302

commit v7 on v5

--- a/solution.py
+++ b/solution.py
@@ -316,11 +316,11 @@
     def columns(bits):
         return lax.dynamic_slice_in_dim(out_weight, (me ^ bits) * 1024, 1024, 1)
 
-    cot_core = to_core(cot)
     cot_chip = to_chip(cot_late)
     cot_diag = to_core(cot_chip)
-    w0, part0 = forward(q, [(chunk0,), comp], (False, True), 0.02)
+    w0, part0 = forward(q, [(chunk0,), comp], (False, True), 0.03)
     part0, cot = lax.optimization_barrier((part0, cot))
+    cot_core = to_core(cot)
     half = dot_nt(columns(0), cot) + dot_nt(columns(1), cot_core)
     half, chunk1, chunk3 = lax.optimization_barrier((half, chunk1, chunk3))
     w13, part13 = forward(q, [(chunk1,), (chunk3,)], (False, False))

time: 70.9 us -> 70.6 us (level)
  local copies, waits for them, and re-layouts: 0.9 us -> 0.05 us
    unnamed x7 -> x9, local copies, waits for them, and re-layouts: 0.88 us -> 0.03 us
  transfers between devices with their start and end apart: 17 -> 17, of which waited for: 11 -> 11; matrix products, arithmetic and copies ran while one was open for 6% -> 7% of each run, Pallas kernels for 24% -> 25%
where the time goes in v7:
time: 70.6 us; the launch traced here: 70.3 us
  starting transfers between devices  24.8 us (35%)
  Pallas kernels  19.4 us (27%)
  waiting for transfers between devices  16.1 us (23%)
  matrix products  6.77 us (10%)
  other arithmetic  1.71 us (2%)
  between operations  1.53 us (2%)
    pallas_call x7, Pallas kernels, call(): pl.pallas_call(kernel, in_specs=specs or [IN_VMEM] * len(operands), out_s...  19.4 us
    ppermute x6, starting transfers between devices, over_z(): return lax.ppermute(a, 'group', group_flip(s, 0))  15.3 us
    ppermute x6, starting transfers between devices, over_x(): return lax.ppermute(a, 'group', group_flip(0, s))  7.89 us
    ppermute x6, waiting for transfers between devices, over_x(): return lax.ppermute(a, 'group', group_flip(0, s))  7.32 us
    ppermute x6, waiting for transfers between devices, over_z(): return lax.ppermute(a, 'group', group_flip(s, 0))  6.48 us
    dot_general x4, matrix products, partial_out(): lax.dot_general(mixed, columns(bits), (((0,), (0,)), ((), ())), preferred...  3.78 us
    dot_general x4, matrix products, dot_nt(): lax.dot_general(a, b, (((1,), (1,)), ((), ())), preferred_element_type=F32)  2.99 us
    ppermute x2, waiting for transfers between devices, to_chip(): return lax.ppermute(a, 'tensor', tensor_flip(2))  1.81 us
  transfers between devices with their start and end apart: 17, of which 11 were waited for; matrix products, arithmetic and copies ran while one was open for 7% of the time, Pallas kernels for 25%

profile of v7, /device:TPU:8, one launch (start us, length us, event | category | flops | bytes accessed | tf_op | source)
XLA Modules:
  0.0 70.3 jit_solution(10046647155063097574)
XLA Ops:
  0.6 0.8 %pad_maximum_fusion.1 = bf16[128,256]{1,0:T(8,128)(2,1)S(1)} fusion(bf16[128,128]{1,0:T(8,128)(2,1)} %bitcast.31, bf16[128,128]{1,0:T(8,128)(2,1)} %bitcast.32), kind=kLoop, calls=%fused_computation.41 | loop fusion | flops 131072 | bytes 131072 | tf_op jit(solution)/shard_map/concatenate | solution.py:305
  1.4 7.3 %collective-permute-start.2 = (bf16[128,256]{1,0:T(8,128)(2,1)S(1)}, bf16[128,256]{1,0:T(8,128)(2,1)S(1)}, u32[]{:S(2)}, u32[]{:S(2)}) collective-permute-start(bf16[128,256]{1,0:T(8,128)(2,1)S(1)} %pad_maximum_fusion.1), channel_id=1, source_target_pairs={{0,32},{4,36},{8,40},{12,44},{16,48},{20,52},{24,56},{28,60},{32,0... | collective-permute-start | bytes 196616 | tf_op jit(solution)/shard_map/ppermute | solution.py:294
  8.7 0.0 collective-permute-start.1
  8.7 1.5 %collective-permute-start = (bf16[128,256]{1,0:T(8,128)(2,1)S(1)}, bf16[128,256]{1,0:T(8,128)(2,1)S(1)}, u32[]{:S(2)}, u32[]{:S(2)}) collective-permute-start(bf16[128,256]{1,0:T(8,128)(2,1)S(1)} %pad_maximum_fusion.1), channel_id=1, source_target_pairs={{0,16},{4,20},{8,24},{12,28},{16,0},{20,4},{24,8},{28,12},{32,48},... | collective-permute-start | bytes 196616 | tf_op jit(solution)/shard_map/ppermute | solution.py:294
  10.2 1.1 %fetch.1 = (bf16[256,1024]{1,0:T(8,128)(2,1)S(1)}, bf16[256,128]{1,0:T(8,128)(2,1)S(1)}, bf16[256,128]{1,0:T(8,128)(2,1)S(1)}) custom-call(bf16[256,1024]{1,0:T(8,128)(2,1)} %bitcast.25, bf16[256,128]{1,0:T(8,128)(2,1)} %bitcast.29, bf16[256,128]{1,0:T(8,128)(2,1)} %bitcast.30), custom_call_target="tpu_custom_call" | custom-call | flops 1000000 | bytes 100000 | tf_op jit(solution)/shard_map/fetch/pallas_call | solution.py:187
  11.2 1.1 %collective-permute-start.6 = (bf16[256,1024]{1,0:T(8,128)(2,1)}, bf16[256,1024]{1,0:T(8,128)(2,1)S(1)}, u32[]{:S(2)}, u32[]{:S(2)}) collective-permute-start(bf16[256,1024]{1,0:T(8,128)(2,1)} %bitcast.26), channel_id=1, source_target_pairs={{0,2},{1,3},{2,0},{3,1},{4,6},{5,7},{6,4},{7,5},{8,10},{9,11},{10,... | collective-permute-start | bytes 1572872 | tf_op jit(solution)/shard_map/ppermute | solution.py:303
  13.0 0.0 slice-start
  13.0 2.3 %collective-permute-done = bf16[128,256]{1,0:T(8,128)(2,1)S(1)} collective-permute-done((bf16[128,256]{1,0:T(8,128)(2,1)S(1)}, bf16[128,256]{1,0:T(8,128)(2,1)S(1)}, u32[]{:S(2)}, u32[]{:S(2)}) %collective-permute-start) | collective-permute-done | bytes 65568 | tf_op jit(solution)/shard_map/ppermute | solution.py:294
  15.3 0.5 collective-permute-done.1
  15.8 0.0 collective-permute-done.2
  15.8 2.8 %collective-permute-start.5 = (bf16[512,256]{1,0:T(8,128)(2,1)S(1)}, bf16[512,256]{1,0:T(8,128)(2,1)S(1)}, u32[]{:S(2)}, u32[]{:S(2)}) collective-permute-start(bf16[512,256]{1,0:T(8,128)(2,1)S(1)} %constant_dynamic-update-slice_fusion.refs_1_.refs_5_), channel_id=1, source_target_pairs={{0,12},{4,8},{8,4},{12,0},{16,28},{20,24},{24,20},{28,16},{32,44},... | collective-permute-start | bytes 786440 | tf_op jit(solution)/shard_map/ppermute | solution.py:297
  18.6 0.2 collective-permute-start.4
  18.9 0.0 copy-start
  18.9 0.0 slice-start.1
  18.9 2.6 %forward.2 = (bf16[512,2048]{1,0:T(8,128)(2,1)S(1)}, bf16[256,2048]{1,0:T(8,128)(2,1)S(1)}, f32[8,1,256]{2,1,0:T(1,128)S(1)}, f32[8,1,256]{2,1,0:T(1,128)S(1)}, f32[1024,256]{1,0:T(8,128)S(1)}) custom-call(bf16[256,1024]{1,0:T(8,128)(2,1)S(1)} %get-tuple-element.53.refs_0_.refs_1_, bf16[512,256]{1,0:T(8,128)(2,1)S(1)} %constant_dynamic-update-slice_fusion.refs_1_.refs_5_, ...), custom_call_target="tpu_custom_call" | custom-call | flops 13421772800 | bytes 98304 | tf_op jit(solution)/shard_map/forward/pallas_call | solution.py:187
  21.4 0.0 copy-done
  21.4 0.1 collective-permute-start.3
  21.5 0.0 slice-done
  21.6 0.0 slice-done.1
  21.6 0.7 %fusion.14 = f32[1024,256]{1,0:T(8,128)S(1)} fusion(bf16[256,1024]{1,0:T(8,128)(2,1)S(1)} %bitcast.28, bf16[1024,4096]{1,0:T(8,128)(2,1)S(1)} %bitcast.24, s32[]{:T(128)S(6)} %select_n.16), kind=kOutput, calls=%fused_computation.14 | convolution fusion | flops 536870912 | bytes 3670020 | tf_op jit(solution)/shard_map/dot_general | solution.py:26
  22.3 3.8 %collective-permute-done.4.refs_1_.refs_5_ = bf16[512,256]{1,0:T(8,128)(2,1)S(1)} collective-permute-done((bf16[512,256]{1,0:T(8,128)(2,1)S(1)}, bf16[512,256]{1,0:T(8,128)(2,1)S(1)}, u32[]{:S(2)}, u32[]{:S(2)}) %collective-permute-start.4) | collective-permute-done | bytes 262176 | tf_op jit(solution)/shard_map/ppermute | solution.py:297
  26.1 0.5 collective-permute-start.8
  26.6 0.4 collective-permute-done.6
  27.0 0.0 collective-permute-start.7
  27.0 0.7 %fusion.6 = f32[1024,256]{1,0:T(8,128)S(1)} fusion(bf16[256,1024]{1,0:T(8,128)(2,1)S(1)} %collective-permute-done.6, bf16[1024,4096]{1,0:T(8,128)(2,1)S(1)} %bitcast.24, s32[]{:T(128)S(6)} %select_n.18), kind=kOutput, calls=%fused_computation.6 | convolution fusion | flops 536870912 | bytes 3670020 | tf_op jit(solution)/shard_map/dot_general | solution.py:26
  27.8 0.0 collective-permute-done.3
  27.8 0.7 %fusion.16 = f32[1024,256]{1,0:T(8,128)S(1)} fusion(f32[1024,256]{1,0:T(8,128)S(1)} %fusion.14, bf16[256,1024]{1,0:T(8,128)(2,1)S(1)} %collective-permute-done.3, bf16[1024,4096]{1,0:T(8,128)(2,1)S(1)} %bitcast.24, s32[]{:T(128)S(6)} %select_n.17), kind=kOutput, calls=%fused_computation.16 | convolution fusion | flops 537133056 | bytes 4718596 | tf_op jit(solution)/shard_map/dot_general | solution.py:26
  28.5 0.0 collective-permute-done.5.refs_2_.refs_6_
  28.5 3.5 %forward.3 = (bf16[512,2048]{1,0:T(8,128)(2,1)S(1)}, bf16[512,2048]{1,0:T(8,128)(2,1)S(1)}, f32[8,1,256]{2,1,0:T(1,128)S(1)}, f32[8,1,256]{2,1,0:T(1,128)S(1)}, f32[1024,256]{1,0:T(8,128)S(1)}) custom-call(bf16[256,1024]{1,0:T(8,128)(2,1)S(1)} %get-tuple-element.53.refs_0_.refs_1_, bf16[512,256]{1,0:T(8,128)(2,1)S(1)} %collective-permute-done.4.refs_1_.refs_5_, ...), custom_call_target="tpu_custom_call" | custom-call | flops 33554432 | bytes 131072 | tf_op jit(solution)/shard_map/forward/pallas_call | solution.py:187
  32.0 0.0 collective-permute-done.7
  32.0 0.8 %fusion.22.refs_2_.refs_1_ = bf16[1024,256]{1,0:T(8,128)(2,1)S(1)} fusion(bf16[256,1024]{1,0:T(8,128)(2,1)S(1)} %collective-permute-done.7, bf16[1024,4096]{1,0:T(8,128)(2,1)S(1)} %bitcast.24, s32[]{:T(128)S(6)} %select_n.19, f32[1024,256]{1,0:T(8,128)S(1)} %fusion.16, f32[1024,256]{1,0:T(8,128)S(1)} %fusion.6), kind=kOutput, calls=%fused_computation.18 | convolution fusion | flops 537657344 | bytes 5242884 | tf_op jit(solution)/shard_map/dot_general | solution.py:26
  32.8 1.1 %collective-permute-done.8.refs_3_.refs_4_ = bf16[512,256]{1,0:T(8,128)(2,1)S(1)} collective-permute-done((bf16[512,256]{1,0:T(8,128)(2,1)S(1)}, bf16[512,256]{1,0:T(8,128)(2,1)S(1)}, u32[]{:S(2)}, u32[]{:S(2)}) %collective-permute-start.8) | collective-permute-done | bytes 262176 | tf_op jit(solution)/shard_map/ppermute | solution.py:297
  33.9 2.1 %forward_merge.1 = (bf16[512,2048]{1,0:T(8,128)(2,1)S(1)}, f32[8,1,256]{2,1,0:T(1,128)S(1)}, f32[8,1,256]{2,1,0:T(1,128)S(1)}, f32[8,1,256]{2,1,0:T(1,128)S(1)},...) custom-call(s32[1,1]{1,0:T(1,128)S(6)} %copy.17.refs_0_, ...), custom_call_target="tpu_custom_call" | custom-call | flops 16777216 | bytes 65536 | tf_op jit(solution)/shard_map/forward_merge/pallas_call | solution.py:187
  36.0 0.7 %fusion.34 = bf16[256,1024]{1,0:T(8,128)(2,1)S(1)} fusion(bf16[1024,256]{1,0:T(8,128)(2,1)S(1)} %get-tuple-element.71, bf16[1024,4096]{1,0:T(8,128)(2,1)S(1)} %bitcast.24, s32[]{:T(128)S(6)} %select_n.19), kind=kOutput, calls=%fused_computation.22 | convolution fusion | flops 537133056 | bytes 3145732 | tf_op jit(solution)/shard_map/dot_general | solution.py:334
  36.8 0.7 %fusion.28 = bf16[256,1024]{1,0:T(8,128)(2,1)S(1)} fusion(bf16[1024,256]{1,0:T(8,128)(2,1)S(1)} %get-tuple-element.71, bf16[1024,4096]{1,0:T(8,128)(2,1)S(1)} %bitcast.24, s32[]{:T(128)S(6)} %select_n.17), kind=kOutput, calls=%fused_computation.20 | convolution fusion | flops 537133056 | bytes 3145732 | tf_op jit(solution)/shard_map/dot_general | solution.py:334
  37.5 0.1 pad_maximum_fusion
  37.6 0.1 collective-permute-start.9
  37.7 2.1 %backward.3 = (bf16[512,256]{1,0:T(8,128)(2,1)S(1)}, f32[1024,256]{1,0:T(8,128)S(1)}) custom-call(bf16[256,1024]{1,0:T(8,128)(2,1)S(1)} %get-tuple-element.53.refs_0_.refs_1_, bf16[1024,256]{1,0:T(8,128)(2,1)S(1)} %fusion.22.refs_2_.refs_1_, f32[8,1,256]{2,1,0:T(1,128)S(1)} %get-tuple-element.72.refs_2_, f32[8,1,256]{2,1,0:T(1,128)S(1)} %get-tuple-element.73.refs_3_, ...), custom_call_target="tpu_custom_call" | custom-call | flops 33554432 | bytes 65536 | tf_op jit(solution)/shard_map/backward/pallas_call | solution.py:187
  39.8 0.5 collective-permute-done.9
  40.3 0.7 %fusion.43 = bf16[256,1024]{1,0:T(8,128)(2,1)S(1)} fusion(bf16[1024,256]{1,0:T(8,128)(2,1)S(1)} %get-tuple-element.71, bf16[1024,4096]{1,0:T(8,128)(2,1)S(1)} %bitcast.24, s32[]{:T(128)S(6)} %select_n.18, bf16[512,1024]{1,0:T(8,128)(2,1)S(1)} %collective-permute-done.9), kind=kOutput, calls=%fused_computation.25 | convolution fusion | flops 538181632 | bytes 3670020 | tf_op jit(solution)/shard_map/dot_general | solution.py:334
  41.1 0.2 collective-permute-start.11
  41.3 2.5 %collective-permute-start.10 = (bf16[512,256]{1,0:T(8,128)(2,1)S(1)}, bf16[512,256]{1,0:T(8,128)(2,1)S(1)}, u32[]{:S(2)}, u32[]{:S(2)}) collective-permute-start(bf16[512,256]{1,0:T(8,128)(2,1)S(1)} %get-tuple-element.77), channel_id=1, source_target_pairs={{0,8},{4,12},{8,0},{12,4},{16,24},{20,28},{24,16},{28,20},{32,40},... | collective-permute-start | bytes 786440 | tf_op jit(solution)/shard_map/ppermute | solution.py:297
  43.8 4.1 %backward.4 = (bf16[512,256]{1,0:T(8,128)(2,1)S(1)}, bf16[512,256]{1,0:T(8,128)(2,1)S(1)}, f32[1024,256]{1,0:T(8,128)S(1)}) custom-call(bf16[256,1024]{1,0:T(8,128)(2,1)S(1)} %get-tuple-element.53.refs_0_.refs_1_, bf16[1024,256]{1,0:T(8,128)(2,1)S(1)} %fusion.22.refs_2_.refs_1_, f32[8,1,256]{2,1,0:T(1,128)S(1)} %get-tuple-element.72.refs_2_, ...), custom_call_target="tpu_custom_call" | custom-call | flops 67108864 | bytes 131072 | tf_op jit(solution)/shard_map/backward/pallas_call | solution.py:187
  47.9 0.7 collective-permute-start.12
  48.6 1.2 %collective-permute-start.13 = (bf16[512,256]{1,0:T(8,128)(2,1)S(1)}, bf16[512,256]{1,0:T(8,128)(2,1)S(1)}, u32[]{:S(2)}, u32[]{:S(2)}) collective-permute-start(bf16[512,256]{1,0:T(8,128)(2,1)S(1)} %get-tuple-element.95), channel_id=1, source_target_pairs={{0,12},{4,8},{8,4},{12,0},{16,28},{20,24},{24,20},{28,16},{32,44},... | collective-permute-start | bytes 786440 | tf_op jit(solution)/shard_map/ppermute | solution.py:297
  49.7 4.0 %backward.5 = (f32[512,256]{1,0:T(8,128)S(1)}, bf16[256,128]{1,0:T(8,128)(2,1)}, bf16[256,128]{1,0:T(8,128)(2,1)}, bf16[256,1024]{1,0:T(8,128)(2,1)}) custom-call(bf16[256,1024]{1,0:T(8,128)(2,1)S(1)} %get-tuple-element.53.refs_0_.refs_1_, bf16[1024,256]{1,0:T(8,128)(2,1)S(1)} %fusion.22.refs_2_.refs_1_, f32[8,1,256]{2,1,0:T(1,128)S(1)} %get-tuple-element.72.refs_2_, ...), custom_call_target="tpu_custom_call" | custom-call | flops 50331648 | bytes 98304 | tf_op jit(solution)/shard_map/backward/pallas_call | solution.py:187
  53.7 0.0 collective-permute-done.10
  53.7 1.4 %collective-permute-done.11 = bf16[256,1024]{1,0:T(8,128)(2,1)S(1)} collective-permute-done((bf16[256,1024]{1,0:T(8,128)(2,1)S(1)}, bf16[256,1024]{1,0:T(8,128)(2,1)S(1)}, u32[]{:S(2)}, u32[]{:S(2)}) %collective-permute-start.11) | collective-permute-done | bytes 524320 | tf_op jit(solution)/shard_map/ppermute | solution.py:303
  55.1 1.2 %collective-permute-done.12 = bf16[512,256]{1,0:T(8,128)(2,1)S(1)} collective-permute-done((bf16[512,256]{1,0:T(8,128)(2,1)S(1)}, bf16[512,256]{1,0:T(8,128)(2,1)S(1)}, u32[]{:S(2)}, u32[]{:S(2)}) %collective-permute-start.12) | collective-permute-done | bytes 262176 | tf_op jit(solution)/shard_map/ppermute | solution.py:297
  56.3 1.2 %collective-permute-done.13 = bf16[512,256]{1,0:T(8,128)(2,1)S(1)} collective-permute-done((bf16[512,256]{1,0:T(8,128)(2,1)S(1)}, bf16[512,256]{1,0:T(8,128)(2,1)S(1)}, u32[]{:S(2)}, u32[]{:S(2)}) %collective-permute-start.13) | collective-permute-done | bytes 262176 | tf_op jit(solution)/shard_map/ppermute | solution.py:297
  57.5 0.2 fusion.73
  57.7 2.0 %collective-permute-start.14 = (bf16[128,256]{1,0:T(8,128)(2,1)S(1)}, bf16[128,256]{1,0:T(8,128)(2,1)S(1)}, u32[]{:S(2)}, u32[]{:S(2)}) collective-permute-start(bf16[128,256]{1,0:T(8,128)(2,1)S(1)} %get-tuple-element.100), channel_id=1, source_target_pairs={{0,16},{4,20},{8,24},{12,28},{16,0},{20,4},{24,8},{28,12},{32,48},... | collective-permute-start | bytes 196616 | tf_op jit(solution)/shard_map/ppermute | solution.py:294
  59.7 3.6 %collective-permute-start.16 = (bf16[128,256]{1,0:T(8,128)(2,1)S(1)}, bf16[128,256]{1,0:T(8,128)(2,1)S(1)}, u32[]{:S(2)}, u32[]{:S(2)}) collective-permute-start(bf16[128,256]{1,0:T(8,128)(2,1)S(1)} %get-tuple-element.101), channel_id=1, source_target_pairs={{0,32},{4,36},{8,40},{12,44},{16,48},{20,52},{24,56},{28,60},{32,0... | collective-permute-start | bytes 196616 | tf_op jit(solution)/shard_map/ppermute | solution.py:294
  63.3 1.0 %collective-permute-start.15 = (bf16[128,256]{1,0:T(8,128)(2,1)S(1)}, bf16[128,256]{1,0:T(8,128)(2,1)S(1)}, u32[]{:S(2)}, u32[]{:S(2)}) collective-permute-start(bf16[128,256]{1,0:T(8,128)(2,1)S(1)} %get-tuple-element.102), channel_id=1, source_target_pairs={{0,48},{4,52},{8,56},{12,60},{16,32},{20,36},{24,40},{28,44},{32,1... | collective-permute-start | bytes 196616 | tf_op jit(solution)/shard_map/ppermute | solution.py:294
  64.3 1.6 %fusion.58 = bf16[1,1,256,1024]{3,2,1,0:T(8,128)(2,1)} fusion(bf16[1024,256]{1,0:T(8,128)(2,1)S(1)} %get-tuple-element.71, bf16[1024,4096]{1,0:T(8,128)(2,1)S(1)} %bitcast.24, s32[]{:T(128)S(6)} %select_n.16, bf16[256,1024]{1,0:T(8,128)(2,1)S(1)} %collective-permute-done.11, bf16[512,1024]{1,0:T(8,128)(2,1)S(1)} %collective-permute-done.9), kind=kOutput, calls=%fused_computation.30 | convolution fusion | flops 538705920 | bytes 4194308 | tf_op jit(solution)/shard_map/dot_general | solution.py:334
  65.9 0.0 collective-permute-done.14
  65.9 2.5 %collective-permute-done.16 = bf16[128,256]{1,0:T(8,128)(2,1)S(1)} collective-permute-done((bf16[128,256]{1,0:T(8,128)(2,1)S(1)}, bf16[128,256]{1,0:T(8,128)(2,1)S(1)}, u32[]{:S(2)}, u32[]{:S(2)}) %collective-permute-start.16) | collective-permute-done | bytes 65568 | tf_op jit(solution)/shard_map/ppermute | solution.py:294
  68.4 1.2 %collective-permute-done.15 = bf16[128,256]{1,0:T(8,128)(2,1)S(1)} collective-permute-done((bf16[128,256]{1,0:T(8,128)(2,1)S(1)}, bf16[128,256]{1,0:T(8,128)(2,1)S(1)}, u32[]{:S(2)}, u32[]{:S(2)}) %collective-permute-start.15) | collective-permute-done | bytes 65568 | tf_op jit(solution)/shard_map/ppermute | solution.py:294
  69.7 0.7 fusion.64
  (9 shorter events, 0.1 us)
Async XLA Ops:
  1.4 14.4 %collective-permute-start.2 = (bf16[128,256]{1,0:T(8,128)(2,1)S(1)}, bf16[128,256]{1,0:T(8,128)(2,1)S(1)}, u32[]{:S(2)}, u32[]{:S(2)}) collective-permute-start(bf16[128,256]{1,0:T(8,128)(2,1)S(1)} %pad_maximum_fusion.1), channel_id=1, source_target_pairs={{0,32},{4,36},{8,40},{12,44},{16,48},{20,52},{24,56},{28,60},{32,0... | collective-permute-start | bytes 196616 | tf_op jit(solution)/shard_map/ppermute | solution.py:294
  8.7 7.1 %collective-permute-start.1 = (bf16[128,256]{1,0:T(8,128)(2,1)S(1)}, bf16[128,256]{1,0:T(8,128)(2,1)S(1)}, u32[]{:S(2)}, u32[]{:S(2)}) collective-permute-start(bf16[128,256]{1,0:T(8,128)(2,1)S(1)} %pad_maximum_fusion.1), channel_id=1, source_target_pairs={{0,48},{4,52},{8,56},{12,60},{16,32},{20,36},{24,40},{28,44},{32,1... | collective-permute-start | bytes 196616 | tf_op jit(solution)/shard_map/ppermute | solution.py:294
  8.7 6.6 %collective-permute-start = (bf16[128,256]{1,0:T(8,128)(2,1)S(1)}, bf16[128,256]{1,0:T(8,128)(2,1)S(1)}, u32[]{:S(2)}, u32[]{:S(2)}) collective-permute-start(bf16[128,256]{1,0:T(8,128)(2,1)S(1)} %pad_maximum_fusion.1), channel_id=1, source_target_pairs={{0,16},{4,20},{8,24},{12,28},{16,0},{20,4},{24,8},{28,12},{32,48},... | collective-permute-start | bytes 196616 | tf_op jit(solution)/shard_map/ppermute | solution.py:294
  11.2 15.8 %collective-permute-start.6 = (bf16[256,1024]{1,0:T(8,128)(2,1)}, bf16[256,1024]{1,0:T(8,128)(2,1)S(1)}, u32[]{:S(2)}, u32[]{:S(2)}) collective-permute-start(bf16[256,1024]{1,0:T(8,128)(2,1)} %bitcast.26), channel_id=1, source_target_pairs={{0,2},{1,3},{2,0},{3,1},{4,6},{5,7},{6,4},{7,5},{8,10},{9,11},{10,... | collective-permute-start | bytes 1572872 | tf_op jit(solution)/shard_map/ppermute | solution.py:303
  13.0 8.5 %slice-start = ((s8[8388608]{0:T(1024)(128)(4,1)}), s8[4194304]{0:T(1024)(128)(4,1)S(1)}, s32[]{:S(2)}) async-start(s8[8388608]{0:T(1024)(128)(4,1)} %bitcast.23), calls=%async_computation | async-start | bytes 8388608
  15.8 12.7 %collective-permute-start.5 = (bf16[512,256]{1,0:T(8,128)(2,1)S(1)}, bf16[512,256]{1,0:T(8,128)(2,1)S(1)}, u32[]{:S(2)}, u32[]{:S(2)}) collective-permute-start(bf16[512,256]{1,0:T(8,128)(2,1)S(1)} %constant_dynamic-update-slice_fusion.refs_1_.refs_5_), channel_id=1, source_target_pairs={{0,12},{4,8},{8,4},{12,0},{16,28},{20,24},{24,20},{28,16},{32,44},... | collective-permute-start | bytes 786440 | tf_op jit(solution)/shard_map/ppermute | solution.py:297
  18.6 7.5 %collective-permute-start.4 = (bf16[512,256]{1,0:T(8,128)(2,1)S(1)}, bf16[512,256]{1,0:T(8,128)(2,1)S(1)}, u32[]{:S(2)}, u32[]{:S(2)}) collective-permute-start(bf16[512,256]{1,0:T(8,128)(2,1)S(1)} %constant_dynamic-update-slice_fusion.refs_1_.refs_5_), channel_id=1, source_target_pairs={{0,4},{4,0},{8,12},{12,8},{16,20},{20,16},{24,28},{28,24},{32,36},... | collective-permute-start | bytes 786440 | tf_op jit(solution)/shard_map/ppermute | solution.py:297
  18.9 2.6 %copy-start = (bf16[1,1,256,1024]{3,2,1,0:T(8,128)(2,1)S(1)}, bf16[1,1,256,1024]{3,2,1,0:T(8,128)(2,1)}, u32[]{:S(2)}) copy-start(bf16[1,1,256,1024]{3,2,1,0:T(8,128)(2,1)} %param.14) | copy-start | bytes 1572868
  18.9 2.7 %slice-start.1 = ((s8[8388608]{0:T(1024)(128)(4,1)}), s8[4194304]{0:T(1024)(128)(4,1)S(1)}, s32[]{:S(2)}) async-start(s8[8388608]{0:T(1024)(128)(4,1)} %bitcast.23), calls=%async_computation.1 | async-start | bytes 8388608
  21.4 6.3 %collective-permute-start.3 = (bf16[256,1024]{1,0:T(8,128)(2,1)S(1)}, bf16[256,1024]{1,0:T(8,128)(2,1)S(1)}, u32[]{:S(2)}, u32[]{:S(2)}) collective-permute-start(bf16[256,1024]{1,0:T(8,128)(2,1)S(1)} %bitcast.27), channel_id=1, source_target_pairs={{0,1},{1,0},{2,3},{3,2},{4,5},{5,4},{6,7},{7,6},{8,9},{9,8},{10,11... | collective-permute-start | bytes 1572872 | tf_op jit(solution)/shard_map/ppermute | solution.py:300
  26.1 7.8 %collective-permute-start.8 = (bf16[512,256]{1,0:T(8,128)(2,1)S(1)}, bf16[512,256]{1,0:T(8,128)(2,1)S(1)}, u32[]{:S(2)}, u32[]{:S(2)}) collective-permute-start(bf16[512,256]{1,0:T(8,128)(2,1)S(1)} %collective-permute-done.4.refs_1_.refs_5_), channel_id=1, source_target_pairs={{0,12},{4,8},{8,4},{12,0},{16,28},{20,24},{24,20},{28,16},{32,44},... | collective-permute-start | bytes 786440 | tf_op jit(solution)/shard_map/ppermute | solution.py:297
  27.0 5.0 %collective-permute-start.7 = (bf16[256,1024]{1,0:T(8,128)(2,1)S(1)}, bf16[256,1024]{1,0:T(8,128)(2,1)S(1)}, u32[]{:S(2)}, u32[]{:S(2)}) collective-permute-start(bf16[256,1024]{1,0:T(8,128)(2,1)S(1)} %collective-permute-done.6), channel_id=1, source_target_pairs={{0,1},{1,0},{2,3},{3,2},{4,5},{5,4},{6,7},{7,6},{8,9},{9,8},{10,11... | collective-permute-start | bytes 1572872 | tf_op jit(solution)/shard_map/ppermute | solution.py:300
  37.6 2.7 %collective-permute-start.9 = (bf16[512,1024]{1,0:T(8,128)(2,1)S(1)}, bf16[512,1024]{1,0:T(8,128)(2,1)S(1)}, u32[]{:S(2)}, u32[]{:S(2)}) collective-permute-start(bf16[512,1024]{1,0:T(8,128)(2,1)S(1)} %pad_maximum_fusion), channel_id=1, source_target_pairs={{0,1},{1,0},{2,3},{3,2},{4,5},{5,4},{6,7},{7,6},{8,9},{9,8},{10,11... | collective-permute-start | bytes 3145736 | tf_op jit(solution)/shard_map/ppermute | solution.py:300
  41.1 14.1 %collective-permute-start.11 = (bf16[256,1024]{1,0:T(8,128)(2,1)S(1)}, bf16[256,1024]{1,0:T(8,128)(2,1)S(1)}, u32[]{:S(2)}, u32[]{:S(2)}) collective-permute-start(bf16[256,1024]{1,0:T(8,128)(2,1)S(1)} %fusion.43), channel_id=1, source_target_pairs={{0,2},{1,3},{2,0},{3,1},{4,6},{5,7},{6,4},{7,5},{8,10},{9,11},{10,... | collective-permute-start | bytes 1572872 | tf_op jit(solution)/shard_map/ppermute | solution.py:303
  41.3 12.4 %collective-permute-start.10 = (bf16[512,256]{1,0:T(8,128)(2,1)S(1)}, bf16[512,256]{1,0:T(8,128)(2,1)S(1)}, u32[]{:S(2)}, u32[]{:S(2)}) collective-permute-start(bf16[512,256]{1,0:T(8,128)(2,1)S(1)} %get-tuple-element.77), channel_id=1, source_target_pairs={{0,8},{4,12},{8,0},{12,4},{16,24},{20,28},{24,16},{28,20},{32,40},... | collective-permute-start | bytes 786440 | tf_op jit(solution)/shard_map/ppermute | solution.py:297
  47.9 8.4 %collective-permute-start.12 = (bf16[512,256]{1,0:T(8,128)(2,1)S(1)}, bf16[512,256]{1,0:T(8,128)(2,1)S(1)}, u32[]{:S(2)}, u32[]{:S(2)}) collective-permute-start(bf16[512,256]{1,0:T(8,128)(2,1)S(1)} %get-tuple-element.94), channel_id=1, source_target_pairs={{0,4},{4,0},{8,12},{12,8},{16,20},{20,16},{24,28},{28,24},{32,36},... | collective-permute-start | bytes 786440 | tf_op jit(solution)/shard_map/ppermute | solution.py:297
  48.6 8.9 %collective-permute-start.13 = (bf16[512,256]{1,0:T(8,128)(2,1)S(1)}, bf16[512,256]{1,0:T(8,128)(2,1)S(1)}, u32[]{:S(2)}, u32[]{:S(2)}) collective-permute-start(bf16[512,256]{1,0:T(8,128)(2,1)S(1)} %get-tuple-element.95), channel_id=1, source_target_pairs={{0,12},{4,8},{8,4},{12,0},{16,28},{20,24},{24,20},{28,16},{32,44},... | collective-permute-start | bytes 786440 | tf_op jit(solution)/shard_map/ppermute | solution.py:297
  57.7 8.2 %collective-permute-start.14 = (bf16[128,256]{1,0:T(8,128)(2,1)S(1)}, bf16[128,256]{1,0:T(8,128)(2,1)S(1)}, u32[]{:S(2)}, u32[]{:S(2)}) collective-permute-start(bf16[128,256]{1,0:T(8,128)(2,1)S(1)} %get-tuple-element.100), channel_id=1, source_target_pairs={{0,16},{4,20},{8,24},{12,28},{16,0},{20,4},{24,8},{28,12},{32,48},... | collective-permute-start | bytes 196616 | tf_op jit(solution)/shard_map/ppermute | solution.py:294
  59.7 8.8 %collective-permute-start.16 = (bf16[128,256]{1,0:T(8,128)(2,1)S(1)}, bf16[128,256]{1,0:T(8,128)(2,1)S(1)}, u32[]{:S(2)}, u32[]{:S(2)}) collective-permute-start(bf16[128,256]{1,0:T(8,128)(2,1)S(1)} %get-tuple-element.101), channel_id=1, source_target_pairs={{0,32},{4,36},{8,40},{12,44},{16,48},{20,52},{24,56},{28,60},{32,0... | collective-permute-start | bytes 196616 | tf_op jit(solution)/shard_map/ppermute | solution.py:294
  63.3 6.4 %collective-permute-start.15 = (bf16[128,256]{1,0:T(8,128)(2,1)S(1)}, bf16[128,256]{1,0:T(8,128)(2,1)S(1)}, u32[]{:S(2)}, u32[]{:S(2)}) collective-permute-start(bf16[128,256]{1,0:T(8,128)(2,1)S(1)} %get-tuple-element.102), channel_id=1, source_target_pairs={{0,48},{4,52},{8,56},{12,60},{16,32},{20,36},{24,40},{28,44},{32,1... | collective-permute-start | bytes 196616 | tf_op jit(solution)/shard_map/ppermute | solution.py:294
